TPU v7x, 256 devices: a whole 4x4x8 slice. The times are simulated.
256 devices in a mesh: gx: 16 (over z, core), gy: 16 (over x, y).
Axes of the slice: x: 4, y: 4, z: 8, core: 2. Of those that a mesh axis runs over, the one named last changes fastest.
Arguments:
- tables: float32 [4096, 32], P(('gx', 'gy')), may hold values from 0 to 8
- table_index: int32 [1024, 8192], P('gx', 'gy'), may hold values from 0 to 4095
- toggle: int32 [1024, 8192], P('gx', 'gy'), may hold values from 0 to 31
- tap_code: int32 [1024, 8192], P('gx', 'gy'), may hold values from 0 to 8
- capacitance: float32 [2, 1024, 8192], P(None, 'gx', 'gy'), may hold values from 0.02 to 0.2
- prior_drop: float32 [2, 1024, 8192], P(None, 'gx', 'gy'), may hold values from 0 to 0.5
Outputs:
- drop_first: float32 [2, 1024, 8192], P(None, 'gx', 'gy')
- drop_second: float32 [2, 1024, 8192], P(None, 'gx', 'gy')
All inputs are finite; a program needn't handle non-finite values.
Results may differ from a plain program's by a relative error of at most 0.0003.
Values sent between devices are 32-bit elements; how exact they have to be, the bound alone decides.
No kernel may reach another device: no remote copies, remote signals or barrier semaphores. Data moves between devices by JAX's collectives and lax.ppermute only.
A program may use at most 64 MiB of HBM per device.

v0:
```python
import math

import jax
import jax.numpy as jnp
from jax import lax
from jax.sharding import PartitionSpec as P

SUBSTEPS = 32
STEPS = 2
ITERS = 3


def extended(cells, sides, width):
    for axis, dim in sides:
        count = lax.axis_size(axis)
        ends = count - 1
        head = lax.slice_in_dim(cells, 0, width, axis=dim)
        tail = lax.slice_in_dim(cells, cells.shape[dim] - width, cells.shape[dim], axis=dim)
        cells = jnp.concatenate(
            [
                lax.ppermute(tail, axis, [(i, (i + 1) % count) for i in range(ends)]),
                cells,
                lax.ppermute(head, axis, [((i + 1) % count, i) for i in range(ends)]),
            ],
            axis=dim,
        )
    return cells


def lateral_conductance():
    return jnp.array([1.0, 4.0], jnp.float32).reshape(2, 1, 1)


def chebyshev_taus():
    theta = 1.05
    delta = 0.95
    return [1.0 / (theta + delta * math.cos((2 * i - 1) * math.pi / 6.0)) for i in (1, 2, 3)]


def substep_weights():
    share = SUBSTEPS // STEPS
    rows = lax.broadcasted_iota(jnp.int32, (SUBSTEPS, SUBSTEPS * STEPS), 0)
    cols = lax.broadcasted_iota(jnp.int32, (SUBSTEPS, SUBSTEPS * STEPS), 1)
    moment = rows + cols // STEPS
    which = cols % STEPS
    valid = (moment < SUBSTEPS) & (moment // share == which)
    return jnp.where(valid, jnp.float32(1.0 / share), jnp.float32(0.0))


def apply_padded(padded, capacity):
    conduct = lateral_conductance()
    center = padded[:, 1:-1, 1:-1]
    beside = padded[:, :-2, 1:-1] + padded[:, 2:, 1:-1] + padded[:, 1:-1, :-2] + padded[:, 1:-1, 2:]
    return (capacity + 4.0 * conduct + 2.0) * center - conduct * beside - 2.0 * center[::-1]


def operate(field, capacity):
    padded = extended(field, (("gx", 1), ("gy", 2)), 1)
    return apply_padded(padded, capacity)


def precondition(resid, capacity, diagonal):
    taus = chebyshev_taus()
    first = taus[0] * resid / diagonal
    second = first + taus[1] * (resid - operate(first, capacity)) / diagonal
    return second + taus[2] * (resid - operate(second, capacity)) / diagonal


def global_inner(left, right):
    return lax.psum(jnp.sum(left * right), ("gx", "gy"))


def solve(rhs, guess, capacity, smoother):
    drop = guess
    resid = rhs - operate(drop, capacity)
    conditioned = smoother(resid)
    aligned = global_inner(resid, conditioned)
    direction = conditioned
    for turn in range(ITERS):
        image = operate(direction, capacity)
        step_size = aligned / lax.psum(jnp.sum(direction * image), ("gx", "gy"))
        drop = drop + step_size * direction
        resid = resid - step_size * image
        if turn + 1 < ITERS:
            conditioned = smoother(resid)
            aligned_next = global_inner(resid, conditioned)
            direction = conditioned + aligned_next / aligned * direction
            aligned = aligned_next
    return drop


def shards(tables, table_index, toggle, tap_code, capacitance, prior_drop):
    weights = substep_weights()
    expanded = jnp.dot(
        lax.all_gather(tables, ("gx", "gy"), axis=0, tiled=True),
        weights,
        precision=lax.Precision.HIGHEST,
    )
    flat = expanded.reshape(-1)
    base = table_index * (SUBSTEPS * STEPS) + toggle * STEPS
    charges = [jnp.take(flat, base + k) for k in range(STEPS)]
    stacked = jnp.stack(charges + [tap_code.astype(jnp.float32)])
    padded = extended(stacked, (("gx", 1), ("gy", 2)), 1)
    rows, cols = table_index.shape
    current = jnp.zeros((STEPS, rows, cols), jnp.float32)
    for shift_row in (-1, 0, 1):
        for shift_col in (-1, 0, 1):
            code = 3 * (shift_row + 1) + (shift_col + 1)
            source = padded[
                :, 1 - shift_row : 1 - shift_row + rows, 1 - shift_col : 1 - shift_col + cols
            ]
            current = current + source[:STEPS] * (source[STEPS] == jnp.float32(code)).astype(
                jnp.float32
            )
    diagonal = capacitance + 4.0 * lateral_conductance() + 2.0

    def smoother(resid):
        return precondition(resid, capacitance, diagonal)

    previous = prior_drop
    results = []
    empty = jnp.zeros((rows, cols), jnp.float32)
    for step in range(STEPS):
        rhs = capacitance * previous + jnp.stack([current[step], empty])
        previous = solve(rhs, previous, capacitance, smoother)
        results.append(previous)
    return (results[0], results[1])


def solution(mesh):
    in_specs = (
        P(("gx", "gy"), None),
        P("gx", "gy"),
        P("gx", "gy"),
        P("gx", "gy"),
        P(None, "gx", "gy"),
        P(None, "gx", "gy"),
    )
    out_specs = (P(None, "gx", "gy"), P(None, "gx", "gy"))
    return jax.shard_map(shards, mesh=mesh, in_specs=in_specs, out_specs=out_specs, check_vma=False)
```

profile of v0, /device:TPU:1, one launch (start us, length us, event | category | flops | bytes accessed | tf_op | source)
XLA Modules:
  0.0 1660.6 jit_solution(11370643203085847066)
XLA Ops:
  1.4 4.9 collective-permute-start.4
  11.1 120.8 %all_gather.3 = f32[4096,32]{1,0:T(8,128)S(1)} all-gather(f32[16,32]{1,0:T(8,128)S(1)} %copy-done.6), channel_id=1, replica_groups=mesh['gx'=16,'gy'=16] {'gx','gy'}, dimensions={0}, use_global_device_ids=true | all-gather | bytes 526336 | tf_op jit(solution)/shard_map/all_gather | solution.py:95
  135.2 180.7 %gather_fusion.1 = f32[32768]{0:T(1024)S(1)} fusion(f32[262144]{0:T(1024)S(1)} %reshape.96, s32[32768]{0:T(1024)} %broadcast_clamp_fusion), kind=kCustom, calls=%fused_computation.1.clone | custom fusion | bytes 393216 | tf_op jit(solution)/shard_map/jit(_take)/gather | solution.py:101
  315.9 180.5 %gather_fusion = f32[32768]{0:T(1024)S(1)} fusion(f32[262144]{0:T(1024)S(1)} %reshape.96, s32[32768]{0:T(1024)S(1)} %broadcast_clamp_fusion.1), kind=kCustom, calls=%fused_computation.clone | custom fusion | bytes 393216 | tf_op jit(solution)/shard_map/jit(_take)/gather | solution.py:101
  505.7 4.6 collective-permute-start.3
  522.5 4.0 collective-permute-start.10
  528.0 4.0 collective-permute-done.11
  546.0 6.5 collective-permute-done.15
  552.9 4.0 collective-permute-start.16
  561.9 5.8 collective-permute-start.18
  569.0 4.0 collective-permute-done.19
  573.9 84.3 %all-reduce.2 = (f32[]{:T(128)}, f32[]{:T(128)}) all-reduce(f32[]{:T(128)} %get-tuple-element.6, f32[]{:T(128)} %get-tuple-element.5), channel_id=1, replica_groups=mesh['gx'=16,'gy'=16] {'gx','gy'}, use_global_device_ids=true, to_apply=%region_1.3 | all-reduce | flops 2 | bytes 16 | tf_op jit(solution)/shard_map/psum | solution.py:70
  670.5 3.9 collective-permute-done.23
  687.1 4.1 collective-permute-done.27
  692.1 81.2 %psum.86 = f32[]{:T(128)} all-reduce(f32[]{:T(128)} %get-tuple-element.30), channel_id=1, replica_groups=mesh['gx'=16,'gy'=16] {'gx','gy'}, use_global_device_ids=true, to_apply=%region_5.7 | all-reduce | flops 1 | bytes 8 | tf_op jit(solution)/shard_map/psum | solution.py:70
  786.2 3.9 collective-permute-done.31
  790.9 78.7 %psum.87 = f32[]{:T(128)} all-reduce(f32[]{:T(128)} %get-tuple-element.28), channel_id=1, replica_groups=mesh['gx'=16,'gy'=16] {'gx','gy'}, use_global_device_ids=true, to_apply=%region_7.9 | all-reduce | flops 1 | bytes 8 | tf_op jit(solution)/shard_map/psum | solution.py:81
  882.6 3.9 collective-permute-done.35
  899.2 4.1 collective-permute-done.39
  904.2 81.0 %psum.88 = f32[]{:T(128)} all-reduce(f32[]{:T(128)} %get-tuple-element.24), channel_id=1, replica_groups=mesh['gx'=16,'gy'=16] {'gx','gy'}, use_global_device_ids=true, to_apply=%region_9.11 | all-reduce | flops 1 | bytes 8 | tf_op jit(solution)/shard_map/psum | solution.py:70
  998.1 3.9 collective-permute-done.43
  1002.9 78.7 %psum.89 = f32[]{:T(128)} all-reduce(f32[]{:T(128)} %fusion.92), channel_id=1, replica_groups=mesh['gx'=16,'gy'=16] {'gx','gy'}, use_global_device_ids=true, to_apply=%region_11.13 | all-reduce | flops 1 | bytes 8 | tf_op jit(solution)/shard_map/psum | solution.py:81
  1111.2 4.1 collective-permute-done.51
  1124.2 5.3 collective-permute-start.54
  1130.9 4.2 collective-permute-done.55
  1153.5 81.3 %all-reduce.1 = (f32[]{:T(128)}, f32[]{:T(128)}) all-reduce(f32[]{:T(128)} %get-tuple-element.4, f32[]{:T(128)} %get-tuple-element.3), channel_id=1, replica_groups=mesh['gx'=16,'gy'=16] {'gx','gy'}, use_global_device_ids=true, to_apply=%region_13.15 | all-reduce | flops 2 | bytes 16 | tf_op jit(solution)/shard_map/psum | solution.py:70
  1264.3 4.1 collective-permute-done.67
  1269.3 80.9 %psum.92 = f32[]{:T(128)} all-reduce(f32[]{:T(128)} %get-tuple-element.17), channel_id=1, replica_groups=mesh['gx'=16,'gy'=16] {'gx','gy'}, use_global_device_ids=true, to_apply=%region_17.19 | all-reduce | flops 1 | bytes 8 | tf_op jit(solution)/shard_map/psum | solution.py:70
  1367.9 78.7 %psum.93 = f32[]{:T(128)} all-reduce(f32[]{:T(128)} %get-tuple-element.15), channel_id=1, replica_groups=mesh['gx'=16,'gy'=16] {'gx','gy'}, use_global_device_ids=true, to_apply=%region_19.21 | all-reduce | flops 1 | bytes 8 | tf_op jit(solution)/shard_map/psum | solution.py:81
  1476.2 4.1 collective-permute-done.79
  1481.2 80.9 %psum.94 = f32[]{:T(128)} all-reduce(f32[]{:T(128)} %get-tuple-element.11), channel_id=1, replica_groups=mesh['gx'=16,'gy'=16] {'gx','gy'}, use_global_device_ids=true, to_apply=%region_21.23 | all-reduce | flops 1 | bytes 8 | tf_op jit(solution)/shard_map/psum | solution.py:70
  1579.8 78.7 %psum.95 = f32[]{:T(128)} all-reduce(f32[]{:T(128)} %fusion.5), channel_id=1, replica_groups=mesh['gx'=16,'gy'=16] {'gx','gy'}, use_global_device_ids=true, to_apply=%region_23.25 | all-reduce | flops 1 | bytes 8 | tf_op jit(solution)/shard_map/psum | solution.py:81
  (260 shorter events, 275.4 us)
Async XLA Ops:
  1.4 499.6 %collective-permute-start.4 = (f32[2,1,512]{2,1,0:T(1,128)S(1)}, f32[2,1,512]{2,1,0:T(1,128)S(1)}, u32[]{:S(2)}, u32[]{:S(2)}) collective-permute-start(f32[2,1,512]{2,1,0:T(1,128)S(1)} %get-tuple-element.134), channel_id=1, source_target_pairs={{0,16},{16,32},{32,48},{48,64},{64,80},{80,96},{96,112},{112,128},... | collective-permute-start | bytes 12296 | tf_op jit(solution)/shard_map/ppermute | solution.py:21
  6.4 494.7 %collective-permute-start.5 = (f32[2,1,512]{2,1,0:T(1,128)S(1)}, f32[2,1,512]{2,1,0:T(1,128)S(1)}, u32[]{:S(2)}, u32[]{:S(2)}) collective-permute-start(f32[2,1,512]{2,1,0:T(1,128)S(1)} %get-tuple-element.135), channel_id=1, source_target_pairs={{16,0},{32,16},{48,32},{64,48},{80,64},{96,80},{112,96},{128,112},... | collective-permute-start | bytes 12296 | tf_op jit(solution)/shard_map/ppermute | solution.py:23
  496.6 7.7 collective-permute-start
  498.5 5.8 collective-permute-start.1
  501.2 12.2 collective-permute-start.6
  503.0 10.4 collective-permute-start.7
  504.4 7.5 collective-permute-start.2
  505.7 7.2 collective-permute-start.3
  514.1 5.4 collective-permute-start.8
  522.5 5.4 collective-permute-start.10
  526.6 5.4 collective-permute-start.11
  532.3 5.4 collective-permute-start.12
  544.7 7.9 collective-permute-start.15
  552.9 5.9 collective-permute-start.16
  561.9 7.1 collective-permute-start.18
  567.6 5.4 collective-permute-start.19
  669.1 5.3 collective-permute-start.23
  674.7 5.8 collective-permute-start.24
  685.7 5.5 collective-permute-start.27
  784.8 5.3 collective-permute-start.31
  886.8 5.8 collective-permute-start.36
  897.8 5.5 collective-permute-start.39
  1098.8 5.8 collective-permute-start.48
  1109.8 5.5 collective-permute-start.51
  1115.6 5.5 collective-permute-start.52
  1124.2 6.7 collective-permute-start.54
  1129.5 5.6 collective-permute-start.55
  1135.4 5.5 collective-permute-start.56
  1251.9 5.8 collective-permute-start.64
  1262.9 5.5 collective-permute-start.67
  1463.8 5.8 collective-permute-start.76
  1474.8 5.5 collective-permute-start.79
  (60 other events, 1211.1 us)
where the time goes:
time: 1670 us; the launch traced here: 1660 us
  blocking collectives  925 us (55%)
  local copies, waits for them, and re-layouts  363 us (22%)
  starting transfers between devices  200 us (12%)
  waiting for transfers between devices  135 us (8%)
  other arithmetic  18.9 us (1%)
    psum x6, blocking collectives, global_inner(): return lax.psum(jnp.sum(left * right), ('gx', 'gy'))  490 us
    gather x4, local copies, waits for them, and re-layouts, shards(): charges = [jnp.take(flat, base + k) for k in range(STEPS)]  361 us
    psum x4, blocking collectives, solve(): step_size = aligned / lax.psum(jnp.sum(direction * image), ('gx', 'gy'))  315 us
    ppermute x42, waiting for transfers between devices, extended(): lax.ppermute(head, axis, [((i + 1) % count, i) for i in range(ends)])  132 us
    ppermute x42, starting transfers between devices, extended(): lax.ppermute(tail, axis, [(i, (i + 1) % count) for i in range(ends)])  129 us
    all_gather x1, blocking collectives, shards(): lax.all_gather(tables, ('gx', 'gy'), axis=0, tiled=True)  121 us
    ppermute x42, starting transfers between devices, extended(): lax.ppermute(head, axis, [((i + 1) % count, i) for i in range(ends)])  71.5 us
  transfers between devices with their start and end apart: 84, of which 58 were waited for; matrix products, arithmetic and copies ran while one was open for 22% of the time, Pallas kernels for 0%

commit v1 on v0

v1 whole, which is shorter than its diff:
```python
import functools
import math

import jax
import jax.numpy as jnp
from jax import lax
from jax.experimental import pallas as pl
from jax.experimental.pallas import tpu as pltpu
from jax.sharding import PartitionSpec as P

SUBSTEPS = 32
STEPS = 2
BOTH = ("gx", "gy")
LANES = 128
HALO = 20
GROUP = 8
LO = 4
CONDUCT = (1.0, 4.0)


def chebyshev_taus():
    theta = 1.05
    delta = 0.95
    return [1.0 / (theta + delta * math.cos((2 * i - 1) * math.pi / 6.0)) for i in (1, 2, 3)]


TAU = chebyshev_taus()
ALPHA = TAU[1] + (1.0 - TAU[1]) * TAU[0]
BETA = TAU[0] * TAU[1]
KEEP = (1.0 - TAU[2]) * BETA / TAU[2]
SHIFT = 0.75
RADIUS = 0.7
BACK = SHIFT / TAU[2]
FORMER = 0.5 * (RADIUS / TAU[2]) ** 2


def params(mib):
    return pltpu.CompilerParams(vmem_limit_bytes=mib * 2**20)


def vmem():
    return pl.BlockSpec(memory_space=pltpu.VMEM)


def address_kernel(table_ref, out_ref):
    table = table_ref[...]
    many = table.shape[0] // LO
    block = jnp.concatenate([table[a * many : (a + 1) * many] for a in range(LO)], axis=1)
    out_ref[...] = jnp.broadcast_to(block[None], out_ref.shape)


def address(table, count):
    many = table.shape[0] // LO
    return pl.pallas_call(
        address_kernel,
        out_shape=jax.ShapeDtypeStruct((count, many, LANES), jnp.float32),
        in_specs=[vmem()],
        out_specs=vmem(),
        compiler_params=params(8),
        name="address",
    )(table)


MANY = 8
CHUNK = 256
UNROLL = 8


def split_kernel(table_refs, pieces_ref):
    for b, ref in enumerate(table_refs):
        across = ref[...].T
        high = across.astype(jnp.bfloat16)
        low = (across - high.astype(jnp.float32)).astype(jnp.bfloat16)
        for p, piece in enumerate((high, low)):
            pieces_ref[pl.ds((2 * p + b) * LANES, LANES), :] = piece


def charges(many, index, toggle, pieces_ref):
    many, inner = many
    cols = index.shape[1]
    groups = pieces_ref.shape[1]
    quarter = many // LO
    held = index & (many - 1)
    device = index // many
    half = (device // inner) & 1
    place = device // (2 * inner) * inner + (device & (inner - 1))
    row = place * quarter + (held & (quarter - 1))
    which = held // quarter + LO * half
    hot = []
    for k in range(groups // CHUNK):
        local = (row - CHUNK * k).astype(jnp.float32).astype(jnp.bfloat16)
        count = lax.broadcasted_iota(jnp.int32, (CHUNK, cols), 0)
        count = count.astype(jnp.float32).astype(jnp.bfloat16)
        same = jnp.broadcast_to(local, (CHUNK, cols)) == count
        hot.append(jnp.where(same, jnp.bfloat16(1), jnp.bfloat16(0)))
    got = jnp.dot(pieces_ref[...], jnp.concatenate(hot, 0), preferred_element_type=jnp.float32)
    half = got.shape[0] // 2
    value = (got[:half] + got[half:]).reshape(MANY, SUBSTEPS, cols)
    chosen = value[0]
    for a in range(1, MANY):
        chosen = jnp.where(which == a, value[a], chosen)
    moment = lax.broadcasted_iota(jnp.int32, (SUBSTEPS, cols), 0) + toggle
    share = SUBSTEPS // STEPS
    means = []
    for k in range(STEPS):
        inside = (moment >= k * share) & (moment < (k + 1) * share)
        total = jnp.sum(jnp.where(inside, chosen, 0.0), axis=0, keepdims=True)
        means.append(total * (1.0 / share))
    return means


def lookup_rows(many, index_ref, toggle_ref, pieces_ref, out_ref):
    rows, cols = index_ref.shape

    def body(i, carry):
        for u in range(UNROLL):
            row = pl.ds(i * UNROLL + u, 1)
            means = charges(many, index_ref[row, :], toggle_ref[row, :], pieces_ref)
            for k, mean in enumerate(means):
                for b in range(cols // LANES):
                    out_ref[k, b, row, :] = mean[:, b * LANES : (b + 1) * LANES]
        return carry

    lax.fori_loop(0, rows // UNROLL, body, 0)


def first_lookup_kernel(many, index_ref, toggle_ref, own_ref, other_ref, out_ref, pieces_ref):
    split_kernel((own_ref, other_ref), pieces_ref)
    lookup_rows(many, index_ref, toggle_ref, pieces_ref, out_ref)


def lookup_cost(cells, pieces):
    flops = 2 * cells * pieces.shape[0] * pieces.shape[1]
    return pl.CostEstimate(flops=flops, bytes_accessed=0, transcendentals=0)


def lookup(index, toggle, table, many):
    rows, cols = index.shape
    charge = jax.ShapeDtypeStruct((STEPS, cols // LANES, rows, LANES), jnp.float32)
    fresh = len(table) == 2
    pieces = table[0]
    if fresh:
        pieces = jax.ShapeDtypeStruct((2 * MANY * SUBSTEPS, pieces.shape[0]), jnp.bfloat16)
    return pl.pallas_call(
        functools.partial(first_lookup_kernel if fresh else lookup_rows, many),
        out_shape=[charge, pieces] if fresh else charge,
        in_specs=[vmem()] * (2 + len(table)),
        out_specs=[vmem()] * 2 if fresh else vmem(),
        compiler_params=params(20),
        cost_estimate=lookup_cost(rows * cols, pieces),
        name="lookup",
    )(index, toggle, *table)


def edge_lookup_kernel(many, left_ref, right_ref, pieces_ref, out_ref, cells_ref, got_ref):
    rows = left_ref.shape[1]
    lane = lax.broadcasted_iota(jnp.int32, (rows, LANES), 1)

    def merge(right, left):
        return jnp.where(lane < HALO, right, jnp.where(lane >= LANES - HALO, left, 0.0))

    for f in range(5):
        out_ref[f] = merge(right_ref[f], left_ref[f])
    pair = lax.broadcasted_iota(jnp.int32, (HALO, LANES), 1)
    for n in range(2):
        near = pltpu.roll(merge(right_ref[5 + n], left_ref[5 + n]), HALO, axis=1)
        turned = jnp.concatenate([near, jnp.zeros_like(near)], axis=0).T
        high = pltpu.roll(turned[HALO : 2 * HALO], LANES - rows, axis=1)
        cells_ref[n] = jnp.where(pair < rows, turned[:HALO], high).astype(jnp.int32)
    got_ref[...] = jnp.zeros_like(got_ref)
    step = 4
    for u in range(HALO // step):
        index, toggle = [
            jnp.concatenate([cells_ref[n, pl.ds(step * u + r, 1), :] for r in range(step)], axis=1)
            for n in range(2)
        ]
        for k, mean in enumerate(charges(many, index, toggle, pieces_ref)):
            for r in range(step):
                got_ref[k, pl.ds(step * u + r, 1), :] = mean[:, r * LANES : (r + 1) * LANES]
    inside = out_ref[0] > 0.0
    for k in range(STEPS):
        back = got_ref[k].T
        left = pltpu.roll(back[:rows], LANES - HALO, axis=1)
        out_ref[5 + k] = jnp.where(inside, merge(back[rows:], left), 0.0)


def edge_lookup(left, right, pieces, many):
    rows = left.shape[1]
    assert 2 * rows == LANES
    return pl.pallas_call(
        functools.partial(edge_lookup_kernel, many),
        out_shape=jax.ShapeDtypeStruct(left.shape, jnp.float32),
        in_specs=[vmem()] * 3,
        out_specs=vmem(),
        scratch_shapes=[
            pltpu.VMEM((2, HALO, LANES), jnp.int32),
            pltpu.VMEM((STEPS, LANES, LANES), jnp.float32),
        ],
        compiler_params=params(20),
        cost_estimate=lookup_cost(2 * HALO * rows, pieces),
        name="edge_lookup",
    )(left, right, pieces)


def sweep(deep, fetch, use):
    def load(i):
        if i < 0:
            return [pltpu.roll(fetch(l, deep - 1), 1, axis=0) for l in range(2)]
        if i >= deep:
            return [pltpu.roll(fetch(l, 0), GROUP - 1, axis=0) for l in range(2)]
        return [fetch(l, i) for l in range(2)]

    held = {}
    for i in range(deep):
        held = {k: v for k, v in held.items() if k in (i - 1, i, i + 1)}
        for k in (i - 1, i, i + 1):
            if k not in held:
                held[k] = load(k)
        for l in range(2):
            center = held[i][l]
            width = center.shape[-1]
            beside = pltpu.roll(center, 1, axis=1) + pltpu.roll(center, width - 1, axis=1)
            around = (held[i - 1][l] + held[i + 1][l]) + beside
            use(l, i, center, around, held[i][1 - l])


def weigh(cap_ref, deep, grid_ref, cross_ref):
    for l in range(2):
        for i in range(deep):
            cap = cap_ref[l, i]
            inverse = jnp.where(cap > 0.0, 1.0 / (cap + (4.0 * CONDUCT[l] + 2.0)), 0.0)
            grid_ref[l, i] = CONDUCT[l] * inverse
            cross_ref[l, i] = 2.0 * inverse


def residual(deep, drop_ref, current, cross_ref, width, start_ref, scaled_ref):
    def use(l, i, center, around, other):
        value = CONDUCT[l] * around + 2.0 * other - (4.0 * CONDUCT[l] + 2.0) * center
        if l == 0:
            value = value + current(i)
        start_ref[l, i] = value[:, :width]
        scaled_ref[l, i] = value * (cross_ref[l, i] * 0.5)

    sweep(deep, lambda l, i: drop_ref[l, i], use)


def krylov(deep, width, cap_ref, grid_ref, cross_ref, scaled_ref, second_ref, basis_ref, image_ref):
    def coupled(l, i, around, other):
        return grid_ref[l, i] * around + cross_ref[l, i] * other

    def use_second(l, i, center, around, other):
        second_ref[l, i] = (ALPHA / BETA) * center + coupled(l, i, around, other)

    for n in range(3):

        def use_basis(l, i, center, around, other, n=n):
            value = KEEP * center + (
                scaled_ref[l, i] + BETA * coupled(l, i, around, other)
            )
            if n == 1:
                value = value - BACK * basis_ref[0, l, i]
            if n == 2:
                value = value - BACK * basis_ref[1, l, i] - FORMER * basis_ref[0, l, i]
            basis_ref[n, l, i] = value

        def use_image(l, i, center, around, other, n=n):
            value = center - coupled(l, i, around, other)
            if n < 2:
                scaled_ref[l, i] = value
            diagonal = cap_ref[l, i][:, :width] + (4.0 * CONDUCT[l] + 2.0)
            image_ref[n, l, i] = value[:, :width] * diagonal

        sweep(deep, lambda l, i: scaled_ref[l, i], use_second)
        sweep(deep, lambda l, i: second_ref[l, i], use_basis)
        sweep(deep, lambda l, i, n=n: basis_ref[n, l, i], use_image)


PAIRS = ((0, 0), (1, 0), (2, 0), (1, 1), (2, 1), (2, 2))


def moments(deep, rows, width, start_ref, basis_ref, image_ref, sums_ref, out_ref):
    sub = lax.broadcasted_iota(jnp.int32, (GROUP, LANES), 0)

    def body(i, totals):
        inside = sub * deep + i < rows
        part = [None] * 9
        for l in range(2):
            for b in range(width // LANES):
                lanes = pl.ds(b * LANES, LANES)
                start = start_ref[l, i, :, lanes]
                basis = [basis_ref[n, l, i, :, lanes] for n in range(3)]
                image = [image_ref[n, l, i, :, lanes] for n in range(3)]
                terms = [start * v for v in basis] + [basis[p] * image[q] for p, q in PAIRS]
                part = [t if p is None else p + t for p, t in zip(part, terms)]
        return [t + jnp.where(inside, p, 0.0) for t, p in zip(totals, part)]

    totals = lax.fori_loop(0, deep, body, [jnp.zeros((GROUP, LANES), jnp.float32)] * 9)
    sums_ref[...] = jnp.zeros_like(sums_ref)
    for k, total in enumerate(totals):
        sums_ref[pl.ds(k, 1), :] = jnp.sum(total, axis=0, keepdims=True)
    row = lax.dot_general(
        jnp.ones((GROUP, LANES), jnp.float32),
        sums_ref[...],
        (((1,), (1,)), ((), ())),
        precision=lax.Precision.HIGHEST,
        preferred_element_type=jnp.float32,
    )
    out_ref[...] = jnp.broadcast_to(row[:1], out_ref.shape)


def weights_of(gathered_ref, spread_ref):
    total = jnp.sum(gathered_ref[...], axis=0, keepdims=True)
    row = lax.broadcasted_iota(jnp.int32, (LANES, LANES), 0)
    lane = lax.broadcasted_iota(jnp.int32, (LANES, LANES), 1)
    spread_ref[...] = lax.dot_general(
        jnp.where(row == lane, jnp.broadcast_to(total, (LANES, LANES)), 0.0),
        jnp.ones((LANES, LANES), jnp.float32),
        (((1,), (0,)), ((), ())),
        precision=lax.Precision.HIGHEST,
        preferred_element_type=jnp.float32,
    )
    b1, b2, b3, h11, h21, h31, h22, h32, h33 = [
        jnp.broadcast_to(spread_ref[pl.ds(k, 1), :], (GROUP, LANES)) for k in range(9)
    ]
    l21 = h21 / h11
    l31 = h31 / h11
    d2 = h22 - l21 * h21
    e32 = h32 - l31 * h21
    l32 = e32 / d2
    d3 = h33 - l31 * h31 - l32 * e32
    y2 = b2 - l21 * b1
    y3 = b3 - l31 * b1 - l32 * y2
    c3 = y3 / d3
    c2 = y2 / d2 - l32 * c3
    c1 = b1 / h11 - l21 * c2 - l31 * c3
    return c1, c2, c3


def widen(value, width):
    return jnp.concatenate([value] * (width // LANES), axis=1)


def spread(natural_ref, l, i, deep, value):
    for b in range(value.shape[1] // LANES):
        natural_ref[l, b, pl.ds(i, GROUP, stride=deep), :] = value[:, b * LANES : (b + 1) * LANES]


def settle(natural_ref, out_ref):
    for b in range(natural_ref.shape[1]):
        out_ref[:, :, pl.ds(b * LANES, LANES)] = natural_ref[:, b, : out_ref.shape[1], :]


def first_kernel(
    deep, rows, width, outer,
    field_ref, edge_ref, above_ref, below_ref, ends_ref, middle_ref,
    basis_ref, drop_ref, cap_ref, later_ref, out_ref,
    whole_ref, grid_ref, cross_ref, start_ref, scaled_ref, second_ref, image_ref, inject_ref, sums_ref,
):
    wide = width + LANES
    blocks = wide // LANES
    inner = pl.ds(0, rows)
    for f in range(7):
        whole_ref[f, blocks - 1, inner, :] = edge_ref[f]
        for b in range(blocks - 1):
            if f < 5:
                whole_ref[f, b, inner, :] = field_ref[f, b]
            else:
                end, middle = ends_ref.at[f - 5, b], middle_ref.at[f - 5, b]
                whole_ref[f, b, pl.ds(0, outer), :] = end[pl.ds(0, outer), :]
                whole_ref[f, b, pl.ds(outer, rows - 2 * outer), :] = middle[...]
                whole_ref[f, b, pl.ds(rows - outer, outer), :] = end[pl.ds(outer, outer), :]
        for ref, place in ((below_ref, pl.ds(rows, HALO)), (above_ref, pl.ds(rows + HALO, HALO))):
            for b in range(blocks - 1):
                whole_ref[f, b, place, :] = ref[f * (blocks - 1) + b]
            whole_ref[f, blocks - 1, place, :] = ref[7 * (blocks - 1) + f]

    def slab(f, i):
        pick = pl.ds(i, GROUP, stride=deep)
        return jnp.concatenate([whole_ref[f, b, pick, :] for b in range(blocks)], axis=1)

    for l in range(2):
        for i in range(deep):
            cap_ref[l, i] = slab(l, i)
            drop_ref[l, i] = slab(2 + l, i)
    weigh(cap_ref, deep, grid_ref, cross_ref)
    for i in range(deep):
        tap = slab(4, i)
        for k in range(STEPS):
            charge = slab(5 + k, i)
            for a in range(3):
                sent = [jnp.where(tap == float(3 * a + b), charge, 0.0) for b in range(3)]
                value = pltpu.roll(sent[0], wide - 1, axis=1) + sent[1] + pltpu.roll(sent[2], 1, axis=1)
                inject_ref[k, a, i] = value

    def current(k, i):
        if i == deep - 1:
            upward = pltpu.roll(inject_ref[k, 0, 0], GROUP - 1, axis=0)
        else:
            upward = inject_ref[k, 0, i + 1]
        if i == 0:
            downward = pltpu.roll(inject_ref[k, 2, deep - 1], 1, axis=0)
        else:
            downward = inject_ref[k, 2, i - 1]
        return upward + inject_ref[k, 1, i] + downward

    for i in range(deep):
        later_ref[i] = current(1, i)
    residual(deep, drop_ref, lambda i: current(0, i), cross_ref, width, start_ref, scaled_ref)
    krylov(deep, width, cap_ref, grid_ref, cross_ref, scaled_ref, second_ref, basis_ref, image_ref)
    moments(deep, rows, width, start_ref, basis_ref, image_ref, sums_ref, out_ref)


def first_step(field, edge, above, below, ends, middle, count):
    rows = field.shape[2]
    width = field.shape[1] * LANES
    wide = width + LANES
    deep = (rows + 2 * HALO) // GROUP
    full = (2, deep, GROUP, wide)
    shapes = [(3, *full), full, full, full[1:], (count, LANES)]
    return pl.pallas_call(
        functools.partial(first_kernel, deep, rows, width, ends.shape[2] // 2),
        out_shape=[jax.ShapeDtypeStruct(s, jnp.float32) for s in shapes],
        in_specs=[vmem()] * 6,
        out_specs=[vmem()] * len(shapes),
        scratch_shapes=[
            pltpu.VMEM((7, wide // LANES, deep * GROUP, LANES), jnp.float32),
            pltpu.VMEM(full, jnp.float32),
            pltpu.VMEM(full, jnp.float32),
            pltpu.VMEM((2, deep, GROUP, width), jnp.float32),
            pltpu.VMEM(full, jnp.float32),
            pltpu.VMEM(full, jnp.float32),
            pltpu.VMEM((3, 2, deep, GROUP, width), jnp.float32),
            pltpu.VMEM((STEPS, 3, *full[1:]), jnp.float32),
            pltpu.VMEM((LANES, LANES), jnp.float32),
        ],
        compiler_params=params(20),
        name="first_step",
    )(field, edge, above, below, ends, middle)


def second_kernel(
    deep, rows, width,
    gathered_ref, basis_ref, drop_ref, cap_ref, later_ref,
    first_ref, next_ref, held_ref, out_ref,
    now_ref, grid_ref, cross_ref, start_ref, scaled_ref, second_ref, image_ref, natural_ref, sums_ref,
):
    wide = width + LANES
    weigh(cap_ref, deep, grid_ref, cross_ref)
    weights = [widen(c, wide) for c in weights_of(gathered_ref, sums_ref)]
    for l in range(2):
        for i in range(deep):
            value = drop_ref[l, i]
            for n in range(3):
                value = value + weights[n] * basis_ref[n, l, i]
            now_ref[l, i] = value
            held_ref[l, i] = value[:, :width]
            spread(natural_ref, l, i, deep, value[:, :width])
    settle(natural_ref, first_ref)
    residual(deep, now_ref, lambda i: later_ref[i], cross_ref, width, start_ref, scaled_ref)
    krylov(deep, width, cap_ref, grid_ref, cross_ref, scaled_ref, second_ref, next_ref, image_ref)
    moments(deep, rows, width, start_ref, next_ref, image_ref, sums_ref, out_ref)


def second_step(gathered, basis, drop, cap, later, rows):
    deep = cap.shape[1]
    wide = cap.shape[-1]
    width = wide - LANES
    full = (2, deep, GROUP, wide)
    shapes = [(2, rows, width), (3, *full), (2, deep, GROUP, width), gathered.shape]
    return pl.pallas_call(
        functools.partial(second_kernel, deep, rows, width),
        out_shape=[jax.ShapeDtypeStruct(s, jnp.float32) for s in shapes],
        in_specs=[vmem()] * 5,
        out_specs=[vmem()] * len(shapes),
        scratch_shapes=[
            pltpu.VMEM(full, jnp.float32),
            pltpu.VMEM(full, jnp.float32),
            pltpu.VMEM(full, jnp.float32),
            pltpu.VMEM((2, deep, GROUP, width), jnp.float32),
            pltpu.VMEM(full, jnp.float32),
            pltpu.VMEM(full, jnp.float32),
            pltpu.VMEM((3, 2, deep, GROUP, width), jnp.float32),
            pltpu.VMEM((2, width // LANES, deep * GROUP, LANES), jnp.float32),
            pltpu.VMEM((LANES, LANES), jnp.float32),
        ],
        compiler_params=params(20),
        name="second_step",
    )(gathered, basis, drop, cap, later)


def last_kernel(deep, rows, width, gathered_ref, basis_ref, held_ref, out_ref, natural_ref, sums_ref):
    weights = [widen(c, width) for c in weights_of(gathered_ref, sums_ref)]
    for l in range(2):
        for i in range(deep):
            value = held_ref[l, i]
            for n in range(3):
                value = value + weights[n] * basis_ref[n, l, i, :, pl.ds(0, width)]
            spread(natural_ref, l, i, deep, value)
    settle(natural_ref, out_ref)


def last_step(gathered, basis, held, rows):
    deep = held.shape[1]
    width = held.shape[-1]
    return pl.pallas_call(
        functools.partial(last_kernel, deep, rows, width),
        out_shape=jax.ShapeDtypeStruct((2, rows, width), jnp.float32),
        in_specs=[vmem()] * 3,
        out_specs=vmem(),
        scratch_shapes=[
            pltpu.VMEM((2, width // LANES, deep * GROUP, LANES), jnp.float32),
            pltpu.VMEM((LANES, LANES), jnp.float32),
        ],
        compiler_params=params(12),
        name="last_step",
    )(gathered, basis, held)


def shift(block, axis, up):
    count = lax.axis_size(axis)
    pairs = [(i, i + 1) for i in range(count - 1)]
    return lax.ppermute(block, axis, pairs if up else [(b, a) for a, b in pairs])


def exchange(block):
    return lax.all_to_all(block, BOTH, 0, 0, tiled=True)


def gather_tables(tables):
    outer, inner = lax.axis_size("gx"), lax.axis_size("gy")
    groups = [
        [x * inner + y for x in range(parity, outer, 2) for y in range(inner)] for parity in range(2)
    ]
    block = address(tables, outer * inner // 2)
    own = lax.all_to_all(block, BOTH, 0, 0, tiled=True, axis_index_groups=groups)
    own = own.reshape(-1, LANES)
    return own, lax.ppermute(own, "gx", [(i, i ^ 1) for i in range(outer)])


def shards(tables, table_index, toggle, tap_code, capacitance, prior_drop):
    rows, cols = table_index.shape
    count = lax.axis_size("gx") * lax.axis_size("gy")
    inner = lax.axis_size("gy")
    many = tables.shape[0], inner
    outer = HALO
    table = gather_tables(tables)
    table_index = table_index ^ ((lax.axis_index("gx") & 1) * (inner * tables.shape[0]))
    codes = [a.astype(jnp.float32)[None] for a in (tap_code, table_index, toggle)]
    field = jnp.concatenate([capacitance, prior_drop, *codes])
    field = field.reshape(-1, rows, cols // LANES, LANES).transpose(0, 2, 1, 3)
    left = shift(field[:, -1], "gy", True)
    right = shift(field[:, 0], "gy", False)
    def ends_of(array):
        return jnp.concatenate([array[:outer], array[-outer:]])

    ends, pieces = lookup(ends_of(table_index), ends_of(toggle), table, many)
    edge = edge_lookup(left, right, pieces, many)

    def late(far):
        cut = slice(-HALO, None) if far else slice(0, HALO)
        charge, lower = [a[:, :, cut].reshape(-1, HALO, LANES) for a in (ends, field[:5])]
        return jnp.concatenate([lower, charge, edge[:, cut]])

    above = shift(late(True), "gx", True)
    below = shift(late(False), "gx", False)
    pieces, edge = lax.optimization_barrier((pieces, edge))
    middle = lookup(table_index[outer:-outer], toggle[outer:-outer], (pieces,), many)
    basis, drop, cap, later, part = first_step(field, edge, above, below, ends, middle, count)
    first, basis, held, part = second_step(exchange(part), basis, drop, cap, later, rows)
    return first, last_step(exchange(part), basis, held, rows)


def solution(mesh):
    in_specs = (
        P(BOTH, None),
        P("gx", "gy"),
        P("gx", "gy"),
        P("gx", "gy"),
        P(None, "gx", "gy"),
        P(None, "gx", "gy"),
    )
    out_specs = (P(None, "gx", "gy"), P(None, "gx", "gy"))
    return jax.shard_map(shards, mesh=mesh, in_specs=in_specs, out_specs=out_specs, check_vma=False)
```

time: 1670 us -> 114 us (0.07)
  blocking collectives: 925 us -> 40.7 us
  local copies, waits for them, and re-layouts: 363 us -> 1.11 us
  starting transfers between devices: 200 us -> 29.3 us
  waiting for transfers between devices: 135 us -> 6.88 us
  Pallas kernels: 0 us -> 32.8 us
  other arithmetic: 18.9 us -> 1.93 us
    psum x10 -> x0, blocking collectives: 805 us -> none  [the longest x6 490 us: global_inner(): return lax.psum(jnp.sum(left * right), ('gx', 'gy'))]
    gather x4 -> x0, local copies, waits for them, and re-layouts: 361 us -> none  [shards(): charges = [jnp.take(flat, base + k) for k in range(STEPS)]]
    ppermute x84 -> x5, starting transfers between devices: 200 us -> 13 us  [the longest x4 10.1 us: shift(): lax.ppermute(block, axis, pairs if up else [(b, a) for a, b in pairs])]
    ppermute x84 -> x5, waiting for transfers between devices: 135 us -> 1.18 us  [the longest x1 1.06 us: gather_tables(): return (own, lax.ppermute(own, 'gx', [(i, i ^ 1) for i in range(outer)]))]
    all_gather x1 -> x0, blocking collectives: 121 us -> none  [shards(): lax.all_gather(tables, ('gx', 'gy'), axis=0, tiled=True)]
    all_to_all x0 -> x2, blocking collectives: none -> 40.7 us  [exchange(): return lax.all_to_all(block, BOTH, 0, 0, tiled=True)]
    pallas_call x0 -> x7, Pallas kernels: none -> 32.8 us  [the longest x2 19.5 us: lookup(): pl.pallas_call(functools.partial(first_lookup_kernel if fresh else lookup...]
  transfers between devices with their start and end apart: 84 -> 6, of which waited for: 58 -> 3; matrix products, arithmetic and copies ran while one was open for 22% -> 2% of each run, Pallas kernels for 0% -> 17%
where the time goes in v1:
time: 114 us
  blocking collectives  40.7 us (36%)
  Pallas kernels  32.8 us (29%)
  starting transfers between devices  29.3 us (26%)
  waiting for transfers between devices  6.88 us (6%)
  other arithmetic  1.93 us (2%)
    all_to_all x2, blocking collectives, exchange(): return lax.all_to_all(block, BOTH, 0, 0, tiled=True)  40.7 us
    pallas_call x2, Pallas kernels, lookup(): pl.pallas_call(functools.partial(first_lookup_kernel if fresh else lookup...  19.5 us
    all_to_all x1, starting transfers between devices, gather_tables(): lax.all_to_all(block, BOTH, 0, 0, tiled=True, axis_index_groups=groups)  16.3 us
    ppermute x4, starting transfers between devices, shift(): lax.ppermute(block, axis, pairs if up else [(b, a) for a, b in pairs])  10.1 us
    all_to_all x1, waiting for transfers between devices, gather_tables(): lax.all_to_all(block, BOTH, 0, 0, tiled=True, axis_index_groups=groups)  5.71 us
    pallas_call x1, Pallas kernels, first_step(): pl.pallas_call(functools.partial(first_kernel, deep, rows, width, ends.sh...  4.82 us
    pallas_call x1, Pallas kernels, second_step(): pl.pallas_call(functools.partial(second_kernel, deep, rows, width), out_s...  4.57 us
    ppermute x1, starting transfers between devices, gather_tables(): return (own, lax.ppermute(own, 'gx', [(i, i ^ 1) for i in range(outer)]))  2.81 us
  transfers between devices with their start and end apart: 6, of which 3 were waited for; matrix products, arithmetic and copies ran while one was open for 2% of the time, Pallas kernels for 17%

profile of v1, /device:TPU:1, one launch (start us, length us, event | category | flops | bytes accessed | tf_op | source)
XLA Modules:
  0.0 113.7 jit_solution(4417609128418147472)
XLA Ops:
  0.6 0.0 copy-start
  0.6 0.0 copy-start.1
  0.7 0.7 copy-done.1
  1.4 0.0 copy-start.4
  1.4 0.8 address.1
  2.2 16.3 %all-to-all-start = ((f32[128,4,128]{2,1,0:T(4,128)}), f32[128,4,128]{2,1,0:T(4,128)S(1)}, u32[]{:S(2)}, u32[]{:S(2)}) async-start(f32[128,4,128]{2,1,0:T(4,128)} %address.1), calls=%async_computation | async-start | bytes 524288 | tf_op jit(solution)/shard_map/all_to_all | solution.py:535
  18.5 0.9 convert_element_type.9
  19.5 0.9 convert_element_type.11
  20.5 0.0 copy-done.4
  20.5 0.0 copy-start.2
  20.6 0.0 copy-done
  20.6 0.0 copy-done.3
  20.8 1.3 %collective-permute-start.2 = (f32[7,64,128]{2,1,0:T(8,128)S(1)}, f32[7,64,128]{2,1,0:T(8,128)S(1)}, u32[]{:S(2)}, u32[]{:S(2)}) collective-permute-start(f32[7,64,128]{2,1,0:T(8,128)S(1)} %get-tuple-element.32), channel_id=1, source_target_pairs={{1,0},{2,1},{3,2},{4,3},{5,4},{6,5},{7,6},{8,7},{9,8},{10,9},{11,1... | collective-permute-start | bytes 688136 | tf_op jit(solution)/shard_map/ppermute | solution.py:522
  22.1 4.0 %collective-permute-start.1 = (f32[7,64,128]{2,1,0:T(8,128)S(1)}, f32[7,64,128]{2,1,0:T(8,128)S(1)}, u32[]{:S(2)}, u32[]{:S(2)}) collective-permute-start(f32[7,64,128]{2,1,0:T(8,128)S(1)} %get-tuple-element.33), channel_id=1, source_target_pairs={{0,1},{1,2},{2,3},{3,4},{4,5},{5,6},{6,7},{7,8},{8,9},{9,10},{10,1... | collective-permute-start | bytes 688136 | tf_op jit(solution)/shard_map/ppermute | solution.py:522
  26.1 0.0 copy-done.2
  26.1 5.7 %all-to-all-done = f32[128,4,128]{2,1,0:T(4,128)S(1)} async-done(((f32[128,4,128]{2,1,0:T(4,128)}), f32[128,4,128]{2,1,0:T(4,128)S(1)}, u32[]{:S(2)}, u32[]{:S(2)}) %all-to-all-start) | async-done | bytes 262176 | tf_op jit(solution)/shard_map/all_to_all | solution.py:535
  31.8 2.8 %collective-permute-start = (f32[512,128]{1,0:T(8,128)S(1)}, f32[512,128]{1,0:T(8,128)S(1)}, u32[]{:S(2)}, u32[]{:S(2)}) collective-permute-start(f32[512,128]{1,0:T(8,128)S(1)} %bitcast.33), channel_id=1, source_target_pairs={{0,16},{16,0},{32,48},{48,32},{64,80},{80,64},{96,112},{112,96},{1... | collective-permute-start | bytes 786440 | tf_op jit(solution)/shard_map/ppermute | solution.py:537
  34.8 1.1 collective-permute-done.other_ref
  35.8 12.3 %lookup.2 = (f32[2,4,40,128]{3,2,1,0:T(8,128)S(1)}, bf16[512,512]{1,0:T(8,128)(2,1)S(1)}) custom-call(s32[40,512]{1,0:T(8,128)S(1)} %get-tuple-element.42.index_ref, s32[40,512]{1,0:T(8,128)S(1)} %get-tuple-element.43.toggle_ref, f32[512,128]{1,0:T(8,128)S(1)} %bitcast.34, f32[512,128]{1,0:T(8,128)S(1)} %collective-permute-done.other_ref), custom_call_target="tpu_custom_call" | custom-call | flops 10737418240 | tf_op jit(solution)/shard_map/lookup/pallas_call | solution.py:144
  48.1 0.0 collective-permute-done.2.right_ref
  48.1 0.0 collective-permute-done.1.left_ref
  48.1 2.0 %edge_lookup.1.edge_ref = f32[7,64,128]{2,1,0:T(8,128)S(1)} custom-call(f32[7,64,128]{2,1,0:T(8,128)S(1)} %collective-permute-done.1.left_ref, f32[7,64,128]{2,1,0:T(8,128)S(1)} %collective-permute-done.2.right_ref, bf16[512,512]{1,0:T(8,128)(2,1)S(1)} %get-tuple-element.18.pieces_ref), custom_call_target="tpu_custom_call" | custom-call | flops 1342177280 | tf_op jit(solution)/shard_map/edge_lookup/pallas_call | solution.py:190
  50.2 2.7 %collective-permute-start.3 = (f32[35,20,128]{2,1,0:T(8,128)S(1)}, f32[35,20,128]{2,1,0:T(8,128)S(1)}, u32[]{:S(2)}, u32[]{:S(2)}) collective-permute-start(f32[35,20,128]{2,1,0:T(8,128)S(1)} %pad_maximum_fusion), channel_id=1, source_target_pairs={{0,16},{16,32},{32,48},{48,64},{64,80},{80,96},{96,112},{112,128},... | collective-permute-start | bytes 1075208 | tf_op jit(solution)/shard_map/ppermute | solution.py:522
  53.0 2.1 %collective-permute-start.4 = (f32[35,20,128]{2,1,0:T(8,128)S(1)}, f32[35,20,128]{2,1,0:T(8,128)S(1)}, u32[]{:S(2)}, u32[]{:S(2)}) collective-permute-start(f32[35,20,128]{2,1,0:T(8,128)S(1)} %pad_maximum_fusion.1), channel_id=1, source_target_pairs={{16,0},{32,16},{48,32},{64,48},{80,64},{96,80},{112,96},{128,112},... | collective-permute-start | bytes 1075208 | tf_op jit(solution)/shard_map/ppermute | solution.py:522
  55.1 7.3 %lookup.3.middle_ref = f32[2,4,24,128]{3,2,1,0:T(8,128)S(1)} custom-call(s32[24,512]{1,0:T(8,128)S(1)} %slice.68.index_ref, s32[24,512]{1,0:T(8,128)S(1)} %slice.59.toggle_ref, bf16[512,512]{1,0:T(8,128)(2,1)S(1)} %get-tuple-element.18.pieces_ref), custom_call_target="tpu_custom_call" | custom-call | flops 6442450944 | tf_op jit(solution)/shard_map/lookup/pallas_call | solution.py:144
  62.4 0.0 collective-permute-done.3.above_ref
  62.4 0.1 collective-permute-done.4.below_ref
  62.5 4.8 %first_step.1 = (f32[3,2,13,8,640]{4,3,2,1,0:T(8,128)S(1)}, f32[2,13,8,640]{3,2,1,0:T(8,128)S(1)}, f32[2,13,8,640]{3,2,1,0:T(8,128)S(1)}, f32[13,8,640]{2,1,0:T(8,128)S(1)}, f32[256,128]{1,0:T(8,128)S(1)}) custom-call(f32[7,4,64,128]{3,2,1,0:T(8,128)S(1)} %bitcast.30, f32[7,64,128]{2,1,0:T(8,128)S(1)} %edge_lookup.1.edge_ref, ...), custom_call_target="tpu_custom_call" | custom-call | tf_op jit(solution)/shard_map/first_step/pallas_call | solution.py:420
  67.3 22.3 %all_to_all.27 = f32[256,1,128]{2,1,0:T(1,128)S(1)} all-to-all(f32[256,1,128]{2,1,0:T(1,128)S(1)} %bitcast.35), channel_id=1, replica_groups=mesh['gx'=16,'gy'=16] {'gx','gy'}, dimensions={0} | all-to-all | bytes 262144 | tf_op jit(solution)/shard_map/all_to_all | solution.py:526
  89.6 4.6 %second_step.1 = (f32[2,64,512]{2,1,0:T(8,128)}, f32[3,2,13,8,640]{4,3,2,1,0:T(8,128)S(1)}, f32[2,13,8,512]{3,2,1,0:T(8,128)S(1)}, f32[256,128]{1,0:T(8,128)S(1)}) custom-call(f32[256,128]{1,0:T(8,128)S(1)} %bitcast.31, f32[3,2,13,8,640]{4,3,2,1,0:T(8,128)S(1)} %get-tuple-element.20.basis_ref, f32[2,13,8,640]{3,2,1,0:T(8,128)S(1)} %get-tuple-element.21.drop_ref, ...), custom_call_target="tpu_custom_call" | custom-call | tf_op jit(solution)/shard_map/second_step/pallas_call | solution.py:470
  94.2 18.4 %all_to_all.28 = f32[256,1,128]{2,1,0:T(1,128)S(1)} all-to-all(f32[256,1,128]{2,1,0:T(1,128)S(1)} %bitcast.36), channel_id=1, replica_groups=mesh['gx'=16,'gy'=16] {'gx','gy'}, dimensions={0} | all-to-all | bytes 262144 | tf_op jit(solution)/shard_map/all_to_all | solution.py:526
  112.6 1.1 last_step.1
  (21 shorter events, 0.5 us)
Async XLA Ops:
  0.6 20.0 %copy-start = (f32[2,64,512]{2,1,0:T(8,128)S(1)}, f32[2,64,512]{2,1,0:T(8,128)}, u32[]{:S(2)}) copy-start(f32[2,64,512]{2,1,0:T(8,128)} %param.10) | copy-start | bytes 786436
  0.6 0.7 copy-start.1
  1.4 19.1 %copy-start.4 = (s32[64,512]{1,0:T(8,128)S(1)}, s32[64,512]{1,0:T(8,128)}, u32[]{:S(2)}) copy-start(s32[64,512]{1,0:T(8,128)} %param.7) | copy-start | bytes 393220
  1.4 19.3 %copy-start.3 = (f32[2,64,512]{2,1,0:T(8,128)S(1)}, f32[2,64,512]{2,1,0:T(8,128)}, u32[]{:S(2)}) copy-start(f32[2,64,512]{2,1,0:T(8,128)} %param.11) | copy-start | bytes 786436
  2.2 29.6 %all-to-all-start = ((f32[128,4,128]{2,1,0:T(4,128)}), f32[128,4,128]{2,1,0:T(4,128)S(1)}, u32[]{:S(2)}, u32[]{:S(2)}) async-start(f32[128,4,128]{2,1,0:T(4,128)} %address.1), calls=%async_computation | async-start | bytes 524288 | tf_op jit(solution)/shard_map/all_to_all | solution.py:535
  20.5 5.5 %copy-start.2 = (s32[64,512]{1,0:T(8,128)S(1)}, s32[64,512]{1,0:T(8,128)}, u32[]{:S(2)}) copy-start(s32[64,512]{1,0:T(8,128)} %param.8) | copy-start | bytes 393220
  20.8 27.3 %collective-permute-start.2 = (f32[7,64,128]{2,1,0:T(8,128)S(1)}, f32[7,64,128]{2,1,0:T(8,128)S(1)}, u32[]{:S(2)}, u32[]{:S(2)}) collective-permute-start(f32[7,64,128]{2,1,0:T(8,128)S(1)} %get-tuple-element.32), channel_id=1, source_target_pairs={{1,0},{2,1},{3,2},{4,3},{5,4},{6,5},{7,6},{8,7},{9,8},{10,9},{11,1... | collective-permute-start | bytes 688136 | tf_op jit(solution)/shard_map/ppermute | solution.py:522
  22.1 26.1 %collective-permute-start.1 = (f32[7,64,128]{2,1,0:T(8,128)S(1)}, f32[7,64,128]{2,1,0:T(8,128)S(1)}, u32[]{:S(2)}, u32[]{:S(2)}) collective-permute-start(f32[7,64,128]{2,1,0:T(8,128)S(1)} %get-tuple-element.33), channel_id=1, source_target_pairs={{0,1},{1,2},{2,3},{3,4},{4,5},{5,6},{6,7},{7,8},{8,9},{9,10},{10,1... | collective-permute-start | bytes 688136 | tf_op jit(solution)/shard_map/ppermute | solution.py:522
  31.8 4.0 %collective-permute-start = (f32[512,128]{1,0:T(8,128)S(1)}, f32[512,128]{1,0:T(8,128)S(1)}, u32[]{:S(2)}, u32[]{:S(2)}) collective-permute-start(f32[512,128]{1,0:T(8,128)S(1)} %bitcast.33), channel_id=1, source_target_pairs={{0,16},{16,0},{32,48},{48,32},{64,80},{80,64},{96,112},{112,96},{1... | collective-permute-start | bytes 786440 | tf_op jit(solution)/shard_map/ppermute | solution.py:537
  50.2 12.2 %collective-permute-start.3 = (f32[35,20,128]{2,1,0:T(8,128)S(1)}, f32[35,20,128]{2,1,0:T(8,128)S(1)}, u32[]{:S(2)}, u32[]{:S(2)}) collective-permute-start(f32[35,20,128]{2,1,0:T(8,128)S(1)} %pad_maximum_fusion), channel_id=1, source_target_pairs={{0,16},{16,32},{32,48},{48,64},{64,80},{80,96},{96,112},{112,128},... | collective-permute-start | bytes 1075208 | tf_op jit(solution)/shard_map/ppermute | solution.py:522
  53.0 9.5 %collective-permute-start.4 = (f32[35,20,128]{2,1,0:T(8,128)S(1)}, f32[35,20,128]{2,1,0:T(8,128)S(1)}, u32[]{:S(2)}, u32[]{:S(2)}) collective-permute-start(f32[35,20,128]{2,1,0:T(8,128)S(1)} %pad_maximum_fusion.1), channel_id=1, source_target_pairs={{16,0},{32,16},{48,32},{64,48},{80,64},{96,80},{112,96},{128,112},... | collective-permute-start | bytes 1075208 | tf_op jit(solution)/shard_map/ppermute | solution.py:522

commit v2 on v1

--- a/solution.py
+++ b/solution.py
@@ -308,8 +308,8 @@
     out_ref[...] = jnp.broadcast_to(row[:1], out_ref.shape)
 
 
-def weights_of(gathered_ref, spread_ref):
-    total = jnp.sum(gathered_ref[...], axis=0, keepdims=True)
+def weights_of(own_ref, other_ref, spread_ref):
+    total = jnp.sum(own_ref[...], axis=0, keepdims=True) + jnp.sum(other_ref[...], axis=0, keepdims=True)
     row = lax.broadcasted_iota(jnp.int32, (LANES, LANES), 0)
     lane = lax.broadcasted_iota(jnp.int32, (LANES, LANES), 1)
     spread_ref[...] = lax.dot_general(
@@ -440,13 +440,13 @@
 
 def second_kernel(
     deep, rows, width,
-    gathered_ref, basis_ref, drop_ref, cap_ref, later_ref,
+    own_ref, other_ref, basis_ref, drop_ref, cap_ref, later_ref,
     first_ref, next_ref, held_ref, out_ref,
     now_ref, grid_ref, cross_ref, start_ref, scaled_ref, second_ref, image_ref, natural_ref, sums_ref,
 ):
     wide = width + LANES
     weigh(cap_ref, deep, grid_ref, cross_ref)
-    weights = [widen(c, wide) for c in weights_of(gathered_ref, sums_ref)]
+    weights = [widen(c, wide) for c in weights_of(own_ref, other_ref, sums_ref)]
     for l in range(2):
         for i in range(deep):
             value = drop_ref[l, i]
@@ -466,11 +466,11 @@
     wide = cap.shape[-1]
     width = wide - LANES
     full = (2, deep, GROUP, wide)
-    shapes = [(2, rows, width), (3, *full), (2, deep, GROUP, width), gathered.shape]
+    shapes = [(2, rows, width), (3, *full), (2, deep, GROUP, width), gathered[0].shape]
     return pl.pallas_call(
         functools.partial(second_kernel, deep, rows, width),
         out_shape=[jax.ShapeDtypeStruct(s, jnp.float32) for s in shapes],
-        in_specs=[vmem()] * 5,
+        in_specs=[vmem()] * 6,
         out_specs=[vmem()] * len(shapes),
         scratch_shapes=[
             pltpu.VMEM(full, jnp.float32),
@@ -485,11 +485,11 @@
         ],
         compiler_params=params(20),
         name="second_step",
-    )(gathered, basis, drop, cap, later)
-
-
-def last_kernel(deep, rows, width, gathered_ref, basis_ref, held_ref, out_ref, natural_ref, sums_ref):
-    weights = [widen(c, width) for c in weights_of(gathered_ref, sums_ref)]
+    )(*gathered, basis, drop, cap, later)
+
+
+def last_kernel(deep, rows, width, own_ref, other_ref, basis_ref, held_ref, out_ref, natural_ref, sums_ref):
+    weights = [widen(c, width) for c in weights_of(own_ref, other_ref, sums_ref)]
     for l in range(2):
         for i in range(deep):
             value = held_ref[l, i]
@@ -505,7 +505,7 @@
     return pl.pallas_call(
         functools.partial(last_kernel, deep, rows, width),
         out_shape=jax.ShapeDtypeStruct((2, rows, width), jnp.float32),
-        in_specs=[vmem()] * 3,
+        in_specs=[vmem()] * 4,
         out_specs=vmem(),
         scratch_shapes=[
             pltpu.VMEM((2, width // LANES, deep * GROUP, LANES), jnp.float32),
@@ -513,7 +513,7 @@
         ],
         compiler_params=params(12),
         name="last_step",
-    )(gathered, basis, held)
+    )(*gathered, basis, held)
 
 
 def shift(block, axis, up):
@@ -522,16 +522,11 @@
     return lax.ppermute(block, axis, pairs if up else [(b, a) for a, b in pairs])
 
 
-def exchange(block):
-    return lax.all_to_all(block, BOTH, 0, 0, tiled=True)
-
-
-def gather_tables(tables):
+def from_all(block):
     outer, inner = lax.axis_size("gx"), lax.axis_size("gy")
     groups = [
         [x * inner + y for x in range(parity, outer, 2) for y in range(inner)] for parity in range(2)
     ]
-    block = address(tables, outer * inner // 2)
     own = lax.all_to_all(block, BOTH, 0, 0, tiled=True, axis_index_groups=groups)
     own = own.reshape(-1, LANES)
     return own, lax.ppermute(own, "gx", [(i, i ^ 1) for i in range(outer)])
@@ -539,17 +534,22 @@
 
 def shards(tables, table_index, toggle, tap_code, capacitance, prior_drop):
     rows, cols = table_index.shape
-    count = lax.axis_size("gx") * lax.axis_size("gy")
     inner = lax.axis_size("gy")
+    count = lax.axis_size("gx") * inner // 2
     many = tables.shape[0], inner
     outer = HALO
-    table = gather_tables(tables)
+    table = from_all(address(tables, count))
     table_index = table_index ^ ((lax.axis_index("gx") & 1) * (inner * tables.shape[0]))
-    codes = [a.astype(jnp.float32)[None] for a in (tap_code, table_index, toggle)]
-    field = jnp.concatenate([capacitance, prior_drop, *codes])
+
+    def columns(cut):
+        codes = jnp.stack([a[:, cut] for a in (tap_code, table_index, toggle)]).astype(jnp.float32)
+        return jnp.concatenate([capacitance[:, :, cut], prior_drop[:, :, cut], codes])
+
+    left = shift(columns(slice(-LANES, None)), "gy", True)
+    right = shift(columns(slice(0, LANES)), "gy", False)
+    field = jnp.concatenate([capacitance, prior_drop, tap_code.astype(jnp.float32)[None]])
     field = field.reshape(-1, rows, cols // LANES, LANES).transpose(0, 2, 1, 3)
-    left = shift(field[:, -1], "gy", True)
-    right = shift(field[:, 0], "gy", False)
+
     def ends_of(array):
         return jnp.concatenate([array[:outer], array[-outer:]])
 
@@ -558,7 +558,7 @@
 
     def late(far):
         cut = slice(-HALO, None) if far else slice(0, HALO)
-        charge, lower = [a[:, :, cut].reshape(-1, HALO, LANES) for a in (ends, field[:5])]
+        charge, lower = [a[:, :, cut].reshape(-1, HALO, LANES) for a in (ends, field)]
         return jnp.concatenate([lower, charge, edge[:, cut]])
 
     above = shift(late(True), "gx", True)
@@ -566,8 +566,8 @@
     pieces, edge = lax.optimization_barrier((pieces, edge))
     middle = lookup(table_index[outer:-outer], toggle[outer:-outer], (pieces,), many)
     basis, drop, cap, later, part = first_step(field, edge, above, below, ends, middle, count)
-    first, basis, held, part = second_step(exchange(part), basis, drop, cap, later, rows)
-    return first, last_step(exchange(part), basis, held, rows)
+    first, basis, held, part = second_step(from_all(part), basis, drop, cap, later, rows)
+    return first, last_step(from_all(part), basis, held, rows)
 
 
 def solution(mesh):

time: 114 us -> 116 us (1.018)
  blocking collectives: 40.7 us -> 36.2 us
  starting transfers between devices: 29.3 us -> 32.4 us
  local copies, waits for them, and re-layouts: 1.11 us -> 3.46 us
  waiting for transfers between devices: 6.88 us -> 8.51 us
    all_to_all x2, blocking collectives: 40.7 us -> 36.2 us  [from_all(): lax.all_to_all(block, BOTH, 0, 0, tiled=True, axis_index_groups=groups)]
    ppermute x1 -> x3, starting transfers between devices: 2.81 us -> 7.2 us  [from_all(): return (own, lax.ppermute(own, 'gx', [(i, i ^ 1) for i in range(outer)]))]
    convert_element_type x3, other arithmetic: 1.86 us -> 0.03 us  [the longest x2 0.02 us: columns(): jnp.stack([a[:, cut] for a in (tap_code, table_index, toggle)])]
    ppermute x1 -> x3, waiting for transfers between devices: 1.06 us -> 2.87 us  [from_all(): return (own, lax.ppermute(own, 'gx', [(i, i ^ 1) for i in range(outer)]))]
    another operation x0 -> x2, local copies, waits for them, and re-layouts: none -> 1.57 us  [columns(): jnp.stack([a[:, cut] for a in (tap_code, table_index, toggle)])]
    ppermute x4, starting transfers between devices: 10.1 us -> 8.77 us  [shift(): lax.ppermute(block, axis, pairs if up else [(b, a) for a, b in pairs])]
  transfers between devices with their start and end apart: 6 -> 8, of which waited for: 3 -> 5; matrix products, arithmetic and copies ran while one was open for 2% -> 3% of each run, Pallas kernels for 17% -> 17%
where the time goes in v2:
time: 116 us; the launch traced here: 115 us
  blocking collectives  36.2 us (31%)
  Pallas kernels  32.7 us (28%)
  starting transfers between devices  32.4 us (28%)
  waiting for transfers between devices  8.51 us (7%)
  local copies, waits for them, and re-layouts  3.46 us (3%)
    all_to_all x2, blocking collectives, from_all(): lax.all_to_all(block, BOTH, 0, 0, tiled=True, axis_index_groups=groups)  36.2 us
    pallas_call x2, Pallas kernels, lookup(): pl.pallas_call(functools.partial(first_lookup_kernel if fresh else lookup...  19.5 us
    all_to_all x1, starting transfers between devices, from_all(): lax.all_to_all(block, BOTH, 0, 0, tiled=True, axis_index_groups=groups)  16.5 us
    ppermute x4, starting transfers between devices, shift(): lax.ppermute(block, axis, pairs if up else [(b, a) for a, b in pairs])  8.77 us
    ppermute x3, starting transfers between devices, from_all(): return (own, lax.ppermute(own, 'gx', [(i, i ^ 1) for i in range(outer)]))  7.2 us
    all_to_all x1, waiting for transfers between devices, from_all(): lax.all_to_all(block, BOTH, 0, 0, tiled=True, axis_index_groups=groups)  5.52 us
    pallas_call x1, Pallas kernels, first_step(): pl.pallas_call(functools.partial(first_kernel, deep, rows, width, ends.sh...  4.8 us
    pallas_call x1, Pallas kernels, second_step(): pl.pallas_call(functools.partial(second_kernel, deep, rows, width), out_s...  4.56 us
  transfers between devices with their start and end apart: 8, of which 5 were waited for; matrix products, arithmetic and copies ran while one was open for 3% of the time, Pallas kernels for 17%

profile of v2, /device:TPU:1, one launch (start us, length us, event | category | flops | bytes accessed | tf_op | source)
XLA Modules:
  0.0 115.4 jit_solution(5916249099991555160)
XLA Ops:
  0.6 0.7 copy-done
  1.3 0.8 address.1
  2.1 16.5 %all-to-all-start = ((f32[128,4,128]{2,1,0:T(4,128)}), f32[128,4,128]{2,1,0:T(4,128)S(1)}, u32[]{:S(2)}, u32[]{:S(2)}) async-start(f32[128,4,128]{2,1,0:T(4,128)} %address.1), calls=%async_computation | async-start | bytes 524288 | tf_op jit(solution)/shard_map/all_to_all | solution.py:530
  18.6 0.8 slice_bitcast_fusion.3
  19.4 0.9 broadcast_xor_fusion
  20.3 0.8 slice_bitcast_fusion
  21.1 1.0 fusion.1
  22.1 2.5 %collective-permute-start.1 = (f32[7,64,128]{2,1,0:T(8,128)S(1)}, f32[7,64,128]{2,1,0:T(8,128)S(1)}, u32[]{:S(2)}, u32[]{:S(2)}) collective-permute-start(f32[7,64,128]{2,1,0:T(8,128)S(1)} %pad_maximum_fusion.2), channel_id=1, source_target_pairs={{0,1},{1,2},{2,3},{3,4},{4,5},{5,6},{6,7},{7,8},{8,9},{9,10},{10,1... | collective-permute-start | bytes 688136 | tf_op jit(solution)/shard_map/ppermute | solution.py:522
  24.7 0.0 copy-start.3
  24.7 1.4 %collective-permute-start.2 = (f32[7,64,128]{2,1,0:T(8,128)S(1)}, f32[7,64,128]{2,1,0:T(8,128)S(1)}, u32[]{:S(2)}, u32[]{:S(2)}) collective-permute-start(f32[7,64,128]{2,1,0:T(8,128)S(1)} %pad_maximum_fusion.3), channel_id=1, source_target_pairs={{1,0},{2,1},{3,2},{4,3},{5,4},{6,5},{7,6},{8,7},{9,8},{10,9},{11,1... | collective-permute-start | bytes 688136 | tf_op jit(solution)/shard_map/ppermute | solution.py:522
  26.3 0.1 maximum_bitcast_fusion.field_ref
  26.4 5.5 %all-to-all-done = f32[128,4,128]{2,1,0:T(4,128)S(1)} async-done(((f32[128,4,128]{2,1,0:T(4,128)}), f32[128,4,128]{2,1,0:T(4,128)S(1)}, u32[]{:S(2)}, u32[]{:S(2)}) %all-to-all-start) | async-done | bytes 262176 | tf_op jit(solution)/shard_map/all_to_all | solution.py:530
  31.9 2.8 %collective-permute-start = (f32[512,128]{1,0:T(8,128)S(1)}, f32[512,128]{1,0:T(8,128)S(1)}, u32[]{:S(2)}, u32[]{:S(2)}) collective-permute-start(f32[512,128]{1,0:T(8,128)S(1)} %bitcast.41), channel_id=1, source_target_pairs={{0,16},{16,0},{32,48},{48,32},{64,80},{80,64},{96,112},{112,96},{1... | collective-permute-start | bytes 786440 | tf_op jit(solution)/shard_map/ppermute | solution.py:532
  34.8 1.1 collective-permute-done.other_ref
  35.9 12.3 %lookup.2 = (f32[2,4,40,128]{3,2,1,0:T(8,128)S(1)}, bf16[512,512]{1,0:T(8,128)(2,1)S(1)}) custom-call(s32[40,512]{1,0:T(8,128)S(1)} %get-tuple-element.50.index_ref, s32[40,512]{1,0:T(8,128)S(1)} %get-tuple-element.51.toggle_ref, f32[512,128]{1,0:T(8,128)S(1)} %bitcast.42, f32[512,128]{1,0:T(8,128)S(1)} %collective-permute-done.other_ref), custom_call_target="tpu_custom_call" | custom-call | flops 10737418240 | tf_op jit(solution)/shard_map/lookup/pallas_call | solution.py:144
  48.2 0.0 collective-permute-done.1.left_ref
  48.2 0.0 collective-permute-done.2.right_ref
  48.2 2.0 %edge_lookup.1.edge_ref = f32[7,64,128]{2,1,0:T(8,128)S(1)} custom-call(f32[7,64,128]{2,1,0:T(8,128)S(1)} %collective-permute-done.1.left_ref, f32[7,64,128]{2,1,0:T(8,128)S(1)} %collective-permute-done.2.right_ref, bf16[512,512]{1,0:T(8,128)(2,1)S(1)} %get-tuple-element.18.pieces_ref), custom_call_target="tpu_custom_call" | custom-call | flops 1342177280 | tf_op jit(solution)/shard_map/edge_lookup/pallas_call | solution.py:190
  50.3 2.8 %collective-permute-start.3 = (f32[35,20,128]{2,1,0:T(8,128)S(1)}, f32[35,20,128]{2,1,0:T(8,128)S(1)}, u32[]{:S(2)}, u32[]{:S(2)}) collective-permute-start(f32[35,20,128]{2,1,0:T(8,128)S(1)} %pad_maximum_fusion), channel_id=1, source_target_pairs={{0,16},{16,32},{32,48},{48,64},{64,80},{80,96},{96,112},{112,128},... | collective-permute-start | bytes 1075208 | tf_op jit(solution)/shard_map/ppermute | solution.py:522
  53.1 2.1 %collective-permute-start.4 = (f32[35,20,128]{2,1,0:T(8,128)S(1)}, f32[35,20,128]{2,1,0:T(8,128)S(1)}, u32[]{:S(2)}, u32[]{:S(2)}) collective-permute-start(f32[35,20,128]{2,1,0:T(8,128)S(1)} %pad_maximum_fusion.1), channel_id=1, source_target_pairs={{16,0},{32,16},{48,32},{64,48},{80,64},{96,80},{112,96},{128,112},... | collective-permute-start | bytes 1075208 | tf_op jit(solution)/shard_map/ppermute | solution.py:522
  55.2 7.2 %lookup.3.middle_ref = f32[2,4,24,128]{3,2,1,0:T(8,128)S(1)} custom-call(s32[24,512]{1,0:T(8,128)S(1)} %slice.96.index_ref, s32[24,512]{1,0:T(8,128)S(1)} %slice.87.toggle_ref, bf16[512,512]{1,0:T(8,128)(2,1)S(1)} %get-tuple-element.18.pieces_ref), custom_call_target="tpu_custom_call" | custom-call | flops 6442450944 | tf_op jit(solution)/shard_map/lookup/pallas_call | solution.py:144
  62.4 0.0 collective-permute-done.3.above_ref
  62.4 0.1 collective-permute-done.4.below_ref
  62.6 4.8 %first_step.1 = (f32[3,2,13,8,640]{4,3,2,1,0:T(8,128)S(1)}, f32[2,13,8,640]{3,2,1,0:T(8,128)S(1)}, f32[2,13,8,640]{3,2,1,0:T(8,128)S(1)}, f32[13,8,640]{2,1,0:T(8,128)S(1)}, f32[128,128]{1,0:T(8,128)S(1)}) custom-call(f32[5,4,64,128]{3,2,1,0:T(8,128)S(1)} %maximum_bitcast_fusion.field_ref, f32[7,64,128]{2,1,0:T(8,128)S(1)} %edge_lookup.1.edge_ref, ...), custom_call_target="tpu_custom_call" | custom-call | tf_op jit(solution)/shard_map/first_step/pallas_call | solution.py:420
  67.4 19.7 %all_to_all.27 = f32[128,1,128]{2,1,0:T(1,128)S(1)} all-to-all(f32[128,1,128]{2,1,0:T(1,128)S(1)} %bitcast.43), channel_id=1, replica_groups={{0,1,2,3,4,5,6,7,8,9,10,11,12,13,14,15,32,33,34,35,36,37,38,39,40,41,42..., dimensions={0} | all-to-all | bytes 131072 | tf_op jit(solution)/shard_map/all_to_all | solution.py:530
  87.1 2.9 %collective-permute-start.5 = (f32[128,128]{1,0:T(8,128)S(1)}, f32[128,128]{1,0:T(8,128)S(1)}, u32[]{:S(2)}, u32[]{:S(2)}) collective-permute-start(f32[128,128]{1,0:T(8,128)S(1)} %bitcast.37), channel_id=1, source_target_pairs={{0,16},{16,0},{32,48},{48,32},{64,80},{80,64},{96,112},{112,96},{1... | collective-permute-start | bytes 196616 | tf_op jit(solution)/shard_map/ppermute | solution.py:532
  90.0 0.9 collective-permute-done.5.other_ref
  90.9 4.6 %second_step.1 = (f32[2,64,512]{2,1,0:T(8,128)}, f32[3,2,13,8,640]{4,3,2,1,0:T(8,128)S(1)}, f32[2,13,8,512]{3,2,1,0:T(8,128)S(1)}, f32[128,128]{1,0:T(8,128)S(1)}) custom-call(f32[128,128]{1,0:T(8,128)S(1)} %bitcast.38, f32[128,128]{1,0:T(8,128)S(1)} %collective-permute-done.5.other_ref, f32[3,2,13,8,640]{4,3,2,1,0:T(8,128)S(1)} %get-tuple-element.20.basis_ref, ...), custom_call_target="tpu_custom_call" | custom-call | tf_op jit(solution)/shard_map/second_step/pallas_call | solution.py:470
  95.4 16.5 %all_to_all.28 = f32[128,1,128]{2,1,0:T(1,128)S(1)} all-to-all(f32[128,1,128]{2,1,0:T(1,128)S(1)} %bitcast.44), channel_id=1, replica_groups={{0,1,2,3,4,5,6,7,8,9,10,11,12,13,14,15,32,33,34,35,36,37,38,39,40,41,42..., dimensions={0} | all-to-all | bytes 131072 | tf_op jit(solution)/shard_map/all_to_all | solution.py:530
  111.9 1.5 %collective-permute-start.6 = (f32[128,128]{1,0:T(8,128)S(1)}, f32[128,128]{1,0:T(8,128)S(1)}, u32[]{:S(2)}, u32[]{:S(2)}) collective-permute-start(f32[128,128]{1,0:T(8,128)S(1)} %bitcast.39), channel_id=1, source_target_pairs={{0,16},{16,0},{32,48},{48,32},{64,80},{80,64},{96,112},{112,96},{1... | collective-permute-start | bytes 196616 | tf_op jit(solution)/shard_map/ppermute | solution.py:532
  113.4 0.9 collective-permute-done.6.other_ref
  114.3 1.1 last_step.1
  (26 shorter events, 0.4 us)
Async XLA Ops:
  0.6 0.7 copy-start
  1.3 24.8 %copy-start.4 = (s32[64,512]{1,0:T(8,128)S(1)}, s32[64,512]{1,0:T(8,128)}, u32[]{:S(2)}) copy-start(s32[64,512]{1,0:T(8,128)} %param.9) | copy-start | bytes 393220
  2.1 24.0 %copy-start.1 = (f32[2,64,512]{2,1,0:T(8,128)S(1)}, f32[2,64,512]{2,1,0:T(8,128)}, u32[]{:S(2)}) copy-start(f32[2,64,512]{2,1,0:T(8,128)} %param.10) | copy-start | bytes 786436
  2.1 24.0 %copy-start.2 = (f32[2,64,512]{2,1,0:T(8,128)S(1)}, f32[2,64,512]{2,1,0:T(8,128)}, u32[]{:S(2)}) copy-start(f32[2,64,512]{2,1,0:T(8,128)} %param.11) | copy-start | bytes 786436
  2.1 29.8 %all-to-all-start = ((f32[128,4,128]{2,1,0:T(4,128)}), f32[128,4,128]{2,1,0:T(4,128)S(1)}, u32[]{:S(2)}, u32[]{:S(2)}) async-start(f32[128,4,128]{2,1,0:T(4,128)} %address.1), calls=%async_computation | async-start | bytes 524288 | tf_op jit(solution)/shard_map/all_to_all | solution.py:530
  22.1 26.1 %collective-permute-start.1 = (f32[7,64,128]{2,1,0:T(8,128)S(1)}, f32[7,64,128]{2,1,0:T(8,128)S(1)}, u32[]{:S(2)}, u32[]{:S(2)}) collective-permute-start(f32[7,64,128]{2,1,0:T(8,128)S(1)} %pad_maximum_fusion.2), channel_id=1, source_target_pairs={{0,1},{1,2},{2,3},{3,4},{4,5},{5,6},{6,7},{7,8},{8,9},{9,10},{10,1... | collective-permute-start | bytes 688136 | tf_op jit(solution)/shard_map/ppermute | solution.py:522
  24.7 1.7 %copy-start.3 = (s32[64,512]{1,0:T(8,128)S(1)}, s32[64,512]{1,0:T(8,128)}, u32[]{:S(2)}) copy-start(s32[64,512]{1,0:T(8,128)} %param.8) | copy-start | bytes 393220
  24.7 23.5 %collective-permute-start.2 = (f32[7,64,128]{2,1,0:T(8,128)S(1)}, f32[7,64,128]{2,1,0:T(8,128)S(1)}, u32[]{:S(2)}, u32[]{:S(2)}) collective-permute-start(f32[7,64,128]{2,1,0:T(8,128)S(1)} %pad_maximum_fusion.3), channel_id=1, source_target_pairs={{1,0},{2,1},{3,2},{4,3},{5,4},{6,5},{7,6},{8,7},{9,8},{10,9},{11,1... | collective-permute-start | bytes 688136 | tf_op jit(solution)/shard_map/ppermute | solution.py:522
  31.9 4.0 %collective-permute-start = (f32[512,128]{1,0:T(8,128)S(1)}, f32[512,128]{1,0:T(8,128)S(1)}, u32[]{:S(2)}, u32[]{:S(2)}) collective-permute-start(f32[512,128]{1,0:T(8,128)S(1)} %bitcast.41), channel_id=1, source_target_pairs={{0,16},{16,0},{32,48},{48,32},{64,80},{80,64},{96,112},{112,96},{1... | collective-permute-start | bytes 786440 | tf_op jit(solution)/shard_map/ppermute | solution.py:532
  50.3 12.2 %collective-permute-start.3 = (f32[35,20,128]{2,1,0:T(8,128)S(1)}, f32[35,20,128]{2,1,0:T(8,128)S(1)}, u32[]{:S(2)}, u32[]{:S(2)}) collective-permute-start(f32[35,20,128]{2,1,0:T(8,128)S(1)} %pad_maximum_fusion), channel_id=1, source_target_pairs={{0,16},{16,32},{32,48},{48,64},{64,80},{80,96},{96,112},{112,128},... | collective-permute-start | bytes 1075208 | tf_op jit(solution)/shard_map/ppermute | solution.py:522
  53.1 9.5 %collective-permute-start.4 = (f32[35,20,128]{2,1,0:T(8,128)S(1)}, f32[35,20,128]{2,1,0:T(8,128)S(1)}, u32[]{:S(2)}, u32[]{:S(2)}) collective-permute-start(f32[35,20,128]{2,1,0:T(8,128)S(1)} %pad_maximum_fusion.1), channel_id=1, source_target_pairs={{16,0},{32,16},{48,32},{64,48},{80,64},{96,80},{112,96},{128,112},... | collective-permute-start | bytes 1075208 | tf_op jit(solution)/shard_map/ppermute | solution.py:522
  87.1 3.8 %collective-permute-start.5 = (f32[128,128]{1,0:T(8,128)S(1)}, f32[128,128]{1,0:T(8,128)S(1)}, u32[]{:S(2)}, u32[]{:S(2)}) collective-permute-start(f32[128,128]{1,0:T(8,128)S(1)} %bitcast.37), channel_id=1, source_target_pairs={{0,16},{16,0},{32,48},{48,32},{64,80},{80,64},{96,112},{112,96},{1... | collective-permute-start | bytes 196616 | tf_op jit(solution)/shard_map/ppermute | solution.py:532
  111.9 2.4 %collective-permute-start.6 = (f32[128,128]{1,0:T(8,128)S(1)}, f32[128,128]{1,0:T(8,128)S(1)}, u32[]{:S(2)}, u32[]{:S(2)}) collective-permute-start(f32[128,128]{1,0:T(8,128)S(1)} %bitcast.39), channel_id=1, source_target_pairs={{0,16},{16,0},{32,48},{48,32},{64,80},{80,64},{96,112},{112,96},{1... | collective-permute-start | bytes 196616 | tf_op jit(solution)/shard_map/ppermute | solution.py:532

commit v3 on v1

--- a/solution.py
+++ b/solution.py
@@ -61,9 +61,52 @@
     )(table)
 
 
+def arrange_kernel(
+    flip, outer,
+    cap_ref, drop_ref, tap_ref, index_ref, toggle_ref,
+    left_ref, right_ref, field_ref, ends_ref, middle_ref,
+):
+    rows, cols = tap_ref.shape
+    blocks = cols // LANES
+    turn = (lax.axis_index("gx") & 1) * flip
+    index = index_ref[...] ^ turn
+    toggle = toggle_ref[...]
+    for n, cells in enumerate((index, toggle)):
+        ends_ref[n, pl.ds(0, outer), :] = cells[:outer]
+        ends_ref[n, pl.ds(outer, outer), :] = cells[rows - outer :]
+        middle_ref[n] = cells[outer : rows - outer]
+    tap = tap_ref[...].astype(jnp.float32)
+    fields = [cap_ref[0], cap_ref[1], drop_ref[0], drop_ref[1], tap]
+    for f, field in enumerate(fields):
+        for b in range(blocks):
+            field_ref[f, b] = field[:, b * LANES : (b + 1) * LANES]
+    fields += [index.astype(jnp.float32), toggle.astype(jnp.float32)]
+    for f, field in enumerate(fields):
+        left_ref[f] = field[:, cols - LANES :]
+        right_ref[f] = field[:, :LANES]
+
+
+def arrange(cap, drop, tap, index, toggle, flip, outer):
+    rows, cols = tap.shape
+    edge = jax.ShapeDtypeStruct((7, rows, LANES), jnp.float32)
+    return pl.pallas_call(
+        functools.partial(arrange_kernel, flip, outer),
+        out_shape=[
+            edge,
+            edge,
+            jax.ShapeDtypeStruct((5, cols // LANES, rows, LANES), jnp.float32),
+            jax.ShapeDtypeStruct((2, 2 * outer, cols), jnp.int32),
+            jax.ShapeDtypeStruct((2, rows - 2 * outer, cols), jnp.int32),
+        ],
+        in_specs=[vmem()] * 5,
+        out_specs=[vmem()] * 5,
+        compiler_params=params(12),
+        name="arrange",
+    )(cap, drop, tap, index, toggle)
+
+
 MANY = 8
 CHUNK = 256
-UNROLL = 8
 
 
 def split_kernel(table_refs, pieces_ref):
@@ -109,24 +152,25 @@
     return means
 
 
-def lookup_rows(many, index_ref, toggle_ref, pieces_ref, out_ref):
-    rows, cols = index_ref.shape
+def lookup_rows(many, cells_ref, pieces_ref, out_ref):
+    _, rows, cols = cells_ref.shape
+    unroll = rows if rows <= 24 else math.gcd(rows, 20)
 
     def body(i, carry):
-        for u in range(UNROLL):
-            row = pl.ds(i * UNROLL + u, 1)
-            means = charges(many, index_ref[row, :], toggle_ref[row, :], pieces_ref)
+        for u in range(unroll):
+            row = pl.ds(i * unroll + u, 1)
+            means = charges(many, cells_ref[0, row, :], cells_ref[1, row, :], pieces_ref)
             for k, mean in enumerate(means):
                 for b in range(cols // LANES):
                     out_ref[k, b, row, :] = mean[:, b * LANES : (b + 1) * LANES]
         return carry
 
-    lax.fori_loop(0, rows // UNROLL, body, 0)
-
-
-def first_lookup_kernel(many, index_ref, toggle_ref, own_ref, other_ref, out_ref, pieces_ref):
+    lax.fori_loop(0, rows // unroll, body, 0)
+
+
+def first_lookup_kernel(many, cells_ref, own_ref, other_ref, out_ref, pieces_ref):
     split_kernel((own_ref, other_ref), pieces_ref)
-    lookup_rows(many, index_ref, toggle_ref, pieces_ref, out_ref)
+    lookup_rows(many, cells_ref, pieces_ref, out_ref)
 
 
 def lookup_cost(cells, pieces):
@@ -134,8 +178,8 @@
     return pl.CostEstimate(flops=flops, bytes_accessed=0, transcendentals=0)
 
 
-def lookup(index, toggle, table, many):
-    rows, cols = index.shape
+def lookup(cells, table, many):
+    _, rows, cols = cells.shape
     charge = jax.ShapeDtypeStruct((STEPS, cols // LANES, rows, LANES), jnp.float32)
     fresh = len(table) == 2
     pieces = table[0]
@@ -144,12 +188,12 @@
     return pl.pallas_call(
         functools.partial(first_lookup_kernel if fresh else lookup_rows, many),
         out_shape=[charge, pieces] if fresh else charge,
-        in_specs=[vmem()] * (2 + len(table)),
+        in_specs=[vmem()] * (1 + len(table)),
         out_specs=[vmem()] * 2 if fresh else vmem(),
         compiler_params=params(20),
         cost_estimate=lookup_cost(rows * cols, pieces),
         name="lookup",
-    )(index, toggle, *table)
+    )(cells, *table)
 
 
 def edge_lookup_kernel(many, left_ref, right_ref, pieces_ref, out_ref, cells_ref, got_ref):
@@ -526,45 +570,41 @@
     return lax.all_to_all(block, BOTH, 0, 0, tiled=True)
 
 
-def gather_tables(tables):
+def by_parity(block):
     outer, inner = lax.axis_size("gx"), lax.axis_size("gy")
     groups = [
         [x * inner + y for x in range(parity, outer, 2) for y in range(inner)] for parity in range(2)
     ]
-    block = address(tables, outer * inner // 2)
     own = lax.all_to_all(block, BOTH, 0, 0, tiled=True, axis_index_groups=groups)
     own = own.reshape(-1, LANES)
     return own, lax.ppermute(own, "gx", [(i, i ^ 1) for i in range(outer)])
 
 
 def shards(tables, table_index, toggle, tap_code, capacitance, prior_drop):
-    rows, cols = table_index.shape
-    count = lax.axis_size("gx") * lax.axis_size("gy")
+    rows = table_index.shape[0]
     inner = lax.axis_size("gy")
+    count = lax.axis_size("gx") * inner
     many = tables.shape[0], inner
     outer = HALO
-    table = gather_tables(tables)
-    table_index = table_index ^ ((lax.axis_index("gx") & 1) * (inner * tables.shape[0]))
-    codes = [a.astype(jnp.float32)[None] for a in (tap_code, table_index, toggle)]
-    field = jnp.concatenate([capacitance, prior_drop, *codes])
-    field = field.reshape(-1, rows, cols // LANES, LANES).transpose(0, 2, 1, 3)
-    left = shift(field[:, -1], "gy", True)
-    right = shift(field[:, 0], "gy", False)
-    def ends_of(array):
-        return jnp.concatenate([array[:outer], array[-outer:]])
-
-    ends, pieces = lookup(ends_of(table_index), ends_of(toggle), table, many)
+    table = by_parity(address(tables, count // 2))
+    flip = inner * tables.shape[0]
+    left, right, field, outside, inside = arrange(
+        capacitance, prior_drop, tap_code, table_index, toggle, flip, outer
+    )
+    left = shift(left, "gy", True)
+    right = shift(right, "gy", False)
+    ends, pieces = lookup(outside, table, many)
     edge = edge_lookup(left, right, pieces, many)
 
     def late(far):
         cut = slice(-HALO, None) if far else slice(0, HALO)
-        charge, lower = [a[:, :, cut].reshape(-1, HALO, LANES) for a in (ends, field[:5])]
+        charge, lower = [a[:, :, cut].reshape(-1, HALO, LANES) for a in (ends, field)]
         return jnp.concatenate([lower, charge, edge[:, cut]])
 
     above = shift(late(True), "gx", True)
     below = shift(late(False), "gx", False)
     pieces, edge = lax.optimization_barrier((pieces, edge))
-    middle = lookup(table_index[outer:-outer], toggle[outer:-outer], (pieces,), many)
+    middle = lookup(inside, (pieces,), many)
     basis, drop, cap, later, part = first_step(field, edge, above, below, ends, middle, count)
     first, basis, held, part = second_step(exchange(part), basis, drop, cap, later, rows)
     return first, last_step(exchange(part), basis, held, rows)

time: 114 us -> 119 us (1.044)
  blocking collectives: 40.7 us -> 70.1 us
  starting transfers between devices: 29.3 us -> 11 us
  waiting for transfers between devices: 6.88 us -> 0.59 us
  local copies, waits for them, and re-layouts: 1.11 us -> 5.37 us
  other arithmetic: 1.93 us -> 0.06 us
  Pallas kernels: 32.8 us -> 31.1 us
    all_to_all x0 -> x1, blocking collectives: none -> 29.4 us  [by_parity(): lax.all_to_all(block, BOTH, 0, 0, tiled=True, axis_index_groups=groups)]
    all_to_all x1 -> x0, starting transfers between devices: 16.3 us -> none  [gather_tables(): lax.all_to_all(block, BOTH, 0, 0, tiled=True, axis_index_groups=groups)]
    all_to_all x1 -> x0, waiting for transfers between devices: 5.71 us -> none  [gather_tables(): lax.all_to_all(block, BOTH, 0, 0, tiled=True, axis_index_groups=groups)]
    unnamed x14 -> x12, local copies, waits for them, and re-layouts: 0.82 us -> 5.3 us
    ppermute x4, starting transfers between devices: 10.1 us -> 8.16 us  [shift(): lax.ppermute(block, axis, pairs if up else [(b, a) for a, b in pairs])]
    convert_element_type x3 -> x0, other arithmetic: 1.86 us -> none  [shards(): a.astype(jnp.float32)[None]]
  transfers between devices with their start and end apart: 6 -> 5, of which waited for: 3 -> 1; matrix products, arithmetic and copies ran while one was open for 2% -> 0% of each run, Pallas kernels for 17% -> 16%
where the time goes in v3:
time: 119 us
  blocking collectives  70.1 us (59%)
  Pallas kernels  31.1 us (26%)
  starting transfers between devices  11 us (9%)
  local copies, waits for them, and re-layouts  5.37 us (5%)
    all_to_all x2, blocking collectives, exchange(): return lax.all_to_all(block, BOTH, 0, 0, tiled=True)  40.7 us
    all_to_all x1, blocking collectives, by_parity(): lax.all_to_all(block, BOTH, 0, 0, tiled=True, axis_index_groups=groups)  29.4 us
    pallas_call x2, Pallas kernels, lookup(): pl.pallas_call(functools.partial(first_lookup_kernel if fresh else lookup...  18.4 us
    ppermute x4, starting transfers between devices, shift(): lax.ppermute(block, axis, pairs if up else [(b, a) for a, b in pairs])  8.16 us
    unnamed x12, local copies, waits for them, and re-layouts  5.3 us
    pallas_call x1, Pallas kernels, first_step(): pl.pallas_call(functools.partial(first_kernel, deep, rows, width, ends.sh...  4.82 us
    pallas_call x1, Pallas kernels, second_step(): pl.pallas_call(functools.partial(second_kernel, deep, rows, width), out_s...  4.56 us
    ppermute x1, starting transfers between devices, by_parity(): return (own, lax.ppermute(own, 'gx', [(i, i ^ 1) for i in range(outer)]))  2.85 us
  transfers between devices with their start and end apart: 5, of which 1 were waited for; matrix products, arithmetic and copies ran while one was open for 0% of the time, Pallas kernels for 16%

profile of v3, /device:TPU:1, one launch (start us, length us, event | category | flops | bytes accessed | tf_op | source)
XLA Modules:
  0.0 119.0 jit_solution(16650949483966049351)
XLA Ops:
  0.6 0.0 copy-start.5
  0.6 0.7 copy-done.5
  1.3 0.1 address.1
  1.4 29.4 %all_to_all.27 = f32[128,4,128]{2,1,0:T(4,128)S(1)} all-to-all(f32[128,4,128]{2,1,0:T(4,128)S(1)} %address.1), channel_id=1, replica_groups={{0,1,2,3,4,5,6,7,8,9,10,11,12,13,14,15,32,33,34,35,36,37,38,39,40,41,42..., dimensions={0} | all-to-all | bytes 524288 | tf_op jit(solution)/shard_map/all_to_all | solution.py:578
  30.8 2.9 %collective-permute-start = (f32[512,128]{1,0:T(8,128)S(1)}, f32[512,128]{1,0:T(8,128)S(1)}, u32[]{:S(2)}, u32[]{:S(2)}) collective-permute-start(f32[512,128]{1,0:T(8,128)S(1)} %bitcast.15), channel_id=1, source_target_pairs={{0,16},{16,0},{32,48},{48,32},{64,80},{80,64},{96,112},{112,96},{1... | collective-permute-start | bytes 786440 | tf_op jit(solution)/shard_map/ppermute | solution.py:580
  33.7 0.0 copy-start
  33.7 0.9 copy-done
  34.6 0.0 copy-start.1
  34.6 0.9 copy-done.1
  35.6 0.0 copy-start.2
  35.6 0.9 copy-done.2
  36.5 0.0 copy-start.3
  36.5 0.9 copy-done.3
  37.4 0.9 copy-done.4
  38.3 0.1 arrange.1
  38.4 2.2 %collective-permute-start.1 = (f32[7,64,128]{2,1,0:T(8,128)S(1)}, f32[7,64,128]{2,1,0:T(8,128)S(1)}, u32[]{:S(2)}, u32[]{:S(2)}) collective-permute-start(f32[7,64,128]{2,1,0:T(8,128)S(1)} %get-tuple-element.23), channel_id=1, source_target_pairs={{0,1},{1,2},{2,3},{3,4},{4,5},{5,6},{6,7},{7,8},{8,9},{9,10},{10,1... | collective-permute-start | bytes 688136 | tf_op jit(solution)/shard_map/ppermute | solution.py:566
  40.6 1.3 %collective-permute-start.2 = (f32[7,64,128]{2,1,0:T(8,128)S(1)}, f32[7,64,128]{2,1,0:T(8,128)S(1)}, u32[]{:S(2)}, u32[]{:S(2)}) collective-permute-start(f32[7,64,128]{2,1,0:T(8,128)S(1)} %get-tuple-element.24), channel_id=1, source_target_pairs={{1,0},{2,1},{3,2},{4,3},{5,4},{6,5},{7,6},{8,7},{9,8},{10,9},{11,1... | collective-permute-start | bytes 688136 | tf_op jit(solution)/shard_map/ppermute | solution.py:566
  41.9 0.0 collective-permute-done.other_ref
  42.0 11.6 %lookup.2 = (f32[2,4,40,128]{3,2,1,0:T(8,128)S(1)}, bf16[512,512]{1,0:T(8,128)(2,1)S(1)}) custom-call(s32[2,40,512]{2,1,0:T(8,128)S(1)} %get-tuple-element.21.cells_ref, f32[512,128]{1,0:T(8,128)S(1)} %bitcast.16, f32[512,128]{1,0:T(8,128)S(1)} %collective-permute-done.other_ref), custom_call_target="tpu_custom_call" | custom-call | flops 10737418240 | tf_op jit(solution)/shard_map/lookup/pallas_call | solution.py:188
  53.6 0.0 collective-permute-done.1.left_ref
  53.6 0.0 collective-permute-done.2.right_ref
  53.6 2.0 %edge_lookup.1.edge_ref = f32[7,64,128]{2,1,0:T(8,128)S(1)} custom-call(f32[7,64,128]{2,1,0:T(8,128)S(1)} %collective-permute-done.1.left_ref, f32[7,64,128]{2,1,0:T(8,128)S(1)} %collective-permute-done.2.right_ref, bf16[512,512]{1,0:T(8,128)(2,1)S(1)} %get-tuple-element.28.pieces_ref), custom_call_target="tpu_custom_call" | custom-call | flops 1342177280 | tf_op jit(solution)/shard_map/edge_lookup/pallas_call | solution.py:234
  55.7 2.6 %collective-permute-start.3 = (f32[35,20,128]{2,1,0:T(8,128)S(1)}, f32[35,20,128]{2,1,0:T(8,128)S(1)}, u32[]{:S(2)}, u32[]{:S(2)}) collective-permute-start(f32[35,20,128]{2,1,0:T(8,128)S(1)} %pad_maximum_fusion), channel_id=1, source_target_pairs={{0,16},{16,32},{32,48},{48,64},{64,80},{80,96},{96,112},{112,128},... | collective-permute-start | bytes 1075208 | tf_op jit(solution)/shard_map/ppermute | solution.py:566
  58.3 2.1 %collective-permute-start.4 = (f32[35,20,128]{2,1,0:T(8,128)S(1)}, f32[35,20,128]{2,1,0:T(8,128)S(1)}, u32[]{:S(2)}, u32[]{:S(2)}) collective-permute-start(f32[35,20,128]{2,1,0:T(8,128)S(1)} %pad_maximum_fusion.1), channel_id=1, source_target_pairs={{16,0},{32,16},{48,32},{64,48},{80,64},{96,80},{112,96},{128,112},... | collective-permute-start | bytes 1075208 | tf_op jit(solution)/shard_map/ppermute | solution.py:566
  60.4 6.8 %lookup.3.middle_ref = f32[2,4,24,128]{3,2,1,0:T(8,128)S(1)} custom-call(s32[2,24,512]{2,1,0:T(8,128)S(1)} %get-tuple-element.27.cells_ref, bf16[512,512]{1,0:T(8,128)(2,1)S(1)} %get-tuple-element.28.pieces_ref), custom_call_target="tpu_custom_call" | custom-call | flops 6442450944 | tf_op jit(solution)/shard_map/lookup/pallas_call | solution.py:188
  67.2 0.0 collective-permute-done.3.above_ref
  67.2 0.6 collective-permute-done.4.below_ref
  67.8 4.8 %first_step.1 = (f32[3,2,13,8,640]{4,3,2,1,0:T(8,128)S(1)}, f32[2,13,8,640]{3,2,1,0:T(8,128)S(1)}, f32[2,13,8,640]{3,2,1,0:T(8,128)S(1)}, f32[13,8,640]{2,1,0:T(8,128)S(1)}, f32[256,128]{1,0:T(8,128)S(1)}) custom-call(f32[5,4,64,128]{3,2,1,0:T(8,128)S(1)} %get-tuple-element.20.field_ref, f32[7,64,128]{2,1,0:T(8,128)S(1)} %edge_lookup.1.edge_ref, ...), custom_call_target="tpu_custom_call" | custom-call | tf_op jit(solution)/shard_map/first_step/pallas_call | solution.py:464
  72.6 22.3 %all_to_all.28 = f32[256,1,128]{2,1,0:T(1,128)S(1)} all-to-all(f32[256,1,128]{2,1,0:T(1,128)S(1)} %bitcast.17), channel_id=1, replica_groups=mesh['gx'=16,'gy'=16] {'gx','gy'}, dimensions={0} | all-to-all | bytes 262144 | tf_op jit(solution)/shard_map/all_to_all | solution.py:570
  95.0 4.6 %second_step.1 = (f32[2,64,512]{2,1,0:T(8,128)}, f32[3,2,13,8,640]{4,3,2,1,0:T(8,128)S(1)}, f32[2,13,8,512]{3,2,1,0:T(8,128)S(1)}, f32[256,128]{1,0:T(8,128)S(1)}) custom-call(f32[256,128]{1,0:T(8,128)S(1)} %bitcast.13, f32[3,2,13,8,640]{4,3,2,1,0:T(8,128)S(1)} %get-tuple-element.30.basis_ref, f32[2,13,8,640]{3,2,1,0:T(8,128)S(1)} %get-tuple-element.31.drop_ref, ...), custom_call_target="tpu_custom_call" | custom-call | tf_op jit(solution)/shard_map/second_step/pallas_call | solution.py:514
  99.5 18.4 %all_to_all.29 = f32[256,1,128]{2,1,0:T(1,128)S(1)} all-to-all(f32[256,1,128]{2,1,0:T(1,128)S(1)} %bitcast.18), channel_id=1, replica_groups=mesh['gx'=16,'gy'=16] {'gx','gy'}, dimensions={0} | all-to-all | bytes 262144 | tf_op jit(solution)/shard_map/all_to_all | solution.py:570
  118.0 1.1 last_step.1
  (6 shorter events, 0.1 us)
Async XLA Ops:
  0.6 0.7 copy-start.5
  30.8 11.1 %collective-permute-start = (f32[512,128]{1,0:T(8,128)S(1)}, f32[512,128]{1,0:T(8,128)S(1)}, u32[]{:S(2)}, u32[]{:S(2)}) collective-permute-start(f32[512,128]{1,0:T(8,128)S(1)} %bitcast.15), channel_id=1, source_target_pairs={{0,16},{16,0},{32,48},{48,32},{64,80},{80,64},{96,112},{112,96},{1... | collective-permute-start | bytes 786440 | tf_op jit(solution)/shard_map/ppermute | solution.py:580
  33.7 0.9 copy-start
  34.6 0.9 copy-start.1
  35.6 0.9 copy-start.2
  36.5 0.9 copy-start.3
  37.4 0.9 copy-start.4
  38.4 15.2 %collective-permute-start.1 = (f32[7,64,128]{2,1,0:T(8,128)S(1)}, f32[7,64,128]{2,1,0:T(8,128)S(1)}, u32[]{:S(2)}, u32[]{:S(2)}) collective-permute-start(f32[7,64,128]{2,1,0:T(8,128)S(1)} %get-tuple-element.23), channel_id=1, source_target_pairs={{0,1},{1,2},{2,3},{3,4},{4,5},{5,6},{6,7},{7,8},{8,9},{9,10},{10,1... | collective-permute-start | bytes 688136 | tf_op jit(solution)/shard_map/ppermute | solution.py:566
  40.6 13.0 %collective-permute-start.2 = (f32[7,64,128]{2,1,0:T(8,128)S(1)}, f32[7,64,128]{2,1,0:T(8,128)S(1)}, u32[]{:S(2)}, u32[]{:S(2)}) collective-permute-start(f32[7,64,128]{2,1,0:T(8,128)S(1)} %get-tuple-element.24), channel_id=1, source_target_pairs={{1,0},{2,1},{3,2},{4,3},{5,4},{6,5},{7,6},{8,7},{9,8},{10,9},{11,1... | collective-permute-start | bytes 688136 | tf_op jit(solution)/shard_map/ppermute | solution.py:566
  55.7 11.5 %collective-permute-start.3 = (f32[35,20,128]{2,1,0:T(8,128)S(1)}, f32[35,20,128]{2,1,0:T(8,128)S(1)}, u32[]{:S(2)}, u32[]{:S(2)}) collective-permute-start(f32[35,20,128]{2,1,0:T(8,128)S(1)} %pad_maximum_fusion), channel_id=1, source_target_pairs={{0,16},{16,32},{32,48},{48,64},{64,80},{80,96},{96,112},{112,128},... | collective-permute-start | bytes 1075208 | tf_op jit(solution)/shard_map/ppermute | solution.py:566
  58.3 9.5 %collective-permute-start.4 = (f32[35,20,128]{2,1,0:T(8,128)S(1)}, f32[35,20,128]{2,1,0:T(8,128)S(1)}, u32[]{:S(2)}, u32[]{:S(2)}) collective-permute-start(f32[35,20,128]{2,1,0:T(8,128)S(1)} %pad_maximum_fusion.1), channel_id=1, source_target_pairs={{16,0},{32,16},{48,32},{64,48},{80,64},{96,80},{112,96},{128,112},... | collective-permute-start | bytes 1075208 | tf_op jit(solution)/shard_map/ppermute | solution.py:566

commit v4 on v1

--- a/solution.py
+++ b/solution.py
@@ -42,28 +42,46 @@
     return pl.BlockSpec(memory_space=pltpu.VMEM)
 
 
-def address_kernel(table_ref, out_ref):
+def address_kernel(
+    table_in, tap_in, index_in, toggle_in, out_ref, codes_ref, table_ref, cells_ref, arrived
+):
+    copies = [pltpu.make_async_copy(table_in, table_ref, arrived.at[3])]
+    for n, source in enumerate((tap_in, index_in, toggle_in)):
+        copies.append(pltpu.make_async_copy(source, cells_ref.at[n], arrived.at[n]))
+    for copy in copies:
+        copy.start()
+    copies[0].wait()
     table = table_ref[...]
     many = table.shape[0] // LO
     block = jnp.concatenate([table[a * many : (a + 1) * many] for a in range(LO)], axis=1)
     out_ref[...] = jnp.broadcast_to(block[None], out_ref.shape)
-
-
-def address(table, count):
+    for n in range(3):
+        copies[1 + n].wait()
+        codes_ref[n] = cells_ref[n].astype(jnp.float32)
+
+
+def address(table, tap, index, toggle, count):
     many = table.shape[0] // LO
     return pl.pallas_call(
         address_kernel,
-        out_shape=jax.ShapeDtypeStruct((count, many, LANES), jnp.float32),
-        in_specs=[vmem()],
-        out_specs=vmem(),
-        compiler_params=params(8),
+        out_shape=[
+            jax.ShapeDtypeStruct((count, many, LANES), jnp.float32),
+            jax.ShapeDtypeStruct((3, *tap.shape), jnp.float32),
+        ],
+        in_specs=[pl.BlockSpec(memory_space=pl.ANY)] * 4,
+        out_specs=[vmem()] * 2,
+        scratch_shapes=[
+            pltpu.VMEM(table.shape, jnp.float32),
+            pltpu.VMEM((3, *tap.shape), jnp.int32),
+            pltpu.SemaphoreType.DMA((4,)),
+        ],
+        compiler_params=params(62),
         name="address",
-    )(table)
+    )(table, tap, index, toggle)
 
 
 MANY = 8
 CHUNK = 256
-UNROLL = 8
 
 
 def split_kernel(table_refs, pieces_ref):
@@ -82,7 +100,7 @@
     quarter = many // LO
     held = index & (many - 1)
     device = index // many
-    half = (device // inner) & 1
+    half = (device // inner + lax.axis_index("gx")) & 1
     place = device // (2 * inner) * inner + (device & (inner - 1))
     row = place * quarter + (held & (quarter - 1))
     which = held // quarter + LO * half
@@ -111,17 +129,18 @@
 
 def lookup_rows(many, index_ref, toggle_ref, pieces_ref, out_ref):
     rows, cols = index_ref.shape
+    unroll = rows if rows <= 24 else math.gcd(rows, 20)
 
     def body(i, carry):
-        for u in range(UNROLL):
-            row = pl.ds(i * UNROLL + u, 1)
+        for u in range(unroll):
+            row = pl.ds(i * unroll + u, 1)
             means = charges(many, index_ref[row, :], toggle_ref[row, :], pieces_ref)
             for k, mean in enumerate(means):
                 for b in range(cols // LANES):
                     out_ref[k, b, row, :] = mean[:, b * LANES : (b + 1) * LANES]
         return carry
 
-    lax.fori_loop(0, rows // UNROLL, body, 0)
+    lax.fori_loop(0, rows // unroll, body, 0)
 
 
 def first_lookup_kernel(many, index_ref, toggle_ref, own_ref, other_ref, out_ref, pieces_ref):
@@ -298,29 +317,17 @@
     sums_ref[...] = jnp.zeros_like(sums_ref)
     for k, total in enumerate(totals):
         sums_ref[pl.ds(k, 1), :] = jnp.sum(total, axis=0, keepdims=True)
-    row = lax.dot_general(
-        jnp.ones((GROUP, LANES), jnp.float32),
-        sums_ref[...],
-        (((1,), (1,)), ((), ())),
-        precision=lax.Precision.HIGHEST,
-        preferred_element_type=jnp.float32,
-    )
-    out_ref[...] = jnp.broadcast_to(row[:1], out_ref.shape)
-
-
-def weights_of(gathered_ref, spread_ref):
+    across = jnp.sum(sums_ref[...], axis=1, keepdims=True)
+    row = lax.broadcasted_iota(jnp.int32, sums_ref.shape, 0)
+    lane = lax.broadcasted_iota(jnp.int32, sums_ref.shape, 1)
+    row = jnp.sum(jnp.where(row == lane, across, 0.0), axis=0, keepdims=True)
+    out_ref[...] = jnp.broadcast_to(row, out_ref.shape)
+
+
+def weights_of(gathered_ref):
     total = jnp.sum(gathered_ref[...], axis=0, keepdims=True)
-    row = lax.broadcasted_iota(jnp.int32, (LANES, LANES), 0)
-    lane = lax.broadcasted_iota(jnp.int32, (LANES, LANES), 1)
-    spread_ref[...] = lax.dot_general(
-        jnp.where(row == lane, jnp.broadcast_to(total, (LANES, LANES)), 0.0),
-        jnp.ones((LANES, LANES), jnp.float32),
-        (((1,), (0,)), ((), ())),
-        precision=lax.Precision.HIGHEST,
-        preferred_element_type=jnp.float32,
-    )
     b1, b2, b3, h11, h21, h31, h22, h32, h33 = [
-        jnp.broadcast_to(spread_ref[pl.ds(k, 1), :], (GROUP, LANES)) for k in range(9)
+        jnp.broadcast_to(total[:, k : k + 1], (GROUP, LANES)) for k in range(9)
     ]
     l21 = h21 / h11
     l31 = h31 / h11
@@ -431,7 +438,7 @@
             pltpu.VMEM(full, jnp.float32),
             pltpu.VMEM((3, 2, deep, GROUP, width), jnp.float32),
             pltpu.VMEM((STEPS, 3, *full[1:]), jnp.float32),
-            pltpu.VMEM((LANES, LANES), jnp.float32),
+            pltpu.VMEM((2 * GROUP, LANES), jnp.float32),
         ],
         compiler_params=params(20),
         name="first_step",
@@ -446,7 +453,7 @@
 ):
     wide = width + LANES
     weigh(cap_ref, deep, grid_ref, cross_ref)
-    weights = [widen(c, wide) for c in weights_of(gathered_ref, sums_ref)]
+    weights = [widen(c, wide) for c in weights_of(gathered_ref)]
     for l in range(2):
         for i in range(deep):
             value = drop_ref[l, i]
@@ -481,15 +488,15 @@
             pltpu.VMEM(full, jnp.float32),
             pltpu.VMEM((3, 2, deep, GROUP, width), jnp.float32),
             pltpu.VMEM((2, width // LANES, deep * GROUP, LANES), jnp.float32),
-            pltpu.VMEM((LANES, LANES), jnp.float32),
+            pltpu.VMEM((2 * GROUP, LANES), jnp.float32),
         ],
         compiler_params=params(20),
         name="second_step",
     )(gathered, basis, drop, cap, later)
 
 
-def last_kernel(deep, rows, width, gathered_ref, basis_ref, held_ref, out_ref, natural_ref, sums_ref):
-    weights = [widen(c, width) for c in weights_of(gathered_ref, sums_ref)]
+def last_kernel(deep, rows, width, gathered_ref, basis_ref, held_ref, out_ref, natural_ref):
+    weights = [widen(c, width) for c in weights_of(gathered_ref)]
     for l in range(2):
         for i in range(deep):
             value = held_ref[l, i]
@@ -509,7 +516,6 @@
         out_specs=vmem(),
         scratch_shapes=[
             pltpu.VMEM((2, width // LANES, deep * GROUP, LANES), jnp.float32),
-            pltpu.VMEM((LANES, LANES), jnp.float32),
         ],
         compiler_params=params(12),
         name="last_step",
@@ -526,12 +532,11 @@
     return lax.all_to_all(block, BOTH, 0, 0, tiled=True)
 
 
-def gather_tables(tables):
+def gather_tables(block):
     outer, inner = lax.axis_size("gx"), lax.axis_size("gy")
     groups = [
         [x * inner + y for x in range(parity, outer, 2) for y in range(inner)] for parity in range(2)
     ]
-    block = address(tables, outer * inner // 2)
     own = lax.all_to_all(block, BOTH, 0, 0, tiled=True, axis_index_groups=groups)
     own = own.reshape(-1, LANES)
     return own, lax.ppermute(own, "gx", [(i, i ^ 1) for i in range(outer)])
@@ -543,10 +548,9 @@
     inner = lax.axis_size("gy")
     many = tables.shape[0], inner
     outer = HALO
-    table = gather_tables(tables)
-    table_index = table_index ^ ((lax.axis_index("gx") & 1) * (inner * tables.shape[0]))
-    codes = [a.astype(jnp.float32)[None] for a in (tap_code, table_index, toggle)]
-    field = jnp.concatenate([capacitance, prior_drop, *codes])
+    block, codes = address(tables, tap_code, table_index, toggle, count // 2)
+    table = gather_tables(block)
+    field = jnp.concatenate([capacitance, prior_drop, codes])
     field = field.reshape(-1, rows, cols // LANES, LANES).transpose(0, 2, 1, 3)
     left = shift(field[:, -1], "gy", True)
     right = shift(field[:, 0], "gy", False)

time: 114 us -> 112 us (0.982)
  waiting for transfers between devices: 6.88 us -> 8.23 us
  blocking collectives: 40.7 us -> 39.4 us
    convert_element_type x3 -> x0, other arithmetic: 1.86 us -> none  [shards(): a.astype(jnp.float32)[None]]
    all_to_all x2, blocking collectives: 40.7 us -> 39.4 us  [exchange(): return lax.all_to_all(block, BOTH, 0, 0, tiled=True)]
    transpose x0 -> x1, other arithmetic: none -> 1.29 us  [shards(): field = field.reshape(-1, rows, cols // LANES, LANES).transpose(0, 2, 1, 3)]
  transfers between devices with their start and end apart: 6 -> 6, of which waited for: 3 -> 3; matrix products, arithmetic and copies ran while one was open for 2% -> 1% of each run, Pallas kernels for 17% -> 16%
where the time goes in v4:
time: 112 us
  blocking collectives  39.4 us (35%)
  Pallas kernels  32.4 us (29%)
  starting transfers between devices  29.4 us (26%)
  waiting for transfers between devices  8.23 us (7%)
  other arithmetic  1.37 us (1%)
    all_to_all x2, blocking collectives, exchange(): return lax.all_to_all(block, BOTH, 0, 0, tiled=True)  39.4 us
    pallas_call x2, Pallas kernels, lookup(): pl.pallas_call(functools.partial(first_lookup_kernel if fresh else lookup...  18.4 us
    all_to_all x1, starting transfers between devices, gather_tables(): lax.all_to_all(block, BOTH, 0, 0, tiled=True, axis_index_groups=groups)  16.5 us
    ppermute x4, starting transfers between devices, shift(): lax.ppermute(block, axis, pairs if up else [(b, a) for a, b in pairs])  10.1 us
    all_to_all x1, waiting for transfers between devices, gather_tables(): lax.all_to_all(block, BOTH, 0, 0, tiled=True, axis_index_groups=groups)  6.58 us
    pallas_call x1, Pallas kernels, first_step(): pl.pallas_call(functools.partial(first_kernel, deep, rows, width, ends.sh...  4.67 us
    pallas_call x1, Pallas kernels, second_step(): pl.pallas_call(functools.partial(second_kernel, deep, rows, width), out_s...  4.49 us
    ppermute x1, starting transfers between devices, gather_tables(): return (own, lax.ppermute(own, 'gx', [(i, i ^ 1) for i in range(outer)]))  2.82 us
  transfers between devices with their start and end apart: 6, of which 3 were waited for; matrix products, arithmetic and copies ran while one was open for 1% of the time, Pallas kernels for 16%

profile of v4, /device:TPU:1, one launch (start us, length us, event | category | flops | bytes accessed | tf_op | source)
XLA Modules:
  0.0 111.8 jit_solution(11565282630973420773)
XLA Ops:
  0.6 1.9 %address.1 = (f32[128,4,128]{2,1,0:T(4,128)}, f32[3,64,512]{2,1,0:T(8,128)}) custom-call(f32[16,32]{1,0:T(8,128)} %table_in.1, s32[64,512]{1,0:T(8,128)} %tap_in.1, s32[64,512]{1,0:T(8,128)} %index_in.1, s32[64,512]{1,0:T(8,128)} %toggle_in.1), custom_call_target="tpu_custom_call" | custom-call | tf_op jit(solution)/shard_map/address/pallas_call | solution.py:65
  2.5 0.0 copy-start
  2.6 16.5 %all-to-all-start = ((f32[128,4,128]{2,1,0:T(4,128)}), f32[128,4,128]{2,1,0:T(4,128)S(1)}, u32[]{:S(2)}, u32[]{:S(2)}) async-start(f32[128,4,128]{2,1,0:T(4,128)} %get-tuple-element.18), calls=%async_computation | async-start | bytes 524288 | tf_op jit(solution)/shard_map/all_to_all | solution.py:540
  19.0 0.0 copy-start.1
  19.1 1.3 %bitcast_bitcast_fusion.field_ref = f32[7,4,64,128]{3,2,1,0:T(8,128)S(1)} fusion(f32[3,64,512]{2,1,0:T(8,128)} %get-tuple-element.17, f32[2,64,512]{2,1,0:T(8,128)} %param.11, f32[2,64,512]{2,1,0:T(8,128)} %param.10), kind=kLoop, calls=%fused_computation | loop fusion | flops 458752 | bytes 1835008 | tf_op jit(solution)/shard_map/transpose | solution.py:554
  20.4 1.3 %collective-permute-start.2 = (f32[7,64,128]{2,1,0:T(8,128)S(1)}, f32[7,64,128]{2,1,0:T(8,128)S(1)}, u32[]{:S(2)}, u32[]{:S(2)}) collective-permute-start(f32[7,64,128]{2,1,0:T(8,128)S(1)} %get-tuple-element.34), channel_id=1, source_target_pairs={{1,0},{2,1},{3,2},{4,3},{5,4},{6,5},{7,6},{8,7},{9,8},{10,9},{11,1... | collective-permute-start | bytes 688136 | tf_op jit(solution)/shard_map/ppermute | solution.py:528
  21.7 4.0 %collective-permute-start.1 = (f32[7,64,128]{2,1,0:T(8,128)S(1)}, f32[7,64,128]{2,1,0:T(8,128)S(1)}, u32[]{:S(2)}, u32[]{:S(2)}) collective-permute-start(f32[7,64,128]{2,1,0:T(8,128)S(1)} %get-tuple-element.35), channel_id=1, source_target_pairs={{0,1},{1,2},{2,3},{3,4},{4,5},{5,6},{6,7},{7,8},{8,9},{9,10},{10,1... | collective-permute-start | bytes 688136 | tf_op jit(solution)/shard_map/ppermute | solution.py:528
  25.7 0.0 copy-done
  25.7 0.0 copy-done.1
  25.8 6.6 %all-to-all-done = f32[128,4,128]{2,1,0:T(4,128)S(1)} async-done(((f32[128,4,128]{2,1,0:T(4,128)}), f32[128,4,128]{2,1,0:T(4,128)S(1)}, u32[]{:S(2)}, u32[]{:S(2)}) %all-to-all-start) | async-done | bytes 262176 | tf_op jit(solution)/shard_map/all_to_all | solution.py:540
  32.3 2.8 %collective-permute-start = (f32[512,128]{1,0:T(8,128)S(1)}, f32[512,128]{1,0:T(8,128)S(1)}, u32[]{:S(2)}, u32[]{:S(2)}) collective-permute-start(f32[512,128]{1,0:T(8,128)S(1)} %bitcast.26), channel_id=1, source_target_pairs={{0,16},{16,0},{32,48},{48,32},{64,80},{80,64},{96,112},{112,96},{1... | collective-permute-start | bytes 786440 | tf_op jit(solution)/shard_map/ppermute | solution.py:542
  35.3 1.1 collective-permute-done.other_ref
  36.3 11.6 %lookup.2 = (f32[2,4,40,128]{3,2,1,0:T(8,128)S(1)}, bf16[512,512]{1,0:T(8,128)(2,1)S(1)}) custom-call(s32[40,512]{1,0:T(8,128)S(1)} %get-tuple-element.44.index_ref, s32[40,512]{1,0:T(8,128)S(1)} %get-tuple-element.45.toggle_ref, f32[512,128]{1,0:T(8,128)S(1)} %bitcast.27, f32[512,128]{1,0:T(8,128)S(1)} %collective-permute-done.other_ref), custom_call_target="tpu_custom_call" | custom-call | flops 10737418240 | tf_op jit(solution)/shard_map/lookup/pallas_call | solution.py:163
  48.0 0.0 collective-permute-done.2.right_ref
  48.0 0.0 collective-permute-done.1.left_ref
  48.0 2.0 %edge_lookup.1.edge_ref = f32[7,64,128]{2,1,0:T(8,128)S(1)} custom-call(f32[7,64,128]{2,1,0:T(8,128)S(1)} %collective-permute-done.1.left_ref, f32[7,64,128]{2,1,0:T(8,128)S(1)} %collective-permute-done.2.right_ref, bf16[512,512]{1,0:T(8,128)(2,1)S(1)} %get-tuple-element.22.pieces_ref), custom_call_target="tpu_custom_call" | custom-call | flops 1342177280 | tf_op jit(solution)/shard_map/edge_lookup/pallas_call | solution.py:209
  50.1 2.7 %collective-permute-start.3 = (f32[35,20,128]{2,1,0:T(8,128)S(1)}, f32[35,20,128]{2,1,0:T(8,128)S(1)}, u32[]{:S(2)}, u32[]{:S(2)}) collective-permute-start(f32[35,20,128]{2,1,0:T(8,128)S(1)} %pad_maximum_fusion), channel_id=1, source_target_pairs={{0,16},{16,32},{32,48},{48,64},{64,80},{80,96},{96,112},{112,128},... | collective-permute-start | bytes 1075208 | tf_op jit(solution)/shard_map/ppermute | solution.py:528
  52.9 2.1 %collective-permute-start.4 = (f32[35,20,128]{2,1,0:T(8,128)S(1)}, f32[35,20,128]{2,1,0:T(8,128)S(1)}, u32[]{:S(2)}, u32[]{:S(2)}) collective-permute-start(f32[35,20,128]{2,1,0:T(8,128)S(1)} %pad_maximum_fusion.1), channel_id=1, source_target_pairs={{16,0},{32,16},{48,32},{64,48},{80,64},{96,80},{112,96},{128,112},... | collective-permute-start | bytes 1075208 | tf_op jit(solution)/shard_map/ppermute | solution.py:528
  55.0 6.8 %lookup.3.middle_ref = f32[2,4,24,128]{3,2,1,0:T(8,128)S(1)} custom-call(s32[24,512]{1,0:T(8,128)S(1)} %slice.58.index_ref, s32[24,512]{1,0:T(8,128)S(1)} %slice.59.toggle_ref, bf16[512,512]{1,0:T(8,128)(2,1)S(1)} %get-tuple-element.22.pieces_ref), custom_call_target="tpu_custom_call" | custom-call | flops 6442450944 | tf_op jit(solution)/shard_map/lookup/pallas_call | solution.py:163
  61.8 0.0 collective-permute-done.3.above_ref
  61.8 0.6 collective-permute-done.4.below_ref
  62.4 4.7 %first_step.1 = (f32[3,2,13,8,640]{4,3,2,1,0:T(8,128)S(1)}, f32[2,13,8,640]{3,2,1,0:T(8,128)S(1)}, f32[2,13,8,640]{3,2,1,0:T(8,128)S(1)}, f32[13,8,640]{2,1,0:T(8,128)S(1)}, f32[256,128]{1,0:T(8,128)S(1)}) custom-call(f32[7,4,64,128]{3,2,1,0:T(8,128)S(1)} %bitcast_bitcast_fusion.field_ref, f32[7,64,128]{2,1,0:T(8,128)S(1)} %edge_lookup.1.edge_ref, ...), custom_call_target="tpu_custom_call" | custom-call | tf_op jit(solution)/shard_map/first_step/pallas_call | solution.py:427
  67.0 20.9 %all_to_all.27 = f32[256,1,128]{2,1,0:T(1,128)S(1)} all-to-all(f32[256,1,128]{2,1,0:T(1,128)S(1)} %bitcast.28), channel_id=1, replica_groups=mesh['gx'=16,'gy'=16] {'gx','gy'}, dimensions={0} | all-to-all | bytes 262144 | tf_op jit(solution)/shard_map/all_to_all | solution.py:532
  88.0 4.5 %second_step.1 = (f32[2,64,512]{2,1,0:T(8,128)}, f32[3,2,13,8,640]{4,3,2,1,0:T(8,128)S(1)}, f32[2,13,8,512]{3,2,1,0:T(8,128)S(1)}, f32[256,128]{1,0:T(8,128)S(1)}) custom-call(f32[256,128]{1,0:T(8,128)S(1)} %bitcast.24, f32[3,2,13,8,640]{4,3,2,1,0:T(8,128)S(1)} %get-tuple-element.24.basis_ref, f32[2,13,8,640]{3,2,1,0:T(8,128)S(1)} %get-tuple-element.25.drop_ref, ...), custom_call_target="tpu_custom_call" | custom-call | tf_op jit(solution)/shard_map/second_step/pallas_call | solution.py:477
  92.5 18.4 %all_to_all.28 = f32[256,1,128]{2,1,0:T(1,128)S(1)} all-to-all(f32[256,1,128]{2,1,0:T(1,128)S(1)} %bitcast.29), channel_id=1, replica_groups=mesh['gx'=16,'gy'=16] {'gx','gy'}, dimensions={0} | all-to-all | bytes 262144 | tf_op jit(solution)/shard_map/all_to_all | solution.py:532
  110.9 1.0 last_step.1
  (11 shorter events, 0.2 us)
Async XLA Ops:
  2.5 23.2 %copy-start = (s32[64,512]{1,0:T(8,128)S(1)}, s32[64,512]{1,0:T(8,128)}, u32[]{:S(2)}) copy-start(s32[64,512]{1,0:T(8,128)} %index_in.1) | copy-start | bytes 393220
  2.6 29.8 %all-to-all-start = ((f32[128,4,128]{2,1,0:T(4,128)}), f32[128,4,128]{2,1,0:T(4,128)S(1)}, u32[]{:S(2)}, u32[]{:S(2)}) async-start(f32[128,4,128]{2,1,0:T(4,128)} %get-tuple-element.18), calls=%async_computation | async-start | bytes 524288 | tf_op jit(solution)/shard_map/all_to_all | solution.py:540
  19.0 6.7 %copy-start.1 = (s32[64,512]{1,0:T(8,128)S(1)}, s32[64,512]{1,0:T(8,128)}, u32[]{:S(2)}) copy-start(s32[64,512]{1,0:T(8,128)} %toggle_in.1) | copy-start | bytes 393220
  20.4 27.6 %collective-permute-start.2 = (f32[7,64,128]{2,1,0:T(8,128)S(1)}, f32[7,64,128]{2,1,0:T(8,128)S(1)}, u32[]{:S(2)}, u32[]{:S(2)}) collective-permute-start(f32[7,64,128]{2,1,0:T(8,128)S(1)} %get-tuple-element.34), channel_id=1, source_target_pairs={{1,0},{2,1},{3,2},{4,3},{5,4},{6,5},{7,6},{8,7},{9,8},{10,9},{11,1... | collective-permute-start | bytes 688136 | tf_op jit(solution)/shard_map/ppermute | solution.py:528
  21.7 26.3 %collective-permute-start.1 = (f32[7,64,128]{2,1,0:T(8,128)S(1)}, f32[7,64,128]{2,1,0:T(8,128)S(1)}, u32[]{:S(2)}, u32[]{:S(2)}) collective-permute-start(f32[7,64,128]{2,1,0:T(8,128)S(1)} %get-tuple-element.35), channel_id=1, source_target_pairs={{0,1},{1,2},{2,3},{3,4},{4,5},{5,6},{6,7},{7,8},{8,9},{9,10},{10,1... | collective-permute-start | bytes 688136 | tf_op jit(solution)/shard_map/ppermute | solution.py:528
  32.3 4.0 %collective-permute-start = (f32[512,128]{1,0:T(8,128)S(1)}, f32[512,128]{1,0:T(8,128)S(1)}, u32[]{:S(2)}, u32[]{:S(2)}) collective-permute-start(f32[512,128]{1,0:T(8,128)S(1)} %bitcast.26), channel_id=1, source_target_pairs={{0,16},{16,0},{32,48},{48,32},{64,80},{80,64},{96,112},{112,96},{1... | collective-permute-start | bytes 786440 | tf_op jit(solution)/shard_map/ppermute | solution.py:542
  50.1 11.7 %collective-permute-start.3 = (f32[35,20,128]{2,1,0:T(8,128)S(1)}, f32[35,20,128]{2,1,0:T(8,128)S(1)}, u32[]{:S(2)}, u32[]{:S(2)}) collective-permute-start(f32[35,20,128]{2,1,0:T(8,128)S(1)} %pad_maximum_fusion), channel_id=1, source_target_pairs={{0,16},{16,32},{32,48},{48,64},{64,80},{80,96},{96,112},{112,128},... | collective-permute-start | bytes 1075208 | tf_op jit(solution)/shard_map/ppermute | solution.py:528
  52.9 9.5 %collective-permute-start.4 = (f32[35,20,128]{2,1,0:T(8,128)S(1)}, f32[35,20,128]{2,1,0:T(8,128)S(1)}, u32[]{:S(2)}, u32[]{:S(2)}) collective-permute-start(f32[35,20,128]{2,1,0:T(8,128)S(1)} %pad_maximum_fusion.1), channel_id=1, source_target_pairs={{16,0},{32,16},{48,32},{64,48},{80,64},{96,80},{112,96},{128,112},... | collective-permute-start | bytes 1075208 | tf_op jit(solution)/shard_map/ppermute | solution.py:528

commit v5 on v4

--- a/solution.py
+++ b/solution.py
@@ -114,15 +114,17 @@
     got = jnp.dot(pieces_ref[...], jnp.concatenate(hot, 0), preferred_element_type=jnp.float32)
     half = got.shape[0] // 2
     value = (got[:half] + got[half:]).reshape(MANY, SUBSTEPS, cols)
-    chosen = value[0]
-    for a in range(1, MANY):
-        chosen = jnp.where(which == a, value[a], chosen)
+    values = [value[a] for a in range(MANY)]
+    for bit in range(MANY.bit_length() - 1):
+        upper = (which >> bit) & 1 == 1
+        values = [jnp.where(upper, v, u) for u, v in zip(values[::2], values[1::2])]
+    chosen = values[0]
     moment = lax.broadcasted_iota(jnp.int32, (SUBSTEPS, cols), 0) + toggle
     share = SUBSTEPS // STEPS
+    window = moment >> (share.bit_length() - 1)
     means = []
     for k in range(STEPS):
-        inside = (moment >= k * share) & (moment < (k + 1) * share)
-        total = jnp.sum(jnp.where(inside, chosen, 0.0), axis=0, keepdims=True)
+        total = jnp.sum(jnp.where(window == k, chosen, 0.0), axis=0, keepdims=True)
         means.append(total * (1.0 / share))
     return means
 

time: 112 us -> 114 us (1.018)
  Pallas kernels: 32.4 us -> 34.2 us
    pallas_call x2, Pallas kernels: 18.4 us -> 20 us  [lookup(): pl.pallas_call(functools.partial(first_lookup_kernel if fresh else lookup...]
  transfers between devices with their start and end apart: 6 -> 6, of which waited for: 3 -> 2; matrix products, arithmetic and copies ran while one was open for 1% -> 1% of each run, Pallas kernels for 16% -> 18%
where the time goes in v5:
time: 114 us
  blocking collectives  39.9 us (35%)
  Pallas kernels  34.2 us (30%)
  starting transfers between devices  29.4 us (26%)
  waiting for transfers between devices  7.66 us (7%)
  other arithmetic  1.37 us (1%)
    all_to_all x2, blocking collectives, exchange(): return lax.all_to_all(block, BOTH, 0, 0, tiled=True)  39.9 us
    pallas_call x2, Pallas kernels, lookup(): pl.pallas_call(functools.partial(first_lookup_kernel if fresh else lookup...  20 us
    all_to_all x1, starting transfers between devices, gather_tables(): lax.all_to_all(block, BOTH, 0, 0, tiled=True, axis_index_groups=groups)  16.5 us
    ppermute x4, starting transfers between devices, shift(): lax.ppermute(block, axis, pairs if up else [(b, a) for a, b in pairs])  10.1 us
    all_to_all x1, waiting for transfers between devices, gather_tables(): lax.all_to_all(block, BOTH, 0, 0, tiled=True, axis_index_groups=groups)  6.58 us
    pallas_call x1, Pallas kernels, first_step(): pl.pallas_call(functools.partial(first_kernel, deep, rows, width, ends.sh...  4.67 us
    pallas_call x1, Pallas kernels, second_step(): pl.pallas_call(functools.partial(second_kernel, deep, rows, width), out_s...  4.49 us
    ppermute x1, starting transfers between devices, gather_tables(): return (own, lax.ppermute(own, 'gx', [(i, i ^ 1) for i in range(outer)]))  2.82 us
  transfers between devices with their start and end apart: 6, of which 2 were waited for; matrix products, arithmetic and copies ran while one was open for 1% of the time, Pallas kernels for 18%

profile of v5, /device:TPU:1, one launch (start us, length us, event | category | flops | bytes accessed | tf_op | source)
XLA Modules:
  0.0 113.6 jit_solution(3905468993327838702)
XLA Ops:
  0.6 1.9 %address.1 = (f32[128,4,128]{2,1,0:T(4,128)}, f32[3,64,512]{2,1,0:T(8,128)}) custom-call(f32[16,32]{1,0:T(8,128)} %table_in.1, s32[64,512]{1,0:T(8,128)} %tap_in.1, s32[64,512]{1,0:T(8,128)} %index_in.1, s32[64,512]{1,0:T(8,128)} %toggle_in.1), custom_call_target="tpu_custom_call" | custom-call | tf_op jit(solution)/shard_map/address/pallas_call | solution.py:65
  2.5 0.0 copy-start
  2.6 16.5 %all-to-all-start = ((f32[128,4,128]{2,1,0:T(4,128)}), f32[128,4,128]{2,1,0:T(4,128)S(1)}, u32[]{:S(2)}, u32[]{:S(2)}) async-start(f32[128,4,128]{2,1,0:T(4,128)} %get-tuple-element.18), calls=%async_computation | async-start | bytes 524288 | tf_op jit(solution)/shard_map/all_to_all | solution.py:542
  19.0 0.0 copy-start.1
  19.1 1.3 %bitcast_bitcast_fusion.field_ref = f32[7,4,64,128]{3,2,1,0:T(8,128)S(1)} fusion(f32[3,64,512]{2,1,0:T(8,128)} %get-tuple-element.17, f32[2,64,512]{2,1,0:T(8,128)} %param.11, f32[2,64,512]{2,1,0:T(8,128)} %param.10), kind=kLoop, calls=%fused_computation | loop fusion | flops 458752 | bytes 1835008 | tf_op jit(solution)/shard_map/transpose | solution.py:556
  20.4 1.3 %collective-permute-start.2 = (f32[7,64,128]{2,1,0:T(8,128)S(1)}, f32[7,64,128]{2,1,0:T(8,128)S(1)}, u32[]{:S(2)}, u32[]{:S(2)}) collective-permute-start(f32[7,64,128]{2,1,0:T(8,128)S(1)} %get-tuple-element.34), channel_id=1, source_target_pairs={{1,0},{2,1},{3,2},{4,3},{5,4},{6,5},{7,6},{8,7},{9,8},{10,9},{11,1... | collective-permute-start | bytes 688136 | tf_op jit(solution)/shard_map/ppermute | solution.py:530
  21.7 4.0 %collective-permute-start.1 = (f32[7,64,128]{2,1,0:T(8,128)S(1)}, f32[7,64,128]{2,1,0:T(8,128)S(1)}, u32[]{:S(2)}, u32[]{:S(2)}) collective-permute-start(f32[7,64,128]{2,1,0:T(8,128)S(1)} %get-tuple-element.35), channel_id=1, source_target_pairs={{0,1},{1,2},{2,3},{3,4},{4,5},{5,6},{6,7},{7,8},{8,9},{9,10},{10,1... | collective-permute-start | bytes 688136 | tf_op jit(solution)/shard_map/ppermute | solution.py:530
  25.7 0.0 copy-done
  25.7 0.0 copy-done.1
  25.8 6.6 %all-to-all-done = f32[128,4,128]{2,1,0:T(4,128)S(1)} async-done(((f32[128,4,128]{2,1,0:T(4,128)}), f32[128,4,128]{2,1,0:T(4,128)S(1)}, u32[]{:S(2)}, u32[]{:S(2)}) %all-to-all-start) | async-done | bytes 262176 | tf_op jit(solution)/shard_map/all_to_all | solution.py:542
  32.3 2.8 %collective-permute-start = (f32[512,128]{1,0:T(8,128)S(1)}, f32[512,128]{1,0:T(8,128)S(1)}, u32[]{:S(2)}, u32[]{:S(2)}) collective-permute-start(f32[512,128]{1,0:T(8,128)S(1)} %bitcast.26), channel_id=1, source_target_pairs={{0,16},{16,0},{32,48},{48,32},{64,80},{80,64},{96,112},{112,96},{1... | collective-permute-start | bytes 786440 | tf_op jit(solution)/shard_map/ppermute | solution.py:544
  35.3 1.1 collective-permute-done.other_ref
  36.3 12.6 %lookup.2 = (f32[2,4,40,128]{3,2,1,0:T(8,128)S(1)}, bf16[512,512]{1,0:T(8,128)(2,1)S(1)}) custom-call(s32[40,512]{1,0:T(8,128)S(1)} %get-tuple-element.44.index_ref, s32[40,512]{1,0:T(8,128)S(1)} %get-tuple-element.45.toggle_ref, f32[512,128]{1,0:T(8,128)S(1)} %bitcast.27, f32[512,128]{1,0:T(8,128)S(1)} %collective-permute-done.other_ref), custom_call_target="tpu_custom_call" | custom-call | flops 10737418240 | tf_op jit(solution)/shard_map/lookup/pallas_call | solution.py:165
  49.0 0.0 collective-permute-done.2.right_ref
  49.0 0.0 collective-permute-done.1.left_ref
  49.0 2.2 %edge_lookup.1.edge_ref = f32[7,64,128]{2,1,0:T(8,128)S(1)} custom-call(f32[7,64,128]{2,1,0:T(8,128)S(1)} %collective-permute-done.1.left_ref, f32[7,64,128]{2,1,0:T(8,128)S(1)} %collective-permute-done.2.right_ref, bf16[512,512]{1,0:T(8,128)(2,1)S(1)} %get-tuple-element.22.pieces_ref), custom_call_target="tpu_custom_call" | custom-call | flops 1342177280 | tf_op jit(solution)/shard_map/edge_lookup/pallas_call | solution.py:211
  51.3 2.7 %collective-permute-start.3 = (f32[35,20,128]{2,1,0:T(8,128)S(1)}, f32[35,20,128]{2,1,0:T(8,128)S(1)}, u32[]{:S(2)}, u32[]{:S(2)}) collective-permute-start(f32[35,20,128]{2,1,0:T(8,128)S(1)} %pad_maximum_fusion), channel_id=1, source_target_pairs={{0,16},{16,32},{32,48},{48,64},{64,80},{80,96},{96,112},{112,128},... | collective-permute-start | bytes 1075208 | tf_op jit(solution)/shard_map/ppermute | solution.py:530
  54.0 2.1 %collective-permute-start.4 = (f32[35,20,128]{2,1,0:T(8,128)S(1)}, f32[35,20,128]{2,1,0:T(8,128)S(1)}, u32[]{:S(2)}, u32[]{:S(2)}) collective-permute-start(f32[35,20,128]{2,1,0:T(8,128)S(1)} %pad_maximum_fusion.1), channel_id=1, source_target_pairs={{16,0},{32,16},{48,32},{64,48},{80,64},{96,80},{112,96},{128,112},... | collective-permute-start | bytes 1075208 | tf_op jit(solution)/shard_map/ppermute | solution.py:530
  56.2 7.4 %lookup.3.middle_ref = f32[2,4,24,128]{3,2,1,0:T(8,128)S(1)} custom-call(s32[24,512]{1,0:T(8,128)S(1)} %slice.58.index_ref, s32[24,512]{1,0:T(8,128)S(1)} %slice.59.toggle_ref, bf16[512,512]{1,0:T(8,128)(2,1)S(1)} %get-tuple-element.22.pieces_ref), custom_call_target="tpu_custom_call" | custom-call | flops 6442450944 | tf_op jit(solution)/shard_map/lookup/pallas_call | solution.py:165
  63.6 0.0 collective-permute-done.3.above_ref
  63.6 0.0 collective-permute-done.4.below_ref
  63.6 4.7 %first_step.1 = (f32[3,2,13,8,640]{4,3,2,1,0:T(8,128)S(1)}, f32[2,13,8,640]{3,2,1,0:T(8,128)S(1)}, f32[2,13,8,640]{3,2,1,0:T(8,128)S(1)}, f32[13,8,640]{2,1,0:T(8,128)S(1)}, f32[256,128]{1,0:T(8,128)S(1)}) custom-call(f32[7,4,64,128]{3,2,1,0:T(8,128)S(1)} %bitcast_bitcast_fusion.field_ref, f32[7,64,128]{2,1,0:T(8,128)S(1)} %edge_lookup.1.edge_ref, ...), custom_call_target="tpu_custom_call" | custom-call | tf_op jit(solution)/shard_map/first_step/pallas_call | solution.py:429
  68.3 21.5 %all_to_all.27 = f32[256,1,128]{2,1,0:T(1,128)S(1)} all-to-all(f32[256,1,128]{2,1,0:T(1,128)S(1)} %bitcast.28), channel_id=1, replica_groups=mesh['gx'=16,'gy'=16] {'gx','gy'}, dimensions={0} | all-to-all | bytes 262144 | tf_op jit(solution)/shard_map/all_to_all | solution.py:534
  89.8 4.5 %second_step.1 = (f32[2,64,512]{2,1,0:T(8,128)}, f32[3,2,13,8,640]{4,3,2,1,0:T(8,128)S(1)}, f32[2,13,8,512]{3,2,1,0:T(8,128)S(1)}, f32[256,128]{1,0:T(8,128)S(1)}) custom-call(f32[256,128]{1,0:T(8,128)S(1)} %bitcast.24, f32[3,2,13,8,640]{4,3,2,1,0:T(8,128)S(1)} %get-tuple-element.24.basis_ref, f32[2,13,8,640]{3,2,1,0:T(8,128)S(1)} %get-tuple-element.25.drop_ref, ...), custom_call_target="tpu_custom_call" | custom-call | tf_op jit(solution)/shard_map/second_step/pallas_call | solution.py:479
  94.3 18.4 %all_to_all.28 = f32[256,1,128]{2,1,0:T(1,128)S(1)} all-to-all(f32[256,1,128]{2,1,0:T(1,128)S(1)} %bitcast.29), channel_id=1, replica_groups=mesh['gx'=16,'gy'=16] {'gx','gy'}, dimensions={0} | all-to-all | bytes 262144 | tf_op jit(solution)/shard_map/all_to_all | solution.py:534
  112.7 1.0 last_step.1
  (11 shorter events, 0.2 us)
Async XLA Ops:
  2.5 23.2 %copy-start = (s32[64,512]{1,0:T(8,128)S(1)}, s32[64,512]{1,0:T(8,128)}, u32[]{:S(2)}) copy-start(s32[64,512]{1,0:T(8,128)} %index_in.1) | copy-start | bytes 393220
  2.6 29.8 %all-to-all-start = ((f32[128,4,128]{2,1,0:T(4,128)}), f32[128,4,128]{2,1,0:T(4,128)S(1)}, u32[]{:S(2)}, u32[]{:S(2)}) async-start(f32[128,4,128]{2,1,0:T(4,128)} %get-tuple-element.18), calls=%async_computation | async-start | bytes 524288 | tf_op jit(solution)/shard_map/all_to_all | solution.py:542
  19.0 6.7 %copy-start.1 = (s32[64,512]{1,0:T(8,128)S(1)}, s32[64,512]{1,0:T(8,128)}, u32[]{:S(2)}) copy-start(s32[64,512]{1,0:T(8,128)} %toggle_in.1) | copy-start | bytes 393220
  20.4 28.6 %collective-permute-start.2 = (f32[7,64,128]{2,1,0:T(8,128)S(1)}, f32[7,64,128]{2,1,0:T(8,128)S(1)}, u32[]{:S(2)}, u32[]{:S(2)}) collective-permute-start(f32[7,64,128]{2,1,0:T(8,128)S(1)} %get-tuple-element.34), channel_id=1, source_target_pairs={{1,0},{2,1},{3,2},{4,3},{5,4},{6,5},{7,6},{8,7},{9,8},{10,9},{11,1... | collective-permute-start | bytes 688136 | tf_op jit(solution)/shard_map/ppermute | solution.py:530
  21.7 27.3 %collective-permute-start.1 = (f32[7,64,128]{2,1,0:T(8,128)S(1)}, f32[7,64,128]{2,1,0:T(8,128)S(1)}, u32[]{:S(2)}, u32[]{:S(2)}) collective-permute-start(f32[7,64,128]{2,1,0:T(8,128)S(1)} %get-tuple-element.35), channel_id=1, source_target_pairs={{0,1},{1,2},{2,3},{3,4},{4,5},{5,6},{6,7},{7,8},{8,9},{9,10},{10,1... | collective-permute-start | bytes 688136 | tf_op jit(solution)/shard_map/ppermute | solution.py:530
  32.3 4.0 %collective-permute-start = (f32[512,128]{1,0:T(8,128)S(1)}, f32[512,128]{1,0:T(8,128)S(1)}, u32[]{:S(2)}, u32[]{:S(2)}) collective-permute-start(f32[512,128]{1,0:T(8,128)S(1)} %bitcast.26), channel_id=1, source_target_pairs={{0,16},{16,0},{32,48},{48,32},{64,80},{80,64},{96,112},{112,96},{1... | collective-permute-start | bytes 786440 | tf_op jit(solution)/shard_map/ppermute | solution.py:544
  51.3 12.3 %collective-permute-start.3 = (f32[35,20,128]{2,1,0:T(8,128)S(1)}, f32[35,20,128]{2,1,0:T(8,128)S(1)}, u32[]{:S(2)}, u32[]{:S(2)}) collective-permute-start(f32[35,20,128]{2,1,0:T(8,128)S(1)} %pad_maximum_fusion), channel_id=1, source_target_pairs={{0,16},{16,32},{32,48},{48,64},{64,80},{80,96},{96,112},{112,128},... | collective-permute-start | bytes 1075208 | tf_op jit(solution)/shard_map/ppermute | solution.py:530
  54.0 9.5 %collective-permute-start.4 = (f32[35,20,128]{2,1,0:T(8,128)S(1)}, f32[35,20,128]{2,1,0:T(8,128)S(1)}, u32[]{:S(2)}, u32[]{:S(2)}) collective-permute-start(f32[35,20,128]{2,1,0:T(8,128)S(1)} %pad_maximum_fusion.1), channel_id=1, source_target_pairs={{16,0},{32,16},{48,32},{64,48},{80,64},{96,80},{112,96},{128,112},... | collective-permute-start | bytes 1075208 | tf_op jit(solution)/shard_map/ppermute | solution.py:530

commit v6 on v4

--- a/solution.py
+++ b/solution.py
@@ -129,18 +129,12 @@
 
 def lookup_rows(many, index_ref, toggle_ref, pieces_ref, out_ref):
     rows, cols = index_ref.shape
-    unroll = rows if rows <= 24 else math.gcd(rows, 20)
-
-    def body(i, carry):
-        for u in range(unroll):
-            row = pl.ds(i * unroll + u, 1)
-            means = charges(many, index_ref[row, :], toggle_ref[row, :], pieces_ref)
-            for k, mean in enumerate(means):
-                for b in range(cols // LANES):
-                    out_ref[k, b, row, :] = mean[:, b * LANES : (b + 1) * LANES]
-        return carry
-
-    lax.fori_loop(0, rows // unroll, body, 0)
+    for r in range(rows):
+        row = pl.ds(r, 1)
+        means = charges(many, index_ref[row, :], toggle_ref[row, :], pieces_ref)
+        for k, mean in enumerate(means):
+            for b in range(cols // LANES):
+                out_ref[k, b, row, :] = mean[:, b * LANES : (b + 1) * LANES]
 
 
 def first_lookup_kernel(many, index_ref, toggle_ref, own_ref, other_ref, out_ref, pieces_ref):

time: 112 us -> 112 us (level)
  no operation moved by 1% of the time
where the time goes in v6:
time: 112 us
  blocking collectives  39.6 us (35%)
  Pallas kernels  32.1 us (29%)
  starting transfers between devices  29.5 us (26%)
  waiting for transfers between devices  8.19 us (7%)
  other arithmetic  1.37 us (1%)
    all_to_all x2, blocking collectives, exchange(): return lax.all_to_all(block, BOTH, 0, 0, tiled=True)  39.6 us
    pallas_call x2, Pallas kernels, lookup(): pl.pallas_call(functools.partial(first_lookup_kernel if fresh else lookup...  18.1 us
    all_to_all x1, starting transfers between devices, gather_tables(): lax.all_to_all(block, BOTH, 0, 0, tiled=True, axis_index_groups=groups)  16.5 us
    ppermute x4, starting transfers between devices, shift(): lax.ppermute(block, axis, pairs if up else [(b, a) for a, b in pairs])  10.2 us
    all_to_all x1, waiting for transfers between devices, gather_tables(): lax.all_to_all(block, BOTH, 0, 0, tiled=True, axis_index_groups=groups)  6.58 us
    pallas_call x1, Pallas kernels, first_step(): pl.pallas_call(functools.partial(first_kernel, deep, rows, width, ends.sh...  4.67 us
    pallas_call x1, Pallas kernels, second_step(): pl.pallas_call(functools.partial(second_kernel, deep, rows, width), out_s...  4.49 us
    ppermute x1, starting transfers between devices, gather_tables(): return (own, lax.ppermute(own, 'gx', [(i, i ^ 1) for i in range(outer)]))  2.82 us
  transfers between devices with their start and end apart: 6, of which 3 were waited for; matrix products, arithmetic and copies ran while one was open for 1% of the time, Pallas kernels for 16%

profile of v6, /device:TPU:1, one launch (start us, length us, event | category | flops | bytes accessed | tf_op | source)
XLA Modules:
  0.0 111.7 jit_solution(17042360103016207919)
XLA Ops:
  0.6 1.9 %address.1 = (f32[128,4,128]{2,1,0:T(4,128)}, f32[3,64,512]{2,1,0:T(8,128)}) custom-call(f32[16,32]{1,0:T(8,128)} %table_in.1, s32[64,512]{1,0:T(8,128)} %tap_in.1, s32[64,512]{1,0:T(8,128)} %index_in.1, s32[64,512]{1,0:T(8,128)} %toggle_in.1), custom_call_target="tpu_custom_call" | custom-call | tf_op jit(solution)/shard_map/address/pallas_call | solution.py:65
  2.5 0.0 copy-start
  2.6 16.5 %all-to-all-start = ((f32[128,4,128]{2,1,0:T(4,128)}), f32[128,4,128]{2,1,0:T(4,128)S(1)}, u32[]{:S(2)}, u32[]{:S(2)}) async-start(f32[128,4,128]{2,1,0:T(4,128)} %get-tuple-element.18), calls=%async_computation | async-start | bytes 524288 | tf_op jit(solution)/shard_map/all_to_all | solution.py:534
  19.0 0.0 copy-start.1
  19.1 1.3 %bitcast_bitcast_fusion.field_ref = f32[7,4,64,128]{3,2,1,0:T(8,128)S(1)} fusion(f32[3,64,512]{2,1,0:T(8,128)} %get-tuple-element.17, f32[2,64,512]{2,1,0:T(8,128)} %param.11, f32[2,64,512]{2,1,0:T(8,128)} %param.10), kind=kLoop, calls=%fused_computation | loop fusion | flops 458752 | bytes 1835008 | tf_op jit(solution)/shard_map/transpose | solution.py:548
  20.4 1.3 %collective-permute-start.2 = (f32[7,64,128]{2,1,0:T(8,128)S(1)}, f32[7,64,128]{2,1,0:T(8,128)S(1)}, u32[]{:S(2)}, u32[]{:S(2)}) collective-permute-start(f32[7,64,128]{2,1,0:T(8,128)S(1)} %get-tuple-element.34), channel_id=1, source_target_pairs={{1,0},{2,1},{3,2},{4,3},{5,4},{6,5},{7,6},{8,7},{9,8},{10,9},{11,1... | collective-permute-start | bytes 688136 | tf_op jit(solution)/shard_map/ppermute | solution.py:522
  21.7 4.0 %collective-permute-start.1 = (f32[7,64,128]{2,1,0:T(8,128)S(1)}, f32[7,64,128]{2,1,0:T(8,128)S(1)}, u32[]{:S(2)}, u32[]{:S(2)}) collective-permute-start(f32[7,64,128]{2,1,0:T(8,128)S(1)} %get-tuple-element.35), channel_id=1, source_target_pairs={{0,1},{1,2},{2,3},{3,4},{4,5},{5,6},{6,7},{7,8},{8,9},{9,10},{10,1... | collective-permute-start | bytes 688136 | tf_op jit(solution)/shard_map/ppermute | solution.py:522
  25.7 0.0 copy-done
  25.7 0.0 copy-done.1
  25.8 6.6 %all-to-all-done = f32[128,4,128]{2,1,0:T(4,128)S(1)} async-done(((f32[128,4,128]{2,1,0:T(4,128)}), f32[128,4,128]{2,1,0:T(4,128)S(1)}, u32[]{:S(2)}, u32[]{:S(2)}) %all-to-all-start) | async-done | bytes 262176 | tf_op jit(solution)/shard_map/all_to_all | solution.py:534
  32.3 2.8 %collective-permute-start = (f32[512,128]{1,0:T(8,128)S(1)}, f32[512,128]{1,0:T(8,128)S(1)}, u32[]{:S(2)}, u32[]{:S(2)}) collective-permute-start(f32[512,128]{1,0:T(8,128)S(1)} %bitcast.26), channel_id=1, source_target_pairs={{0,16},{16,0},{32,48},{48,32},{64,80},{80,64},{96,112},{112,96},{1... | collective-permute-start | bytes 786440 | tf_op jit(solution)/shard_map/ppermute | solution.py:536
  35.3 1.1 collective-permute-done.other_ref
  36.3 11.3 %lookup.2 = (f32[2,4,40,128]{3,2,1,0:T(8,128)S(1)}, bf16[512,512]{1,0:T(8,128)(2,1)S(1)}) custom-call(s32[40,512]{1,0:T(8,128)S(1)} %get-tuple-element.44.index_ref, s32[40,512]{1,0:T(8,128)S(1)} %get-tuple-element.45.toggle_ref, f32[512,128]{1,0:T(8,128)S(1)} %bitcast.27, f32[512,128]{1,0:T(8,128)S(1)} %collective-permute-done.other_ref), custom_call_target="tpu_custom_call" | custom-call | flops 10737418240 | tf_op jit(solution)/shard_map/lookup/pallas_call | solution.py:157
  47.6 0.0 collective-permute-done.2.right_ref
  47.6 0.0 collective-permute-done.1.left_ref
  47.6 2.0 %edge_lookup.1.edge_ref = f32[7,64,128]{2,1,0:T(8,128)S(1)} custom-call(f32[7,64,128]{2,1,0:T(8,128)S(1)} %collective-permute-done.1.left_ref, f32[7,64,128]{2,1,0:T(8,128)S(1)} %collective-permute-done.2.right_ref, bf16[512,512]{1,0:T(8,128)(2,1)S(1)} %get-tuple-element.22.pieces_ref), custom_call_target="tpu_custom_call" | custom-call | flops 1342177280 | tf_op jit(solution)/shard_map/edge_lookup/pallas_call | solution.py:203
  49.7 2.7 %collective-permute-start.3 = (f32[35,20,128]{2,1,0:T(8,128)S(1)}, f32[35,20,128]{2,1,0:T(8,128)S(1)}, u32[]{:S(2)}, u32[]{:S(2)}) collective-permute-start(f32[35,20,128]{2,1,0:T(8,128)S(1)} %pad_maximum_fusion), channel_id=1, source_target_pairs={{0,16},{16,32},{32,48},{48,64},{64,80},{80,96},{96,112},{112,128},... | collective-permute-start | bytes 1075208 | tf_op jit(solution)/shard_map/ppermute | solution.py:522
  52.5 2.1 %collective-permute-start.4 = (f32[35,20,128]{2,1,0:T(8,128)S(1)}, f32[35,20,128]{2,1,0:T(8,128)S(1)}, u32[]{:S(2)}, u32[]{:S(2)}) collective-permute-start(f32[35,20,128]{2,1,0:T(8,128)S(1)} %pad_maximum_fusion.1), channel_id=1, source_target_pairs={{16,0},{32,16},{48,32},{64,48},{80,64},{96,80},{112,96},{128,112},... | collective-permute-start | bytes 1075208 | tf_op jit(solution)/shard_map/ppermute | solution.py:522
  54.7 6.8 %lookup.3.middle_ref = f32[2,4,24,128]{3,2,1,0:T(8,128)S(1)} custom-call(s32[24,512]{1,0:T(8,128)S(1)} %slice.58.index_ref, s32[24,512]{1,0:T(8,128)S(1)} %slice.59.toggle_ref, bf16[512,512]{1,0:T(8,128)(2,1)S(1)} %get-tuple-element.22.pieces_ref), custom_call_target="tpu_custom_call" | custom-call | flops 6442450944 | tf_op jit(solution)/shard_map/lookup/pallas_call | solution.py:157
  61.4 0.0 collective-permute-done.3.above_ref
  61.5 0.5 collective-permute-done.4.below_ref
  62.0 4.7 %first_step.1 = (f32[3,2,13,8,640]{4,3,2,1,0:T(8,128)S(1)}, f32[2,13,8,640]{3,2,1,0:T(8,128)S(1)}, f32[2,13,8,640]{3,2,1,0:T(8,128)S(1)}, f32[13,8,640]{2,1,0:T(8,128)S(1)}, f32[256,128]{1,0:T(8,128)S(1)}) custom-call(f32[7,4,64,128]{3,2,1,0:T(8,128)S(1)} %bitcast_bitcast_fusion.field_ref, f32[7,64,128]{2,1,0:T(8,128)S(1)} %edge_lookup.1.edge_ref, ...), custom_call_target="tpu_custom_call" | custom-call | tf_op jit(solution)/shard_map/first_step/pallas_call | solution.py:421
  66.7 21.2 %all_to_all.27 = f32[256,1,128]{2,1,0:T(1,128)S(1)} all-to-all(f32[256,1,128]{2,1,0:T(1,128)S(1)} %bitcast.28), channel_id=1, replica_groups=mesh['gx'=16,'gy'=16] {'gx','gy'}, dimensions={0} | all-to-all | bytes 262144 | tf_op jit(solution)/shard_map/all_to_all | solution.py:526
  87.8 4.5 %second_step.1 = (f32[2,64,512]{2,1,0:T(8,128)}, f32[3,2,13,8,640]{4,3,2,1,0:T(8,128)S(1)}, f32[2,13,8,512]{3,2,1,0:T(8,128)S(1)}, f32[256,128]{1,0:T(8,128)S(1)}) custom-call(f32[256,128]{1,0:T(8,128)S(1)} %bitcast.24, f32[3,2,13,8,640]{4,3,2,1,0:T(8,128)S(1)} %get-tuple-element.24.basis_ref, f32[2,13,8,640]{3,2,1,0:T(8,128)S(1)} %get-tuple-element.25.drop_ref, ...), custom_call_target="tpu_custom_call" | custom-call | tf_op jit(solution)/shard_map/second_step/pallas_call | solution.py:471
  92.3 18.4 %all_to_all.28 = f32[256,1,128]{2,1,0:T(1,128)S(1)} all-to-all(f32[256,1,128]{2,1,0:T(1,128)S(1)} %bitcast.29), channel_id=1, replica_groups=mesh['gx'=16,'gy'=16] {'gx','gy'}, dimensions={0} | all-to-all | bytes 262144 | tf_op jit(solution)/shard_map/all_to_all | solution.py:526
  110.7 1.0 last_step.1
  (11 shorter events, 0.2 us)
Async XLA Ops:
  2.5 23.2 %copy-start = (s32[64,512]{1,0:T(8,128)S(1)}, s32[64,512]{1,0:T(8,128)}, u32[]{:S(2)}) copy-start(s32[64,512]{1,0:T(8,128)} %index_in.1) | copy-start | bytes 393220
  2.6 29.8 %all-to-all-start = ((f32[128,4,128]{2,1,0:T(4,128)}), f32[128,4,128]{2,1,0:T(4,128)S(1)}, u32[]{:S(2)}, u32[]{:S(2)}) async-start(f32[128,4,128]{2,1,0:T(4,128)} %get-tuple-element.18), calls=%async_computation | async-start | bytes 524288 | tf_op jit(solution)/shard_map/all_to_all | solution.py:534
  19.0 6.7 %copy-start.1 = (s32[64,512]{1,0:T(8,128)S(1)}, s32[64,512]{1,0:T(8,128)}, u32[]{:S(2)}) copy-start(s32[64,512]{1,0:T(8,128)} %toggle_in.1) | copy-start | bytes 393220
  20.4 27.2 %collective-permute-start.2 = (f32[7,64,128]{2,1,0:T(8,128)S(1)}, f32[7,64,128]{2,1,0:T(8,128)S(1)}, u32[]{:S(2)}, u32[]{:S(2)}) collective-permute-start(f32[7,64,128]{2,1,0:T(8,128)S(1)} %get-tuple-element.34), channel_id=1, source_target_pairs={{1,0},{2,1},{3,2},{4,3},{5,4},{6,5},{7,6},{8,7},{9,8},{10,9},{11,1... | collective-permute-start | bytes 688136 | tf_op jit(solution)/shard_map/ppermute | solution.py:522
  21.7 25.9 %collective-permute-start.1 = (f32[7,64,128]{2,1,0:T(8,128)S(1)}, f32[7,64,128]{2,1,0:T(8,128)S(1)}, u32[]{:S(2)}, u32[]{:S(2)}) collective-permute-start(f32[7,64,128]{2,1,0:T(8,128)S(1)} %get-tuple-element.35), channel_id=1, source_target_pairs={{0,1},{1,2},{2,3},{3,4},{4,5},{5,6},{6,7},{7,8},{8,9},{9,10},{10,1... | collective-permute-start | bytes 688136 | tf_op jit(solution)/shard_map/ppermute | solution.py:522
  32.3 4.0 %collective-permute-start = (f32[512,128]{1,0:T(8,128)S(1)}, f32[512,128]{1,0:T(8,128)S(1)}, u32[]{:S(2)}, u32[]{:S(2)}) collective-permute-start(f32[512,128]{1,0:T(8,128)S(1)} %bitcast.26), channel_id=1, source_target_pairs={{0,16},{16,0},{32,48},{48,32},{64,80},{80,64},{96,112},{112,96},{1... | collective-permute-start | bytes 786440 | tf_op jit(solution)/shard_map/ppermute | solution.py:536
  49.7 11.7 %collective-permute-start.3 = (f32[35,20,128]{2,1,0:T(8,128)S(1)}, f32[35,20,128]{2,1,0:T(8,128)S(1)}, u32[]{:S(2)}, u32[]{:S(2)}) collective-permute-start(f32[35,20,128]{2,1,0:T(8,128)S(1)} %pad_maximum_fusion), channel_id=1, source_target_pairs={{0,16},{16,32},{32,48},{48,64},{64,80},{80,96},{96,112},{112,128},... | collective-permute-start | bytes 1075208 | tf_op jit(solution)/shard_map/ppermute | solution.py:522
  52.5 9.5 %collective-permute-start.4 = (f32[35,20,128]{2,1,0:T(8,128)S(1)}, f32[35,20,128]{2,1,0:T(8,128)S(1)}, u32[]{:S(2)}, u32[]{:S(2)}) collective-permute-start(f32[35,20,128]{2,1,0:T(8,128)S(1)} %pad_maximum_fusion.1), channel_id=1, source_target_pairs={{16,0},{32,16},{48,32},{64,48},{80,64},{96,80},{112,96},{128,112},... | collective-permute-start | bytes 1075208 | tf_op jit(solution)/shard_map/ppermute | solution.py:522

commit v7 on v6

--- a/solution.py
+++ b/solution.py
@@ -307,7 +307,9 @@
                 part = [t if p is None else p + t for p, t in zip(part, terms)]
         return [t + jnp.where(inside, p, 0.0) for t, p in zip(totals, part)]
 
-    totals = lax.fori_loop(0, deep, body, [jnp.zeros((GROUP, LANES), jnp.float32)] * 9)
+    totals = [jnp.zeros((GROUP, LANES), jnp.float32)] * 9
+    for i in range(deep):
+        totals = body(i, totals)
     sums_ref[...] = jnp.zeros_like(sums_ref)
     for k, total in enumerate(totals):
         sums_ref[pl.ds(k, 1), :] = jnp.sum(total, axis=0, keepdims=True)
@@ -354,8 +356,8 @@
 def first_kernel(
     deep, rows, width, outer,
     field_ref, edge_ref, above_ref, below_ref, ends_ref, middle_ref,
-    basis_ref, drop_ref, cap_ref, later_ref, out_ref,
-    whole_ref, grid_ref, cross_ref, start_ref, scaled_ref, second_ref, image_ref, inject_ref, sums_ref,
+    basis_ref, drop_ref, cap_ref, grid_ref, cross_ref, later_ref, out_ref,
+    whole_ref, start_ref, scaled_ref, second_ref, image_ref, inject_ref, sums_ref,
 ):
     wide = width + LANES
     blocks = wide // LANES
@@ -417,7 +419,7 @@
     wide = width + LANES
     deep = (rows + 2 * HALO) // GROUP
     full = (2, deep, GROUP, wide)
-    shapes = [(3, *full), full, full, full[1:], (count, LANES)]
+    shapes = [(3, *full), full, full, full, full, full[1:], (count, LANES)]
     return pl.pallas_call(
         functools.partial(first_kernel, deep, rows, width, ends.shape[2] // 2),
         out_shape=[jax.ShapeDtypeStruct(s, jnp.float32) for s in shapes],
@@ -425,8 +427,6 @@
         out_specs=[vmem()] * len(shapes),
         scratch_shapes=[
             pltpu.VMEM((7, wide // LANES, deep * GROUP, LANES), jnp.float32),
-            pltpu.VMEM(full, jnp.float32),
-            pltpu.VMEM(full, jnp.float32),
             pltpu.VMEM((2, deep, GROUP, width), jnp.float32),
             pltpu.VMEM(full, jnp.float32),
             pltpu.VMEM(full, jnp.float32),
@@ -441,12 +441,11 @@
 
 def second_kernel(
     deep, rows, width,
-    gathered_ref, basis_ref, drop_ref, cap_ref, later_ref,
+    gathered_ref, basis_ref, drop_ref, cap_ref, grid_ref, cross_ref, later_ref,
     first_ref, next_ref, held_ref, out_ref,
-    now_ref, grid_ref, cross_ref, start_ref, scaled_ref, second_ref, image_ref, natural_ref, sums_ref,
+    now_ref, start_ref, scaled_ref, second_ref, image_ref, natural_ref, sums_ref,
 ):
     wide = width + LANES
-    weigh(cap_ref, deep, grid_ref, cross_ref)
     weights = [widen(c, wide) for c in weights_of(gathered_ref)]
     for l in range(2):
         for i in range(deep):
@@ -462,7 +461,7 @@
     moments(deep, rows, width, start_ref, next_ref, image_ref, sums_ref, out_ref)
 
 
-def second_step(gathered, basis, drop, cap, later, rows):
+def second_step(gathered, basis, drop, cap, grid, cross, later, rows):
     deep = cap.shape[1]
     wide = cap.shape[-1]
     width = wide - LANES
@@ -471,11 +470,9 @@
     return pl.pallas_call(
         functools.partial(second_kernel, deep, rows, width),
         out_shape=[jax.ShapeDtypeStruct(s, jnp.float32) for s in shapes],
-        in_specs=[vmem()] * 5,
+        in_specs=[vmem()] * 7,
         out_specs=[vmem()] * len(shapes),
         scratch_shapes=[
-            pltpu.VMEM(full, jnp.float32),
-            pltpu.VMEM(full, jnp.float32),
             pltpu.VMEM(full, jnp.float32),
             pltpu.VMEM((2, deep, GROUP, width), jnp.float32),
             pltpu.VMEM(full, jnp.float32),
@@ -486,7 +483,7 @@
         ],
         compiler_params=params(20),
         name="second_step",
-    )(gathered, basis, drop, cap, later)
+    )(gathered, basis, drop, cap, grid, cross, later)
 
 
 def last_kernel(deep, rows, width, gathered_ref, basis_ref, held_ref, out_ref, natural_ref):
@@ -563,8 +560,8 @@
     below = shift(late(False), "gx", False)
     pieces, edge = lax.optimization_barrier((pieces, edge))
     middle = lookup(table_index[outer:-outer], toggle[outer:-outer], (pieces,), many)
-    basis, drop, cap, later, part = first_step(field, edge, above, below, ends, middle, count)
-    first, basis, held, part = second_step(exchange(part), basis, drop, cap, later, rows)
+    basis, *state, part = first_step(field, edge, above, below, ends, middle, count)
+    first, basis, held, part = second_step(exchange(part), basis, *state, rows)
     return first, last_step(exchange(part), basis, held, rows)
 
 

time: 112 us -> 112 us (level)
  no operation moved by 1% of the time
where the time goes in v7:
time: 112 us
  blocking collectives  39.6 us (35%)
  Pallas kernels  32 us (29%)
  starting transfers between devices  29.5 us (26%)
  waiting for transfers between devices  8.19 us (7%)
  other arithmetic  1.37 us (1%)
    all_to_all x2, blocking collectives, exchange(): return lax.all_to_all(block, BOTH, 0, 0, tiled=True)  39.6 us
    pallas_call x2, Pallas kernels, lookup(): pl.pallas_call(functools.partial(first_lookup_kernel if fresh else lookup...  18.1 us
    all_to_all x1, starting transfers between devices, gather_tables(): lax.all_to_all(block, BOTH, 0, 0, tiled=True, axis_index_groups=groups)  16.5 us
    ppermute x4, starting transfers between devices, shift(): lax.ppermute(block, axis, pairs if up else [(b, a) for a, b in pairs])  10.2 us
    all_to_all x1, waiting for transfers between devices, gather_tables(): lax.all_to_all(block, BOTH, 0, 0, tiled=True, axis_index_groups=groups)  6.58 us
    pallas_call x1, Pallas kernels, first_step(): pl.pallas_call(functools.partial(first_kernel, deep, rows, width, ends.sh...  4.7 us
    pallas_call x1, Pallas kernels, second_step(): pl.pallas_call(functools.partial(second_kernel, deep, rows, width), out_s...  4.41 us
    ppermute x1, starting transfers between devices, gather_tables(): return (own, lax.ppermute(own, 'gx', [(i, i ^ 1) for i in range(outer)]))  2.81 us
  transfers between devices with their start and end apart: 6, of which 3 were waited for; matrix products, arithmetic and copies ran while one was open for 1% of the time, Pallas kernels for 16%

profile of v7, /device:TPU:1, one launch (start us, length us, event | category | flops | bytes accessed | tf_op | source)
XLA Modules:
  0.0 111.7 jit_solution(16034866889795409392)
XLA Ops:
  0.6 1.9 %address.1 = (f32[128,4,128]{2,1,0:T(4,128)}, f32[3,64,512]{2,1,0:T(8,128)}) custom-call(f32[16,32]{1,0:T(8,128)} %table_in.1, s32[64,512]{1,0:T(8,128)} %tap_in.1, s32[64,512]{1,0:T(8,128)} %index_in.1, s32[64,512]{1,0:T(8,128)} %toggle_in.1), custom_call_target="tpu_custom_call" | custom-call | tf_op jit(solution)/shard_map/address/pallas_call | solution.py:65
  2.5 0.0 copy-start
  2.6 16.5 %all-to-all-start = ((f32[128,4,128]{2,1,0:T(4,128)}), f32[128,4,128]{2,1,0:T(4,128)S(1)}, u32[]{:S(2)}, u32[]{:S(2)}) async-start(f32[128,4,128]{2,1,0:T(4,128)} %get-tuple-element.20), calls=%async_computation | async-start | bytes 524288 | tf_op jit(solution)/shard_map/all_to_all | solution.py:531
  19.0 0.0 copy-start.1
  19.1 1.3 %bitcast_bitcast_fusion.field_ref = f32[7,4,64,128]{3,2,1,0:T(8,128)S(1)} fusion(f32[3,64,512]{2,1,0:T(8,128)} %get-tuple-element.19, f32[2,64,512]{2,1,0:T(8,128)} %param.11, f32[2,64,512]{2,1,0:T(8,128)} %param.10), kind=kLoop, calls=%fused_computation | loop fusion | flops 458752 | bytes 1835008 | tf_op jit(solution)/shard_map/transpose | solution.py:545
  20.4 1.3 %collective-permute-start.2 = (f32[7,64,128]{2,1,0:T(8,128)S(1)}, f32[7,64,128]{2,1,0:T(8,128)S(1)}, u32[]{:S(2)}, u32[]{:S(2)}) collective-permute-start(f32[7,64,128]{2,1,0:T(8,128)S(1)} %get-tuple-element.38), channel_id=1, source_target_pairs={{1,0},{2,1},{3,2},{4,3},{5,4},{6,5},{7,6},{8,7},{9,8},{10,9},{11,1... | collective-permute-start | bytes 688136 | tf_op jit(solution)/shard_map/ppermute | solution.py:519
  21.7 4.0 %collective-permute-start.1 = (f32[7,64,128]{2,1,0:T(8,128)S(1)}, f32[7,64,128]{2,1,0:T(8,128)S(1)}, u32[]{:S(2)}, u32[]{:S(2)}) collective-permute-start(f32[7,64,128]{2,1,0:T(8,128)S(1)} %get-tuple-element.39), channel_id=1, source_target_pairs={{0,1},{1,2},{2,3},{3,4},{4,5},{5,6},{6,7},{7,8},{8,9},{9,10},{10,1... | collective-permute-start | bytes 688136 | tf_op jit(solution)/shard_map/ppermute | solution.py:519
  25.7 0.0 copy-done
  25.7 0.0 copy-done.1
  25.8 6.6 %all-to-all-done = f32[128,4,128]{2,1,0:T(4,128)S(1)} async-done(((f32[128,4,128]{2,1,0:T(4,128)}), f32[128,4,128]{2,1,0:T(4,128)S(1)}, u32[]{:S(2)}, u32[]{:S(2)}) %all-to-all-start) | async-done | bytes 262176 | tf_op jit(solution)/shard_map/all_to_all | solution.py:531
  32.3 2.8 %collective-permute-start = (f32[512,128]{1,0:T(8,128)S(1)}, f32[512,128]{1,0:T(8,128)S(1)}, u32[]{:S(2)}, u32[]{:S(2)}) collective-permute-start(f32[512,128]{1,0:T(8,128)S(1)} %bitcast.26), channel_id=1, source_target_pairs={{0,16},{16,0},{32,48},{48,32},{64,80},{80,64},{96,112},{112,96},{1... | collective-permute-start | bytes 786440 | tf_op jit(solution)/shard_map/ppermute | solution.py:533
  35.3 1.1 collective-permute-done.other_ref
  36.3 11.3 %lookup.2 = (f32[2,4,40,128]{3,2,1,0:T(8,128)S(1)}, bf16[512,512]{1,0:T(8,128)(2,1)S(1)}) custom-call(s32[40,512]{1,0:T(8,128)S(1)} %get-tuple-element.48.index_ref, s32[40,512]{1,0:T(8,128)S(1)} %get-tuple-element.49.toggle_ref, f32[512,128]{1,0:T(8,128)S(1)} %bitcast.27, f32[512,128]{1,0:T(8,128)S(1)} %collective-permute-done.other_ref), custom_call_target="tpu_custom_call" | custom-call | flops 10737418240 | tf_op jit(solution)/shard_map/lookup/pallas_call | solution.py:157
  47.6 0.0 collective-permute-done.2.right_ref
  47.6 0.0 collective-permute-done.1.left_ref
  47.6 2.0 %edge_lookup.1.edge_ref = f32[7,64,128]{2,1,0:T(8,128)S(1)} custom-call(f32[7,64,128]{2,1,0:T(8,128)S(1)} %collective-permute-done.1.left_ref, f32[7,64,128]{2,1,0:T(8,128)S(1)} %collective-permute-done.2.right_ref, bf16[512,512]{1,0:T(8,128)(2,1)S(1)} %get-tuple-element.24.pieces_ref), custom_call_target="tpu_custom_call" | custom-call | flops 1342177280 | tf_op jit(solution)/shard_map/edge_lookup/pallas_call | solution.py:203
  49.7 2.8 %collective-permute-start.3 = (f32[35,20,128]{2,1,0:T(8,128)S(1)}, f32[35,20,128]{2,1,0:T(8,128)S(1)}, u32[]{:S(2)}, u32[]{:S(2)}) collective-permute-start(f32[35,20,128]{2,1,0:T(8,128)S(1)} %pad_maximum_fusion), channel_id=1, source_target_pairs={{0,16},{16,32},{32,48},{48,64},{64,80},{80,96},{96,112},{112,128},... | collective-permute-start | bytes 1075208 | tf_op jit(solution)/shard_map/ppermute | solution.py:519
  52.5 2.1 %collective-permute-start.4 = (f32[35,20,128]{2,1,0:T(8,128)S(1)}, f32[35,20,128]{2,1,0:T(8,128)S(1)}, u32[]{:S(2)}, u32[]{:S(2)}) collective-permute-start(f32[35,20,128]{2,1,0:T(8,128)S(1)} %pad_maximum_fusion.1), channel_id=1, source_target_pairs={{16,0},{32,16},{48,32},{64,48},{80,64},{96,80},{112,96},{128,112},... | collective-permute-start | bytes 1075208 | tf_op jit(solution)/shard_map/ppermute | solution.py:519
  54.7 6.8 %lookup.3.middle_ref = f32[2,4,24,128]{3,2,1,0:T(8,128)S(1)} custom-call(s32[24,512]{1,0:T(8,128)S(1)} %slice.58.index_ref, s32[24,512]{1,0:T(8,128)S(1)} %slice.59.toggle_ref, bf16[512,512]{1,0:T(8,128)(2,1)S(1)} %get-tuple-element.24.pieces_ref), custom_call_target="tpu_custom_call" | custom-call | flops 6442450944 | tf_op jit(solution)/shard_map/lookup/pallas_call | solution.py:157
  61.4 0.0 collective-permute-done.3.above_ref
  61.5 0.5 collective-permute-done.4.below_ref
  62.0 4.7 %first_step.1 = (f32[3,2,13,8,640]{4,3,2,1,0:T(8,128)S(1)}, f32[2,13,8,640]{3,2,1,0:T(8,128)S(1)}, f32[2,13,8,640]{3,2,1,0:T(8,128)S(1)}, f32[2,13,8,640]{3,2,1,...) custom-call(f32[7,4,64,128]{3,2,1,0:T(8,128)S(1)} %bitcast_bitcast_fusion.field_ref, ...), custom_call_target="tpu_custom_call" | custom-call | tf_op jit(solution)/shard_map/first_step/pallas_call | solution.py:423
  66.7 21.2 %all_to_all.27 = f32[256,1,128]{2,1,0:T(1,128)S(1)} all-to-all(f32[256,1,128]{2,1,0:T(1,128)S(1)} %bitcast.28), channel_id=1, replica_groups=mesh['gx'=16,'gy'=16] {'gx','gy'}, dimensions={0} | all-to-all | bytes 262144 | tf_op jit(solution)/shard_map/all_to_all | solution.py:523
  87.9 4.4 %second_step.1 = (f32[2,64,512]{2,1,0:T(8,128)}, f32[3,2,13,8,640]{4,3,2,1,0:T(8,128)S(1)}, f32[2,13,8,512]{3,2,1,0:T(8,128)S(1)}, f32[256,128]{1,0:T(8,128)S(1)}) custom-call(f32[256,128]{1,0:T(8,128)S(1)} %bitcast.24, f32[3,2,13,8,640]{4,3,2,1,0:T(8,128)S(1)} %get-tuple-element.26.basis_ref, f32[2,13,8,640]{3,2,1,0:T(8,128)S(1)} %get-tuple-element.27.drop_ref, ...), custom_call_target="tpu_custom_call" | custom-call | tf_op jit(solution)/shard_map/second_step/pallas_call | solution.py:470
  92.3 18.4 %all_to_all.28 = f32[256,1,128]{2,1,0:T(1,128)S(1)} all-to-all(f32[256,1,128]{2,1,0:T(1,128)S(1)} %bitcast.29), channel_id=1, replica_groups=mesh['gx'=16,'gy'=16] {'gx','gy'}, dimensions={0} | all-to-all | bytes 262144 | tf_op jit(solution)/shard_map/all_to_all | solution.py:523
  110.7 1.0 last_step.1
  (11 shorter events, 0.2 us)
Async XLA Ops:
  2.5 23.2 %copy-start = (s32[64,512]{1,0:T(8,128)S(1)}, s32[64,512]{1,0:T(8,128)}, u32[]{:S(2)}) copy-start(s32[64,512]{1,0:T(8,128)} %index_in.1) | copy-start | bytes 393220
  2.6 29.8 %all-to-all-start = ((f32[128,4,128]{2,1,0:T(4,128)}), f32[128,4,128]{2,1,0:T(4,128)S(1)}, u32[]{:S(2)}, u32[]{:S(2)}) async-start(f32[128,4,128]{2,1,0:T(4,128)} %get-tuple-element.20), calls=%async_computation | async-start | bytes 524288 | tf_op jit(solution)/shard_map/all_to_all | solution.py:531
  19.0 6.7 %copy-start.1 = (s32[64,512]{1,0:T(8,128)S(1)}, s32[64,512]{1,0:T(8,128)}, u32[]{:S(2)}) copy-start(s32[64,512]{1,0:T(8,128)} %toggle_in.1) | copy-start | bytes 393220
  20.4 27.2 %collective-permute-start.2 = (f32[7,64,128]{2,1,0:T(8,128)S(1)}, f32[7,64,128]{2,1,0:T(8,128)S(1)}, u32[]{:S(2)}, u32[]{:S(2)}) collective-permute-start(f32[7,64,128]{2,1,0:T(8,128)S(1)} %get-tuple-element.38), channel_id=1, source_target_pairs={{1,0},{2,1},{3,2},{4,3},{5,4},{6,5},{7,6},{8,7},{9,8},{10,9},{11,1... | collective-permute-start | bytes 688136 | tf_op jit(solution)/shard_map/ppermute | solution.py:519
  21.7 25.9 %collective-permute-start.1 = (f32[7,64,128]{2,1,0:T(8,128)S(1)}, f32[7,64,128]{2,1,0:T(8,128)S(1)}, u32[]{:S(2)}, u32[]{:S(2)}) collective-permute-start(f32[7,64,128]{2,1,0:T(8,128)S(1)} %get-tuple-element.39), channel_id=1, source_target_pairs={{0,1},{1,2},{2,3},{3,4},{4,5},{5,6},{6,7},{7,8},{8,9},{9,10},{10,1... | collective-permute-start | bytes 688136 | tf_op jit(solution)/shard_map/ppermute | solution.py:519
  32.3 4.0 %collective-permute-start = (f32[512,128]{1,0:T(8,128)S(1)}, f32[512,128]{1,0:T(8,128)S(1)}, u32[]{:S(2)}, u32[]{:S(2)}) collective-permute-start(f32[512,128]{1,0:T(8,128)S(1)} %bitcast.26), channel_id=1, source_target_pairs={{0,16},{16,0},{32,48},{48,32},{64,80},{80,64},{96,112},{112,96},{1... | collective-permute-start | bytes 786440 | tf_op jit(solution)/shard_map/ppermute | solution.py:533
  49.7 11.7 %collective-permute-start.3 = (f32[35,20,128]{2,1,0:T(8,128)S(1)}, f32[35,20,128]{2,1,0:T(8,128)S(1)}, u32[]{:S(2)}, u32[]{:S(2)}) collective-permute-start(f32[35,20,128]{2,1,0:T(8,128)S(1)} %pad_maximum_fusion), channel_id=1, source_target_pairs={{0,16},{16,32},{32,48},{48,64},{64,80},{80,96},{96,112},{112,128},... | collective-permute-start | bytes 1075208 | tf_op jit(solution)/shard_map/ppermute | solution.py:519
  52.5 9.5 %collective-permute-start.4 = (f32[35,20,128]{2,1,0:T(8,128)S(1)}, f32[35,20,128]{2,1,0:T(8,128)S(1)}, u32[]{:S(2)}, u32[]{:S(2)}) collective-permute-start(f32[35,20,128]{2,1,0:T(8,128)S(1)} %pad_maximum_fusion.1), channel_id=1, source_target_pairs={{16,0},{32,16},{48,32},{64,48},{80,64},{96,80},{112,96},{128,112},... | collective-permute-start | bytes 1075208 | tf_op jit(solution)/shard_map/ppermute | solution.py:519

commit v8 on v6

--- a/solution.py
+++ b/solution.py
@@ -121,7 +121,9 @@
     share = SUBSTEPS // STEPS
     means = []
     for k in range(STEPS):
-        inside = (moment >= k * share) & (moment < (k + 1) * share)
+        inside = moment < (k + 1) * share
+        if k:
+            inside &= moment >= k * share
         total = jnp.sum(jnp.where(inside, chosen, 0.0), axis=0, keepdims=True)
         means.append(total * (1.0 / share))
     return means

time: 112 us -> 112 us (level)
  no operation moved by 1% of the time
where the time goes in v8:
time: 112 us
  blocking collectives  39.5 us (35%)
  Pallas kernels  31.9 us (28%)
  starting transfers between devices  29.5 us (26%)
  waiting for transfers between devices  8.26 us (7%)
  other arithmetic  1.37 us (1%)
    all_to_all x2, blocking collectives, exchange(): return lax.all_to_all(block, BOTH, 0, 0, tiled=True)  39.5 us
    pallas_call x2, Pallas kernels, lookup(): pl.pallas_call(functools.partial(first_lookup_kernel if fresh else lookup...  17.9 us
    all_to_all x1, starting transfers between devices, gather_tables(): lax.all_to_all(block, BOTH, 0, 0, tiled=True, axis_index_groups=groups)  16.5 us
    ppermute x4, starting transfers between devices, shift(): lax.ppermute(block, axis, pairs if up else [(b, a) for a, b in pairs])  10.2 us
    all_to_all x1, waiting for transfers between devices, gather_tables(): lax.all_to_all(block, BOTH, 0, 0, tiled=True, axis_index_groups=groups)  6.58 us
    pallas_call x1, Pallas kernels, first_step(): pl.pallas_call(functools.partial(first_kernel, deep, rows, width, ends.sh...  4.67 us
    pallas_call x1, Pallas kernels, second_step(): pl.pallas_call(functools.partial(second_kernel, deep, rows, width), out_s...  4.49 us
    ppermute x1, starting transfers between devices, gather_tables(): return (own, lax.ppermute(own, 'gx', [(i, i ^ 1) for i in range(outer)]))  2.82 us
  transfers between devices with their start and end apart: 6, of which 3 were waited for; matrix products, arithmetic and copies ran while one was open for 1% of the time, Pallas kernels for 16%

profile of v8, /device:TPU:1, one launch (start us, length us, event | category | flops | bytes accessed | tf_op | source)
XLA Modules:
  0.0 111.5 jit_solution(1498281971563455403)
XLA Ops:
  0.6 1.9 %address.1 = (f32[128,4,128]{2,1,0:T(4,128)}, f32[3,64,512]{2,1,0:T(8,128)}) custom-call(f32[16,32]{1,0:T(8,128)} %table_in.1, s32[64,512]{1,0:T(8,128)} %tap_in.1, s32[64,512]{1,0:T(8,128)} %index_in.1, s32[64,512]{1,0:T(8,128)} %toggle_in.1), custom_call_target="tpu_custom_call" | custom-call | tf_op jit(solution)/shard_map/address/pallas_call | solution.py:65
  2.5 0.0 copy-start
  2.6 16.5 %all-to-all-start = ((f32[128,4,128]{2,1,0:T(4,128)}), f32[128,4,128]{2,1,0:T(4,128)S(1)}, u32[]{:S(2)}, u32[]{:S(2)}) async-start(f32[128,4,128]{2,1,0:T(4,128)} %get-tuple-element.18), calls=%async_computation | async-start | bytes 524288 | tf_op jit(solution)/shard_map/all_to_all | solution.py:536
  19.0 0.0 copy-start.1
  19.1 1.3 %bitcast_bitcast_fusion.field_ref = f32[7,4,64,128]{3,2,1,0:T(8,128)S(1)} fusion(f32[3,64,512]{2,1,0:T(8,128)} %get-tuple-element.17, f32[2,64,512]{2,1,0:T(8,128)} %param.11, f32[2,64,512]{2,1,0:T(8,128)} %param.10), kind=kLoop, calls=%fused_computation | loop fusion | flops 458752 | bytes 1835008 | tf_op jit(solution)/shard_map/transpose | solution.py:550
  20.4 1.3 %collective-permute-start.2 = (f32[7,64,128]{2,1,0:T(8,128)S(1)}, f32[7,64,128]{2,1,0:T(8,128)S(1)}, u32[]{:S(2)}, u32[]{:S(2)}) collective-permute-start(f32[7,64,128]{2,1,0:T(8,128)S(1)} %get-tuple-element.34), channel_id=1, source_target_pairs={{1,0},{2,1},{3,2},{4,3},{5,4},{6,5},{7,6},{8,7},{9,8},{10,9},{11,1... | collective-permute-start | bytes 688136 | tf_op jit(solution)/shard_map/ppermute | solution.py:524
  21.7 4.0 %collective-permute-start.1 = (f32[7,64,128]{2,1,0:T(8,128)S(1)}, f32[7,64,128]{2,1,0:T(8,128)S(1)}, u32[]{:S(2)}, u32[]{:S(2)}) collective-permute-start(f32[7,64,128]{2,1,0:T(8,128)S(1)} %get-tuple-element.35), channel_id=1, source_target_pairs={{0,1},{1,2},{2,3},{3,4},{4,5},{5,6},{6,7},{7,8},{8,9},{9,10},{10,1... | collective-permute-start | bytes 688136 | tf_op jit(solution)/shard_map/ppermute | solution.py:524
  25.7 0.0 copy-done
  25.7 0.0 copy-done.1
  25.8 6.6 %all-to-all-done = f32[128,4,128]{2,1,0:T(4,128)S(1)} async-done(((f32[128,4,128]{2,1,0:T(4,128)}), f32[128,4,128]{2,1,0:T(4,128)S(1)}, u32[]{:S(2)}, u32[]{:S(2)}) %all-to-all-start) | async-done | bytes 262176 | tf_op jit(solution)/shard_map/all_to_all | solution.py:536
  32.3 2.8 %collective-permute-start = (f32[512,128]{1,0:T(8,128)S(1)}, f32[512,128]{1,0:T(8,128)S(1)}, u32[]{:S(2)}, u32[]{:S(2)}) collective-permute-start(f32[512,128]{1,0:T(8,128)S(1)} %bitcast.26), channel_id=1, source_target_pairs={{0,16},{16,0},{32,48},{48,32},{64,80},{80,64},{96,112},{112,96},{1... | collective-permute-start | bytes 786440 | tf_op jit(solution)/shard_map/ppermute | solution.py:538
  35.3 1.1 collective-permute-done.other_ref
  36.3 11.2 %lookup.2 = (f32[2,4,40,128]{3,2,1,0:T(8,128)S(1)}, bf16[512,512]{1,0:T(8,128)(2,1)S(1)}) custom-call(s32[40,512]{1,0:T(8,128)S(1)} %get-tuple-element.44.index_ref, s32[40,512]{1,0:T(8,128)S(1)} %get-tuple-element.45.toggle_ref, f32[512,128]{1,0:T(8,128)S(1)} %bitcast.27, f32[512,128]{1,0:T(8,128)S(1)} %collective-permute-done.other_ref), custom_call_target="tpu_custom_call" | custom-call | flops 10737418240 | tf_op jit(solution)/shard_map/lookup/pallas_call | solution.py:159
  47.5 0.0 collective-permute-done.2.right_ref
  47.5 0.0 collective-permute-done.1.left_ref
  47.6 2.0 %edge_lookup.1.edge_ref = f32[7,64,128]{2,1,0:T(8,128)S(1)} custom-call(f32[7,64,128]{2,1,0:T(8,128)S(1)} %collective-permute-done.1.left_ref, f32[7,64,128]{2,1,0:T(8,128)S(1)} %collective-permute-done.2.right_ref, bf16[512,512]{1,0:T(8,128)(2,1)S(1)} %get-tuple-element.22.pieces_ref), custom_call_target="tpu_custom_call" | custom-call | flops 1342177280 | tf_op jit(solution)/shard_map/edge_lookup/pallas_call | solution.py:205
  49.6 2.7 %collective-permute-start.3 = (f32[35,20,128]{2,1,0:T(8,128)S(1)}, f32[35,20,128]{2,1,0:T(8,128)S(1)}, u32[]{:S(2)}, u32[]{:S(2)}) collective-permute-start(f32[35,20,128]{2,1,0:T(8,128)S(1)} %pad_maximum_fusion), channel_id=1, source_target_pairs={{0,16},{16,32},{32,48},{48,64},{64,80},{80,96},{96,112},{112,128},... | collective-permute-start | bytes 1075208 | tf_op jit(solution)/shard_map/ppermute | solution.py:524
  52.4 2.1 %collective-permute-start.4 = (f32[35,20,128]{2,1,0:T(8,128)S(1)}, f32[35,20,128]{2,1,0:T(8,128)S(1)}, u32[]{:S(2)}, u32[]{:S(2)}) collective-permute-start(f32[35,20,128]{2,1,0:T(8,128)S(1)} %pad_maximum_fusion.1), channel_id=1, source_target_pairs={{16,0},{32,16},{48,32},{64,48},{80,64},{96,80},{112,96},{128,112},... | collective-permute-start | bytes 1075208 | tf_op jit(solution)/shard_map/ppermute | solution.py:524
  54.6 6.7 %lookup.3.middle_ref = f32[2,4,24,128]{3,2,1,0:T(8,128)S(1)} custom-call(s32[24,512]{1,0:T(8,128)S(1)} %slice.58.index_ref, s32[24,512]{1,0:T(8,128)S(1)} %slice.59.toggle_ref, bf16[512,512]{1,0:T(8,128)(2,1)S(1)} %get-tuple-element.22.pieces_ref), custom_call_target="tpu_custom_call" | custom-call | flops 6442450944 | tf_op jit(solution)/shard_map/lookup/pallas_call | solution.py:159
  61.3 0.0 collective-permute-done.3.above_ref
  61.3 0.6 collective-permute-done.4.below_ref
  61.9 4.7 %first_step.1 = (f32[3,2,13,8,640]{4,3,2,1,0:T(8,128)S(1)}, f32[2,13,8,640]{3,2,1,0:T(8,128)S(1)}, f32[2,13,8,640]{3,2,1,0:T(8,128)S(1)}, f32[13,8,640]{2,1,0:T(8,128)S(1)}, f32[256,128]{1,0:T(8,128)S(1)}) custom-call(f32[7,4,64,128]{3,2,1,0:T(8,128)S(1)} %bitcast_bitcast_fusion.field_ref, f32[7,64,128]{2,1,0:T(8,128)S(1)} %edge_lookup.1.edge_ref, ...), custom_call_target="tpu_custom_call" | custom-call | tf_op jit(solution)/shard_map/first_step/pallas_call | solution.py:423
  66.6 21.1 %all_to_all.27 = f32[256,1,128]{2,1,0:T(1,128)S(1)} all-to-all(f32[256,1,128]{2,1,0:T(1,128)S(1)} %bitcast.28), channel_id=1, replica_groups=mesh['gx'=16,'gy'=16] {'gx','gy'}, dimensions={0} | all-to-all | bytes 262144 | tf_op jit(solution)/shard_map/all_to_all | solution.py:528
  87.7 4.5 %second_step.1 = (f32[2,64,512]{2,1,0:T(8,128)}, f32[3,2,13,8,640]{4,3,2,1,0:T(8,128)S(1)}, f32[2,13,8,512]{3,2,1,0:T(8,128)S(1)}, f32[256,128]{1,0:T(8,128)S(1)}) custom-call(f32[256,128]{1,0:T(8,128)S(1)} %bitcast.24, f32[3,2,13,8,640]{4,3,2,1,0:T(8,128)S(1)} %get-tuple-element.24.basis_ref, f32[2,13,8,640]{3,2,1,0:T(8,128)S(1)} %get-tuple-element.25.drop_ref, ...), custom_call_target="tpu_custom_call" | custom-call | tf_op jit(solution)/shard_map/second_step/pallas_call | solution.py:473
  92.1 18.4 %all_to_all.28 = f32[256,1,128]{2,1,0:T(1,128)S(1)} all-to-all(f32[256,1,128]{2,1,0:T(1,128)S(1)} %bitcast.29), channel_id=1, replica_groups=mesh['gx'=16,'gy'=16] {'gx','gy'}, dimensions={0} | all-to-all | bytes 262144 | tf_op jit(solution)/shard_map/all_to_all | solution.py:528
  110.6 1.0 last_step.1
  (11 shorter events, 0.2 us)
Async XLA Ops:
  2.5 23.2 %copy-start = (s32[64,512]{1,0:T(8,128)S(1)}, s32[64,512]{1,0:T(8,128)}, u32[]{:S(2)}) copy-start(s32[64,512]{1,0:T(8,128)} %index_in.1) | copy-start | bytes 393220
  2.6 29.8 %all-to-all-start = ((f32[128,4,128]{2,1,0:T(4,128)}), f32[128,4,128]{2,1,0:T(4,128)S(1)}, u32[]{:S(2)}, u32[]{:S(2)}) async-start(f32[128,4,128]{2,1,0:T(4,128)} %get-tuple-element.18), calls=%async_computation | async-start | bytes 524288 | tf_op jit(solution)/shard_map/all_to_all | solution.py:536
  19.0 6.7 %copy-start.1 = (s32[64,512]{1,0:T(8,128)S(1)}, s32[64,512]{1,0:T(8,128)}, u32[]{:S(2)}) copy-start(s32[64,512]{1,0:T(8,128)} %toggle_in.1) | copy-start | bytes 393220
  20.4 27.1 %collective-permute-start.2 = (f32[7,64,128]{2,1,0:T(8,128)S(1)}, f32[7,64,128]{2,1,0:T(8,128)S(1)}, u32[]{:S(2)}, u32[]{:S(2)}) collective-permute-start(f32[7,64,128]{2,1,0:T(8,128)S(1)} %get-tuple-element.34), channel_id=1, source_target_pairs={{1,0},{2,1},{3,2},{4,3},{5,4},{6,5},{7,6},{8,7},{9,8},{10,9},{11,1... | collective-permute-start | bytes 688136 | tf_op jit(solution)/shard_map/ppermute | solution.py:524
  21.7 25.9 %collective-permute-start.1 = (f32[7,64,128]{2,1,0:T(8,128)S(1)}, f32[7,64,128]{2,1,0:T(8,128)S(1)}, u32[]{:S(2)}, u32[]{:S(2)}) collective-permute-start(f32[7,64,128]{2,1,0:T(8,128)S(1)} %get-tuple-element.35), channel_id=1, source_target_pairs={{0,1},{1,2},{2,3},{3,4},{4,5},{5,6},{6,7},{7,8},{8,9},{9,10},{10,1... | collective-permute-start | bytes 688136 | tf_op jit(solution)/shard_map/ppermute | solution.py:524
  32.3 4.0 %collective-permute-start = (f32[512,128]{1,0:T(8,128)S(1)}, f32[512,128]{1,0:T(8,128)S(1)}, u32[]{:S(2)}, u32[]{:S(2)}) collective-permute-start(f32[512,128]{1,0:T(8,128)S(1)} %bitcast.26), channel_id=1, source_target_pairs={{0,16},{16,0},{32,48},{48,32},{64,80},{80,64},{96,112},{112,96},{1... | collective-permute-start | bytes 786440 | tf_op jit(solution)/shard_map/ppermute | solution.py:538
  49.6 11.7 %collective-permute-start.3 = (f32[35,20,128]{2,1,0:T(8,128)S(1)}, f32[35,20,128]{2,1,0:T(8,128)S(1)}, u32[]{:S(2)}, u32[]{:S(2)}) collective-permute-start(f32[35,20,128]{2,1,0:T(8,128)S(1)} %pad_maximum_fusion), channel_id=1, source_target_pairs={{0,16},{16,32},{32,48},{48,64},{64,80},{80,96},{96,112},{112,128},... | collective-permute-start | bytes 1075208 | tf_op jit(solution)/shard_map/ppermute | solution.py:524
  52.4 9.5 %collective-permute-start.4 = (f32[35,20,128]{2,1,0:T(8,128)S(1)}, f32[35,20,128]{2,1,0:T(8,128)S(1)}, u32[]{:S(2)}, u32[]{:S(2)}) collective-permute-start(f32[35,20,128]{2,1,0:T(8,128)S(1)} %pad_maximum_fusion.1), channel_id=1, source_target_pairs={{16,0},{32,16},{48,32},{64,48},{80,64},{96,80},{112,96},{128,112},... | collective-permute-start | bytes 1075208 | tf_op jit(solution)/shard_map/ppermute | solution.py:524
